TPU v7x, 512 devices: a whole 4x4x16 slice. The times are simulated.
512 devices in a mesh: space: 8 (over x, core), energy: 64 (over z, y).
Axes of the slice: x: 4, y: 4, z: 16, core: 2. Of those that a mesh axis runs over, the one named last changes fastest.
Arguments:
- lesser_in: bfloat16 [64, 8, 2, 256, 256], P('energy', 'space'), may hold values from -6 to 6
- retarded: bfloat16 [64, 8, 2, 256, 256], P('energy', 'space'), may hold values from -0.25 to 0.25
- coupling: bfloat16 [8, 2, 256, 256], P('space'), may hold values from -0.25 to 0.25
- interaction: bfloat16 [8, 128, 65536], P('space', None, 'energy'), may hold values from -1.5 to 1.5
Outputs:
- self_energy: bfloat16 [64, 8, 2, 256, 256], P('energy', 'space')
All inputs are finite; a program needn't handle non-finite values.
Results may differ from a plain program's by a relative error of at most 0.029.
Values may be sent and summed in bfloat16 or wider, within the bound.
No kernel may reach another device: no remote copies, remote signals or barrier semaphores. Data moves between devices by JAX's collectives and lax.ppermute only.
A program may use at most 128 MiB of HBM per device.

v0:
```python
import math

import jax
import jax.numpy as jnp
from jax import lax
from jax.sharding import Mesh
from jax.sharding import PartitionSpec as P

ENERGY = ("energy_0", "energy_1")


def passed_along(array, axis, by):
    count = lax.axis_size(axis)
    pairs = [(i, i + by) for i in range(count) if 0 <= i + by < count]
    return lax.ppermute(array, axis, pairs)


def split_up(array, dim, count):
    shape = array.shape
    pieces = array.reshape(*shape[:dim], count, shape[dim] // count, *shape[dim + 1 :])
    return jnp.moveaxis(pieces, dim, 0)


def in_order(pieces, dim):
    shape = list(pieces.shape[1:])
    shape[dim] *= pieces.shape[0]
    return jnp.moveaxis(pieces, 0, dim).reshape(shape)


def moved_by_axis(pieces, axes, turns):
    shape = [lax.axis_size(a) for a in axes]
    pieces = pieces.reshape(*shape, *pieces.shape[1:])
    for k in turns:
        pieces = lax.all_to_all(pieces, axes[k], split_axis=k, concat_axis=k, tiled=True)
    return pieces.reshape(-1, *pieces.shape[len(axes) :])


def one_axis_at_a_time(array, axes, turns, split_dim, concat_dim):
    pieces = split_up(array, split_dim, lax.axis_size(axes))
    return in_order(moved_by_axis(pieces, axes, turns), concat_dim)


def product(left_real, left_imag, right_real, right_imag):
    real_part = jnp.dot(left_real, right_real, preferred_element_type=jnp.float32) - jnp.dot(
        left_imag, right_imag, preferred_element_type=jnp.float32
    )
    imag_part = jnp.dot(left_real, right_imag, preferred_element_type=jnp.float32) + jnp.dot(
        left_imag, right_real, preferred_element_type=jnp.float32
    )
    return (real_part, imag_part)


def contract(former, latter):
    return lax.dot_general(
        former, latter, (((1,), (1,)), ((), ())), preferred_element_type=jnp.float32
    )


def product_adjoint(left_real, left_imag, right_real, right_imag):
    real_part = contract(left_real, right_real) + contract(left_imag, right_imag)
    imag_part = contract(left_imag, right_real) - contract(left_real, right_imag)
    return (real_part, imag_part)


def phase_table(row_count, column_count, length):
    row_index = jnp.arange(row_count, dtype=jnp.int32)[:, None]
    column_index = jnp.arange(column_count, dtype=jnp.int32)[None, :]
    residue = row_index * column_index % length
    return residue.astype(jnp.float32) * (2.0 * math.pi / length)


def finish(spectrum_real, spectrum_imag, weights, energy_count, length):
    forward_scale = energy_count ** (-0.5)
    inverse_scale = length ** (-0.5)
    spectrum_real = spectrum_real * forward_scale
    spectrum_imag = spectrum_imag * forward_scale
    weight_values = weights.astype(jnp.float32)
    squared_real = (
        (spectrum_real * spectrum_real - spectrum_imag * spectrum_imag) * weight_values
    ).astype(jnp.bfloat16)
    squared_imag = (2.0 * spectrum_real * spectrum_imag * weight_values).astype(jnp.bfloat16)
    inverse_phase = phase_table(energy_count, length, length)
    inverse_real = jnp.cos(inverse_phase).astype(jnp.bfloat16)
    inverse_imag = jnp.sin(inverse_phase).astype(jnp.bfloat16)
    out_real, out_imag = product(inverse_real, inverse_imag, squared_real, squared_imag)
    return jnp.stack([out_real * inverse_scale, out_imag * inverse_scale], axis=1).astype(
        jnp.bfloat16
    )


def batched(pattern, former, latter):
    return jnp.einsum(pattern, former, latter, preferred_element_type=jnp.float32)


def local(lesser_in, retarded, coupling, interaction):
    local_count = lesser_in.shape[0]
    block_order = coupling.shape[-1]
    groups = lax.axis_size(ENERGY)
    sections = lax.axis_size("space")
    energy_count = local_count * groups
    length = 2 * energy_count
    section_index = lax.axis_index("space")
    resolvent_real = retarded[:, 0, 0]
    resolvent_imag = retarded[:, 0, 1]
    lesser_real = lesser_in[:, 0, 0]
    lesser_imag = lesser_in[:, 0, 1]
    coupling_real = coupling[0, 0]
    coupling_imag = coupling[0, 1]
    map_real = (
        batched("eij,jk->eik", resolvent_real, coupling_real)
        - batched("eij,jk->eik", resolvent_imag, coupling_imag)
    ).astype(jnp.bfloat16)
    map_imag = (
        batched("eij,jk->eik", resolvent_real, coupling_imag)
        + batched("eij,jk->eik", resolvent_imag, coupling_real)
    ).astype(jnp.bfloat16)
    half_real = (
        batched("eij,ejk->eik", resolvent_real, lesser_real)
        - batched("eij,ejk->eik", resolvent_imag, lesser_imag)
    ).astype(jnp.bfloat16)
    half_imag = (
        batched("eij,ejk->eik", resolvent_real, lesser_imag)
        + batched("eij,ejk->eik", resolvent_imag, lesser_real)
    ).astype(jnp.bfloat16)
    source_real = batched("eij,ekj->eik", half_real, resolvent_real) + batched(
        "eij,ekj->eik", half_imag, resolvent_imag
    )
    source_imag = batched("eij,ekj->eik", half_imag, resolvent_real) - batched(
        "eij,ekj->eik", half_real, resolvent_imag
    )
    forward_phase = phase_table(length, energy_count, length)
    forward_real = jnp.cos(forward_phase).astype(jnp.bfloat16)
    forward_imag = (-jnp.sin(forward_phase)).astype(jnp.bfloat16)

    def advance(incoming, energy_slot):
        step_map_real = lax.dynamic_index_in_dim(map_real, energy_slot, 0, keepdims=False)
        step_map_imag = lax.dynamic_index_in_dim(map_imag, energy_slot, 0, keepdims=False)
        step_source_real = lax.dynamic_index_in_dim(source_real, energy_slot, 0, keepdims=False)
        step_source_imag = lax.dynamic_index_in_dim(source_imag, energy_slot, 0, keepdims=False)
        carry_real, carry_imag = product(step_map_real, step_map_imag, incoming[0], incoming[1])
        carry_real = carry_real.astype(jnp.bfloat16)
        carry_imag = carry_imag.astype(jnp.bfloat16)
        grown_real, grown_imag = product_adjoint(
            carry_real, carry_imag, step_map_real, step_map_imag
        )
        return jnp.stack([step_source_real + grown_real, step_source_imag + grown_imag]).astype(
            jnp.bfloat16
        )

    zero_block = jnp.zeros((2, block_order, block_order), jnp.bfloat16)
    initial = jnp.zeros((local_count, 2, block_order, block_order), jnp.bfloat16)

    def advance_section(counter, state):
        previous, gathered = state
        incoming = passed_along(previous, "space", 1)
        energy_slot = counter - section_index
        active = jnp.logical_and(energy_slot >= 0, energy_slot < local_count)
        clamped = jnp.clip(energy_slot, 0, local_count - 1)
        newest = lax.cond(active, lambda: advance(incoming, clamped), lambda: zero_block)
        placed = lax.dynamic_update_index_in_dim(gathered, newest, clamped, 0)
        gathered = jnp.where(active, placed, gathered)
        return (newest, gathered)

    final_block, gathered = lax.fori_loop(
        0, local_count + sections - 1, advance_section, (zero_block, initial)
    )
    entries = one_axis_at_a_time(
        gathered.reshape(local_count, 2, block_order * block_order), ENERGY, (0, 1), 2, 0
    )
    spectrum_real, spectrum_imag = product(forward_real, forward_imag, entries[:, 0], entries[:, 1])
    result = finish(spectrum_real, spectrum_imag, interaction[0], energy_count, length)
    returned = lax.all_to_all(result, ENERGY, split_axis=0, concat_axis=2, tiled=True)
    return returned.reshape(local_count, 1, 2, block_order, block_order)


def solution(mesh):
    split = Mesh(
        mesh.devices.reshape(mesh.shape["space"], 16, 4), ("space", "energy_0", "energy_1")
    )
    in_specs = (
        P(ENERGY, "space", None, None, None),
        P(ENERGY, "space", None, None, None),
        P("space", None, None, None),
        P("space", None, ENERGY),
    )
    out_specs = P(ENERGY, "space", None, None, None)
    return jax.shard_map(local, mesh=split, in_specs=in_specs, out_specs=out_specs, check_vma=False)
```

profile of v0, /device:TPU:2, one launch (start us, length us, event | category | flops | bytes accessed | tf_op | source)
XLA Modules:
  0.0 154.9 jit_solution(4746505653799863960)
XLA Ops:
  0.0 1.2 fusion.55
  1.4 0.8 copy-done.2
  4.3 0.7 broadcast_in_dim.23
  5.0 71.9 %while.16 = (s32[]{:T(128)}, bf16[2,256,256]{2,1,0:T(8,128)(2,1)}, bf16[1,2,256,256]{3,2,1,0:T(8,128)(2,1)S(1)}, s32[]{:T(128)}, f32[1,256,256]{2,1,0:T(8,128)S(...) while((s32[]{:T(128)}, bf16[2,256,256]{2,1,0:T(8,128)(2,1)}, ...), condition=%wide.region_3.4_spmd.clone, body=%wide.region_0.3_spmd.clone.sunk | while | flops 269615104 | bytes 8126710 | solution.py:164
  5.0 1.9 %collective-permute-start = (bf16[2,256,256]{2,1,0:T(8,128)(2,1)}, bf16[2,256,256]{2,1,0:T(8,128)(2,1)S(1)}, u32[]{:S(2)}, u32[]{:S(2)}) collective-permute-start(bf16[2,256,256]{2,1,0:T(8,128)(2,1)} %get-tuple-element.296), channel_id=1, source_target_pairs={{0,64},{64,128},{128,192},{192,256},{256,320},{320,384},{384,448},... | collective-permute-start | bytes 786440 | tf_op jit(solution)/shard_map/while/body/eval_jaxpr/ppermute | solution.py:15
  6.9 6.0 %collective-permute-done = bf16[2,256,256]{2,1,0:T(8,128)(2,1)S(1)} collective-permute-done((bf16[2,256,256]{2,1,0:T(8,128)(2,1)}, bf16[2,256,256]{2,1,0:T(8,128)(2,1)S(1)}, u32[]{:S(2)}, u32[]{:S(2)}) %collective-permute-start) | collective-permute-done | bytes 262176 | tf_op jit(solution)/shard_map/while/body/eval_jaxpr/ppermute | solution.py:15
  12.9 0.7 conditional.3
  12.9 0.7 broadcast_in_dim.19
  13.8 1.9 %collective-permute-start = (bf16[2,256,256]{2,1,0:T(8,128)(2,1)}, bf16[2,256,256]{2,1,0:T(8,128)(2,1)S(1)}, u32[]{:S(2)}, u32[]{:S(2)}) collective-permute-start(bf16[2,256,256]{2,1,0:T(8,128)(2,1)} %get-tuple-element.296), channel_id=1, source_target_pairs={{0,64},{64,128},{128,192},{192,256},{256,320},{320,384},{384,448},... | collective-permute-start | bytes 786440 | tf_op jit(solution)/shard_map/while/body/eval_jaxpr/ppermute | solution.py:15
  15.7 6.0 %collective-permute-done = bf16[2,256,256]{2,1,0:T(8,128)(2,1)S(1)} collective-permute-done((bf16[2,256,256]{2,1,0:T(8,128)(2,1)}, bf16[2,256,256]{2,1,0:T(8,128)(2,1)S(1)}, u32[]{:S(2)}, u32[]{:S(2)}) %collective-permute-start) | collective-permute-done | bytes 262176 | tf_op jit(solution)/shard_map/while/body/eval_jaxpr/ppermute | solution.py:15
  21.7 0.7 conditional.3
  21.7 0.7 broadcast_in_dim.19
  22.5 1.9 %collective-permute-start = (bf16[2,256,256]{2,1,0:T(8,128)(2,1)}, bf16[2,256,256]{2,1,0:T(8,128)(2,1)S(1)}, u32[]{:S(2)}, u32[]{:S(2)}) collective-permute-start(bf16[2,256,256]{2,1,0:T(8,128)(2,1)} %get-tuple-element.296), channel_id=1, source_target_pairs={{0,64},{64,128},{128,192},{192,256},{256,320},{320,384},{384,448},... | collective-permute-start | bytes 786440 | tf_op jit(solution)/shard_map/while/body/eval_jaxpr/ppermute | solution.py:15
  24.5 6.0 %collective-permute-done = bf16[2,256,256]{2,1,0:T(8,128)(2,1)S(1)} collective-permute-done((bf16[2,256,256]{2,1,0:T(8,128)(2,1)}, bf16[2,256,256]{2,1,0:T(8,128)(2,1)S(1)}, u32[]{:S(2)}, u32[]{:S(2)}) %collective-permute-start) | collective-permute-done | bytes 262176 | tf_op jit(solution)/shard_map/while/body/eval_jaxpr/ppermute | solution.py:15
  30.5 2.4 %conditional.3 = (bf16[2,256,256]{2,1,0:T(8,128)(2,1)}, bf16[1,2,256,256]{3,2,1,0:T(8,128)(2,1)S(1)}) conditional(s32[]{:T(128)} %convert_element_type.162, () %tuple.50, (f32[1,256,256]{2,1,0:T(8,128)S(1)}, bf16[1,256,256]{2,1,0:T(8,128)(2,1)S(1)}, bf16[2,256,256]{2,1,0:T(8,128)(2,1)S(1)}, bf16[1,256,256]{2,1,0:T(8,128)(2,1)S(1)}, ...), branch_computations={%region_1.1_spmd, %region_2.2_spmd} | conditional | flops 269352960 | bytes 6291472 | solution.py:159
  32.2 0.7 pad_maximum_fusion
  33.0 1.9 %collective-permute-start = (bf16[2,256,256]{2,1,0:T(8,128)(2,1)}, bf16[2,256,256]{2,1,0:T(8,128)(2,1)S(1)}, u32[]{:S(2)}, u32[]{:S(2)}) collective-permute-start(bf16[2,256,256]{2,1,0:T(8,128)(2,1)} %get-tuple-element.296), channel_id=1, source_target_pairs={{0,64},{64,128},{128,192},{192,256},{256,320},{320,384},{384,448},... | collective-permute-start | bytes 786440 | tf_op jit(solution)/shard_map/while/body/eval_jaxpr/ppermute | solution.py:15
  34.9 6.0 %collective-permute-done = bf16[2,256,256]{2,1,0:T(8,128)(2,1)S(1)} collective-permute-done((bf16[2,256,256]{2,1,0:T(8,128)(2,1)}, bf16[2,256,256]{2,1,0:T(8,128)(2,1)S(1)}, u32[]{:S(2)}, u32[]{:S(2)}) %collective-permute-start) | collective-permute-done | bytes 262176 | tf_op jit(solution)/shard_map/while/body/eval_jaxpr/ppermute | solution.py:15
  40.9 0.7 conditional.3
  40.9 0.7 broadcast_in_dim.19
  41.8 1.9 %collective-permute-start = (bf16[2,256,256]{2,1,0:T(8,128)(2,1)}, bf16[2,256,256]{2,1,0:T(8,128)(2,1)S(1)}, u32[]{:S(2)}, u32[]{:S(2)}) collective-permute-start(bf16[2,256,256]{2,1,0:T(8,128)(2,1)} %get-tuple-element.296), channel_id=1, source_target_pairs={{0,64},{64,128},{128,192},{192,256},{256,320},{320,384},{384,448},... | collective-permute-start | bytes 786440 | tf_op jit(solution)/shard_map/while/body/eval_jaxpr/ppermute | solution.py:15
  43.7 6.0 %collective-permute-done = bf16[2,256,256]{2,1,0:T(8,128)(2,1)S(1)} collective-permute-done((bf16[2,256,256]{2,1,0:T(8,128)(2,1)}, bf16[2,256,256]{2,1,0:T(8,128)(2,1)S(1)}, u32[]{:S(2)}, u32[]{:S(2)}) %collective-permute-start) | collective-permute-done | bytes 262176 | tf_op jit(solution)/shard_map/while/body/eval_jaxpr/ppermute | solution.py:15
  49.7 0.7 conditional.3
  49.7 0.7 broadcast_in_dim.19
  50.6 1.9 %collective-permute-start = (bf16[2,256,256]{2,1,0:T(8,128)(2,1)}, bf16[2,256,256]{2,1,0:T(8,128)(2,1)S(1)}, u32[]{:S(2)}, u32[]{:S(2)}) collective-permute-start(bf16[2,256,256]{2,1,0:T(8,128)(2,1)} %get-tuple-element.296), channel_id=1, source_target_pairs={{0,64},{64,128},{128,192},{192,256},{256,320},{320,384},{384,448},... | collective-permute-start | bytes 786440 | tf_op jit(solution)/shard_map/while/body/eval_jaxpr/ppermute | solution.py:15
  52.5 6.0 %collective-permute-done = bf16[2,256,256]{2,1,0:T(8,128)(2,1)S(1)} collective-permute-done((bf16[2,256,256]{2,1,0:T(8,128)(2,1)}, bf16[2,256,256]{2,1,0:T(8,128)(2,1)S(1)}, u32[]{:S(2)}, u32[]{:S(2)}) %collective-permute-start) | collective-permute-done | bytes 262176 | tf_op jit(solution)/shard_map/while/body/eval_jaxpr/ppermute | solution.py:15
  58.5 0.7 conditional.3
  58.5 0.7 broadcast_in_dim.19
  59.4 1.9 %collective-permute-start = (bf16[2,256,256]{2,1,0:T(8,128)(2,1)}, bf16[2,256,256]{2,1,0:T(8,128)(2,1)S(1)}, u32[]{:S(2)}, u32[]{:S(2)}) collective-permute-start(bf16[2,256,256]{2,1,0:T(8,128)(2,1)} %get-tuple-element.296), channel_id=1, source_target_pairs={{0,64},{64,128},{128,192},{192,256},{256,320},{320,384},{384,448},... | collective-permute-start | bytes 786440 | tf_op jit(solution)/shard_map/while/body/eval_jaxpr/ppermute | solution.py:15
  61.3 6.0 %collective-permute-done = bf16[2,256,256]{2,1,0:T(8,128)(2,1)S(1)} collective-permute-done((bf16[2,256,256]{2,1,0:T(8,128)(2,1)}, bf16[2,256,256]{2,1,0:T(8,128)(2,1)S(1)}, u32[]{:S(2)}, u32[]{:S(2)}) %collective-permute-start) | collective-permute-done | bytes 262176 | tf_op jit(solution)/shard_map/while/body/eval_jaxpr/ppermute | solution.py:15
  67.3 0.7 conditional.3
  67.3 0.7 broadcast_in_dim.19
  68.1 1.9 %collective-permute-start = (bf16[2,256,256]{2,1,0:T(8,128)(2,1)}, bf16[2,256,256]{2,1,0:T(8,128)(2,1)S(1)}, u32[]{:S(2)}, u32[]{:S(2)}) collective-permute-start(bf16[2,256,256]{2,1,0:T(8,128)(2,1)} %get-tuple-element.296), channel_id=1, source_target_pairs={{0,64},{64,128},{128,192},{192,256},{256,320},{320,384},{384,448},... | collective-permute-start | bytes 786440 | tf_op jit(solution)/shard_map/while/body/eval_jaxpr/ppermute | solution.py:15
  70.1 6.0 %collective-permute-done = bf16[2,256,256]{2,1,0:T(8,128)(2,1)S(1)} collective-permute-done((bf16[2,256,256]{2,1,0:T(8,128)(2,1)}, bf16[2,256,256]{2,1,0:T(8,128)(2,1)S(1)}, u32[]{:S(2)}, u32[]{:S(2)}) %collective-permute-start) | collective-permute-done | bytes 262176 | tf_op jit(solution)/shard_map/while/body/eval_jaxpr/ppermute | solution.py:15
  76.1 0.7 conditional.3
  76.1 0.7 broadcast_in_dim.19
  77.5 33.1 %all_to_all.25 = bf16[16,4,1,2,1024]{4,1,3,2,0:T(4,128)(2,1)S(1)} all-to-all(bf16[16,4,1,2,1024]{4,1,3,2,0:T(4,128)(2,1)S(1)} %copy.8), channel_id=1, replica_groups=mesh['space'=8,'energy_0'=16,'energy_1'=4] {'energy_0'}, dimensions={0} | all-to-all | bytes 524288 | tf_op jit(solution)/shard_map/all_to_all | solution.py:34
  110.8 10.9 %all_to_all.26 = bf16[16,4,1,2,1024]{4,0,3,2,1:T(8,128)(2,1)S(1)} all-to-all(bf16[16,4,1,2,1024]{4,0,3,2,1:T(8,128)(2,1)S(1)} %copy.9), channel_id=1, replica_groups=mesh['space'=8,'energy_0'=16,'energy_1'=4] {'energy_1'}, dimensions={1} | all-to-all | bytes 524288 | tf_op jit(solution)/shard_map/all_to_all | solution.py:34
  122.0 0.4 fusion.145
  122.4 0.4 fusion.47
  122.8 0.4 fusion.43
  123.3 0.5 convolution_subtract_fusion.2
  123.7 0.5 copy-done.3
  124.2 0.5 fusion.41
  125.0 0.3 fusion.111
  125.3 0.3 fusion.38
  126.3 27.8 %all_to_all.27 = bf16[64,2,1024]{2,1,0:T(2,128)(2,1)S(1)} all-to-all(bf16[64,2,1024]{2,1,0:T(2,128)(2,1)S(1)} %copy.11), channel_id=1, replica_groups=mesh['space'=8,'energy_0'=16,'energy_1'=4] {'energy_0','energy_1'}, dimensions={0} | all-to-all | bytes 524288 | tf_op jit(solution)/shard_map/all_to_all | solution.py:172
  154.1 0.9 reshape.108
  (52 shorter events, 6.7 us)
Async XLA Ops:
  0.0 1.2 copy-start.1
  0.0 1.2 copy-start
  1.2 1.0 copy-start.2
  5.0 7.9 %collective-permute-start = (bf16[2,256,256]{2,1,0:T(8,128)(2,1)}, bf16[2,256,256]{2,1,0:T(8,128)(2,1)S(1)}, u32[]{:S(2)}, u32[]{:S(2)}) collective-permute-start(bf16[2,256,256]{2,1,0:T(8,128)(2,1)} %get-tuple-element.296), channel_id=1, source_target_pairs={{0,64},{64,128},{128,192},{192,256},{256,320},{320,384},{384,448},... | collective-permute-start | bytes 786440 | tf_op jit(solution)/shard_map/while/body/eval_jaxpr/ppermute | solution.py:15
  13.8 7.9 %collective-permute-start = (bf16[2,256,256]{2,1,0:T(8,128)(2,1)}, bf16[2,256,256]{2,1,0:T(8,128)(2,1)S(1)}, u32[]{:S(2)}, u32[]{:S(2)}) collective-permute-start(bf16[2,256,256]{2,1,0:T(8,128)(2,1)} %get-tuple-element.296), channel_id=1, source_target_pairs={{0,64},{64,128},{128,192},{192,256},{256,320},{320,384},{384,448},... | collective-permute-start | bytes 786440 | tf_op jit(solution)/shard_map/while/body/eval_jaxpr/ppermute | solution.py:15
  22.5 7.9 %collective-permute-start = (bf16[2,256,256]{2,1,0:T(8,128)(2,1)}, bf16[2,256,256]{2,1,0:T(8,128)(2,1)S(1)}, u32[]{:S(2)}, u32[]{:S(2)}) collective-permute-start(bf16[2,256,256]{2,1,0:T(8,128)(2,1)} %get-tuple-element.296), channel_id=1, source_target_pairs={{0,64},{64,128},{128,192},{192,256},{256,320},{320,384},{384,448},... | collective-permute-start | bytes 786440 | tf_op jit(solution)/shard_map/while/body/eval_jaxpr/ppermute | solution.py:15
  33.0 7.9 %collective-permute-start = (bf16[2,256,256]{2,1,0:T(8,128)(2,1)}, bf16[2,256,256]{2,1,0:T(8,128)(2,1)S(1)}, u32[]{:S(2)}, u32[]{:S(2)}) collective-permute-start(bf16[2,256,256]{2,1,0:T(8,128)(2,1)} %get-tuple-element.296), channel_id=1, source_target_pairs={{0,64},{64,128},{128,192},{192,256},{256,320},{320,384},{384,448},... | collective-permute-start | bytes 786440 | tf_op jit(solution)/shard_map/while/body/eval_jaxpr/ppermute | solution.py:15
  41.8 7.9 %collective-permute-start = (bf16[2,256,256]{2,1,0:T(8,128)(2,1)}, bf16[2,256,256]{2,1,0:T(8,128)(2,1)S(1)}, u32[]{:S(2)}, u32[]{:S(2)}) collective-permute-start(bf16[2,256,256]{2,1,0:T(8,128)(2,1)} %get-tuple-element.296), channel_id=1, source_target_pairs={{0,64},{64,128},{128,192},{192,256},{256,320},{320,384},{384,448},... | collective-permute-start | bytes 786440 | tf_op jit(solution)/shard_map/while/body/eval_jaxpr/ppermute | solution.py:15
  50.6 7.9 %collective-permute-start = (bf16[2,256,256]{2,1,0:T(8,128)(2,1)}, bf16[2,256,256]{2,1,0:T(8,128)(2,1)S(1)}, u32[]{:S(2)}, u32[]{:S(2)}) collective-permute-start(bf16[2,256,256]{2,1,0:T(8,128)(2,1)} %get-tuple-element.296), channel_id=1, source_target_pairs={{0,64},{64,128},{128,192},{192,256},{256,320},{320,384},{384,448},... | collective-permute-start | bytes 786440 | tf_op jit(solution)/shard_map/while/body/eval_jaxpr/ppermute | solution.py:15
  59.4 7.9 %collective-permute-start = (bf16[2,256,256]{2,1,0:T(8,128)(2,1)}, bf16[2,256,256]{2,1,0:T(8,128)(2,1)S(1)}, u32[]{:S(2)}, u32[]{:S(2)}) collective-permute-start(bf16[2,256,256]{2,1,0:T(8,128)(2,1)} %get-tuple-element.296), channel_id=1, source_target_pairs={{0,64},{64,128},{128,192},{192,256},{256,320},{320,384},{384,448},... | collective-permute-start | bytes 786440 | tf_op jit(solution)/shard_map/while/body/eval_jaxpr/ppermute | solution.py:15
  68.1 7.9 %collective-permute-start = (bf16[2,256,256]{2,1,0:T(8,128)(2,1)}, bf16[2,256,256]{2,1,0:T(8,128)(2,1)S(1)}, u32[]{:S(2)}, u32[]{:S(2)}) collective-permute-start(bf16[2,256,256]{2,1,0:T(8,128)(2,1)} %get-tuple-element.296), channel_id=1, source_target_pairs={{0,64},{64,128},{128,192},{192,256},{256,320},{320,384},{384,448},... | collective-permute-start | bytes 786440 | tf_op jit(solution)/shard_map/while/body/eval_jaxpr/ppermute | solution.py:15
  123.3 1.0 copy-start.3
where the time goes:
time: 155 us
  blocking collectives  71.8 us (46%)
  waiting for transfers between devices  47.7 us (31%)
  starting transfers between devices  15.3 us (10%)
  local copies, waits for them, and re-layouts  9.69 us (6%)
  matrix products  8.07 us (5%)
  other arithmetic  1.63 us (1%)
    ppermute x8, waiting for transfers between devices, passed_along(): return lax.ppermute(array, axis, pairs)  47.7 us
    all_to_all x2, blocking collectives, moved_by_axis(): lax.all_to_all(pieces, axes[k], split_axis=k, concat_axis=k, tiled=True)  44.1 us
    all_to_all x1, blocking collectives, local(): lax.all_to_all(result, ENERGY, split_axis=0, concat_axis=2, tiled=True)  27.8 us
    ppermute x8, starting transfers between devices, passed_along(): return lax.ppermute(array, axis, pairs)  15.3 us
    broadcast_in_dim x8, local copies, waits for them, and re-layouts, local(): zero_block = jnp.zeros((2, block_order, block_order), jnp.bfloat16)  5.77 us
    dot_general x12, matrix products, batched(): jnp.einsum(pattern, former, latter, preferred_element_type=jnp.float32)  3.38 us
  transfers between devices with their start and end apart: 8, of which 8 were waited for; matrix products, arithmetic and copies ran while one was open for 0% of the time, Pallas kernels for 0%

commit v1 on v0

v1 whole, which is shorter than its diff:
```python
import math

import jax
import jax.numpy as jnp
from jax import lax
from jax.sharding import Mesh
from jax.sharding import PartitionSpec as P

SPACE = ("chip", "core")
BF16 = jnp.bfloat16
F32 = jnp.float32


def product(left_real, left_imag, right_real, right_imag):
    real_part = jnp.dot(left_real, right_real, preferred_element_type=F32) - jnp.dot(
        left_imag, right_imag, preferred_element_type=F32
    )
    imag_part = jnp.dot(left_real, right_imag, preferred_element_type=F32) + jnp.dot(
        left_imag, right_real, preferred_element_type=F32
    )
    return (real_part, imag_part)


def contract(former, latter):
    return lax.dot_general(former, latter, (((1,), (1,)), ((), ())), preferred_element_type=F32)


def product_adjoint(left_real, left_imag, right_real, right_imag):
    real_part = contract(left_real, right_real) + contract(left_imag, right_imag)
    imag_part = contract(left_imag, right_real) - contract(left_real, right_imag)
    return (real_part, imag_part)


def rounded(pair):
    return (pair[0].astype(BF16), pair[1].astype(BF16))


def applied(matrix, source, green):
    carried = rounded(product(*matrix, *green))
    grown = product_adjoint(*carried, *matrix)
    return (source[0] + grown[0], source[1] + grown[1])


def phase_table(row_count, column_count, length):
    row_index = jnp.arange(row_count, dtype=jnp.int32)[:, None]
    column_index = jnp.arange(column_count, dtype=jnp.int32)[None, :]
    residue = row_index * column_index % length
    return residue.astype(F32) * (2.0 * math.pi / length)


def finish(spectrum_real, spectrum_imag, weights, energy_count, length):
    forward_scale = energy_count ** (-0.5)
    inverse_scale = length ** (-0.5)
    spectrum_real = spectrum_real * forward_scale
    spectrum_imag = spectrum_imag * forward_scale
    weight_values = weights.astype(F32)
    squared_real = (
        (spectrum_real * spectrum_real - spectrum_imag * spectrum_imag) * weight_values
    ).astype(BF16)
    squared_imag = (2.0 * spectrum_real * spectrum_imag * weight_values).astype(BF16)
    inverse_phase = phase_table(energy_count, length, length)
    inverse_real = jnp.cos(inverse_phase).astype(BF16)
    inverse_imag = jnp.sin(inverse_phase).astype(BF16)
    out_real, out_imag = product(inverse_real, inverse_imag, squared_real, squared_imag)
    return jnp.stack([out_real * inverse_scale, out_imag * inverse_scale], axis=1).astype(BF16)


def local(lesser_in, retarded, coupling, interaction):
    block_order = coupling.shape[-1]
    energy_count = lax.axis_size("energy")
    chips = lax.axis_size("chip")
    length = 2 * energy_count
    second = lax.axis_index("core") == 1
    resolvent = (retarded[0, 0, 0], retarded[0, 0, 1])
    matrix = rounded(product(*resolvent, coupling[0, 0], coupling[0, 1]))
    half = rounded(product(*resolvent, lesser_in[0, 0, 0], lesser_in[0, 0, 1]))
    source = product_adjoint(*half, *resolvent)

    first_source = lax.all_gather(jnp.stack(rounded(source)), "core")[0]
    first_matrix = lax.all_gather(jnp.stack(matrix), "core")[0]
    both_matrix = rounded(product(*matrix, first_matrix[0], first_matrix[1]))
    both_source = applied(matrix, source, (first_source[0], first_source[1]))
    matrix = tuple(jnp.where(second, a, b) for a, b in zip(both_matrix, matrix))
    source = tuple(jnp.where(second, a, b) for a, b in zip(both_source, source))

    incoming = jnp.zeros((2, block_order, block_order), BF16)
    green = jnp.stack(rounded(source))
    for hop in range(chips - 1):
        arrived = lax.ppermute(green, SPACE, [(2 * hop + 1, 2 * hop + 3)])
        incoming = incoming + arrived
        green = jnp.stack(rounded(applied(matrix, source, (incoming[0], incoming[1]))))
    incoming = lax.all_gather(incoming, "core")[1]
    green = jnp.stack(rounded(applied(matrix, source, (incoming[0], incoming[1]))))

    entries = green.reshape(2, energy_count, -1).swapaxes(0, 1)
    entries = lax.all_to_all(entries, "energy", split_axis=0, concat_axis=0, tiled=True)
    forward_phase = phase_table(length, energy_count, length)
    forward_real = jnp.cos(forward_phase).astype(BF16)
    forward_imag = (-jnp.sin(forward_phase)).astype(BF16)
    spectrum_real, spectrum_imag = product(forward_real, forward_imag, entries[:, 0], entries[:, 1])
    result = finish(spectrum_real, spectrum_imag, interaction[0], energy_count, length)
    returned = lax.all_to_all(result, "energy", split_axis=0, concat_axis=0, tiled=True)
    return returned.swapaxes(0, 1).reshape(1, 1, 2, block_order, block_order)


def solution(mesh):
    split = Mesh(
        mesh.devices.reshape(mesh.shape["space"] // 2, 2, mesh.shape["energy"]),
        ("chip", "core", "energy"),
    )
    in_specs = (
        P("energy", SPACE, None, None, None),
        P("energy", SPACE, None, None, None),
        P(SPACE, None, None, None),
        P(SPACE, None, "energy"),
    )
    out_specs = P("energy", SPACE, None, None, None)
    return jax.shard_map(local, mesh=split, in_specs=in_specs, out_specs=out_specs, check_vma=False)
```

time: 155 us -> 108 us (0.70)
  the two profiles are of different devices: /device:TPU:2 before, /device:TPU:6 now
where the time goes in v1:
time: 108 us
  blocking collectives  87.5 us (81%)
  matrix products  13.7 us (13%)
  local copies, waits for them, and re-layouts  2.9 us (3%)
  starting transfers between devices  2.03 us (2%)
    all_to_all x1, blocking collectives, local(): lax.all_to_all(entries, 'energy', split_axis=0, concat_axis=0, tiled=True)  38.1 us
    all_to_all x1, blocking collectives, local(): lax.all_to_all(result, 'energy', split_axis=0, concat_axis=0, tiled=True)  26.7 us
    all_gather x1, blocking collectives, local(): incoming = lax.all_gather(incoming, 'core')[1]  18.4 us
    dot_general x20, matrix products, contract(): lax.dot_general(former, latter, (((1,), (1,)), ((), ())), preferred_eleme...  4.37 us
    dot_general x9, matrix products, product(): jnp.dot(left_real, right_imag, preferred_element_type=F32)  3.05 us
    all_gather x1, blocking collectives, local(): first_source = lax.all_gather(jnp.stack(rounded(source)), 'core')[0]  2.18 us
    all_gather x1, blocking collectives, local(): first_matrix = lax.all_gather(jnp.stack(matrix), 'core')[0]  2.18 us
    dot_general x9, matrix products, product(): jnp.dot(left_imag, right_real, preferred_element_type=F32)  2.16 us
  transfers between devices with their start and end apart: 3, of which 0 were waited for; matrix products, arithmetic and copies ran while one was open for 1% of the time, Pallas kernels for 0%

profile of v1, /device:TPU:6, one launch (start us, length us, event | category | flops | bytes accessed | tf_op | source)
XLA Modules:
  0.0 107.7 jit_solution(10064913252791147956)
XLA Ops:
  0.0 1.2 %fusion.51 = f32[256,256]{1,0:T(8,128)S(1)} fusion(bf16[1,1,2,256,256]{4,3,2,1,0:T(8,128)(2,1)} %param.4, bf16[1,1,2,256,256]{4,3,2,1,0:T(8,128)(2,1)} %param.5), kind=kOutput, calls=%fused_computation.100 | convolution fusion | flops 33554432 | bytes 524288 | tf_op jit(solution)/shard_map/dot_general | solution.py:18
  1.4 0.8 copy-done.2
  2.8 0.2 fusion.64
  3.2 0.2 fusion.68
  3.4 0.2 convolution_subtract_fusion.11
  3.8 0.2 convolution_add_fusion.12
  4.1 2.2 %all-gather = bf16[4,256,256]{2,1,0:T(8,128)(2,1)S(1)} all-gather(bf16[2,256,256]{2,1,0:T(8,128)(2,1)S(1)} %pad_maximum_fusion), channel_id=2, replica_groups=mesh['chip'=4,'core'=2,'energy'=64] {'core'}, dimensions={0}, use_global_device_ids=true | all-gather | bytes 786432 | tf_op jit(solution)/shard_map/all_gather | solution.py:79
  7.1 0.2 fusion.151
  7.3 0.2 fusion.17
  7.5 0.2 fusion.150
  7.7 0.2 fusion.10
  8.0 0.2 fusion.12
  8.3 0.7 collective-permute-start
  9.0 2.2 %all-gather.1 = bf16[4,256,256]{2,1,0:T(8,128)(2,1)S(1)} all-gather(bf16[2,256,256]{2,1,0:T(8,128)(2,1)S(1)} %pad_maximum_fusion.1), channel_id=3, replica_groups=mesh['chip'=4,'core'=2,'energy'=64] {'core'}, dimensions={0}, use_global_device_ids=true | all-gather | bytes 786432 | tf_op jit(solution)/shard_map/all_gather | solution.py:80
  11.4 0.2 fusion.22
  11.7 0.2 fusion.42
  12.3 0.2 fusion.153
  12.9 0.2 fusion.152
  13.2 0.2 fusion.40
  13.4 0.2 fusion.41
  13.7 0.7 collective-permute-start.1
  14.8 0.2 fusion.27
  15.0 0.2 fusion.155
  15.4 0.2 fusion.154
  15.6 0.2 fusion.38
  15.9 0.2 fusion.39
  16.1 0.7 collective-permute-start.2
  16.9 18.4 %all-gather.2 = bf16[4,256,256]{2,1,0:T(8,128)(2,1)S(1)} all-gather(bf16[2,256,256]{2,1,0:T(8,128)(2,1)S(1)} %add.115), channel_id=4, replica_groups=mesh['chip'=4,'core'=2,'energy'=64] {'core'}, dimensions={0}, use_global_device_ids=true | all-gather | bytes 786432 | tf_op jit(solution)/shard_map/all_gather | solution.py:92
  35.9 0.2 fusion.157
  36.1 0.2 fusion.30
  36.3 0.2 fusion.156
  36.5 0.2 fusion.33
  36.8 0.2 fusion.32
  37.1 0.6 maximum_bitcast_fusion
  37.7 38.1 %all_to_all.10 = bf16[64,2,1024]{2,1,0:T(2,128)(2,1)S(1)} all-to-all(bf16[64,2,1024]{2,1,0:T(2,128)(2,1)S(1)} %maximum_bitcast_fusion), channel_id=1, replica_groups=mesh['chip'=4,'core'=2,'energy'=64] {'energy'}, dimensions={0} | all-to-all | bytes 524288 | tf_op jit(solution)/shard_map/all_to_all | solution.py:96
  75.8 0.4 fusion.149
  76.1 0.4 fusion.107
  76.6 0.4 fusion.108
  77.0 0.5 convolution_subtract_fusion
  77.5 0.5 copy-done.3
  78.0 0.5 fusion.43
  78.5 0.3 fusion.115
  78.8 0.3 fusion.116
  79.1 0.3 fusion.36
  79.4 0.3 fusion.37
  79.8 0.3 copy.12
  80.1 26.7 %all_to_all.11 = bf16[64,2,1024]{2,1,0:T(2,128)(2,1)S(1)} all-to-all(bf16[64,2,1024]{2,1,0:T(2,128)(2,1)S(1)} %copy.12), channel_id=1, replica_groups=mesh['chip'=4,'core'=2,'energy'=64] {'energy'}, dimensions={0} | all-to-all | bytes 524288 | tf_op jit(solution)/shard_map/all_to_all | solution.py:102
  106.8 0.9 reshape.22
  (45 shorter events, 4.6 us)
Async XLA Ops:
  0.0 1.2 %copy-start.1 = (bf16[1,1,2,256,256]{4,3,2,1,0:T(8,128)(2,1)S(1)}, bf16[1,1,2,256,256]{4,3,2,1,0:T(8,128)(2,1)}, u32[]{:S(2)}) copy-start(bf16[1,1,2,256,256]{4,3,2,1,0:T(8,128)(2,1)} %param.4) | copy-start | bytes 786436
  0.0 1.2 %copy-start = (bf16[1,1,2,256,256]{4,3,2,1,0:T(8,128)(2,1)S(1)}, bf16[1,1,2,256,256]{4,3,2,1,0:T(8,128)(2,1)}, u32[]{:S(2)}) copy-start(bf16[1,1,2,256,256]{4,3,2,1,0:T(8,128)(2,1)} %param.5) | copy-start | bytes 786436
  1.2 1.0 copy-start.2
  8.3 3.7 %collective-permute-start = (bf16[2,256,256]{2,1,0:T(8,128)(2,1)S(1)}, bf16[2,256,256]{2,1,0:T(8,128)(2,1)S(1)}, u32[]{:S(2)}, u32[]{:S(2)}) collective-permute-start(bf16[2,256,256]{2,1,0:T(8,128)(2,1)S(1)} %pad_maximum_fusion.2), channel_id=1, source_target_pairs={{64,192},{65,193},{66,194},{67,195},{68,196},{69,197},{70,198},{71... | collective-permute-start | bytes 786440 | tf_op jit(solution)/shard_map/ppermute | solution.py:89
  13.7 0.7 collective-permute-start.1
  16.1 0.7 collective-permute-start.2
  77.0 1.0 copy-start.3

commit v2 on v1

v2 whole, which is shorter than its diff:
```python
import functools
import math

import jax
import jax.numpy as jnp
from jax import lax
from jax.experimental import pallas as pl
from jax.experimental.pallas import tpu as pltpu
from jax.sharding import Mesh
from jax.sharding import PartitionSpec as P

SPACE = ("chip", "core")
BF16 = jnp.bfloat16
F32 = jnp.float32
LANES = 128
ROWS = 8


def dot(left, right):
    return jnp.dot(left, right, preferred_element_type=F32)


def dot_adjoint(left, right):
    return lax.dot_general(left, right, (((1,), (1,)), ((), ())), preferred_element_type=F32)


def product(left, right):
    real_part = dot(left[0], right[0]) - dot(left[1], right[1])
    imag_part = dot(left[0], right[1]) + dot(left[1], right[0])
    return (real_part, imag_part)


def product_adjoint(left, right):
    real_part = dot_adjoint(left[0], right[0]) + dot_adjoint(left[1], right[1])
    imag_part = dot_adjoint(left[1], right[0]) - dot_adjoint(left[0], right[1])
    return (real_part, imag_part)


def rounded(pair):
    return (pair[0].astype(BF16), pair[1].astype(BF16))


def parts(ref):
    return (ref[0], ref[1])


def put(ref, pair):
    ref[0] = pair[0].astype(ref.dtype)
    ref[1] = pair[1].astype(ref.dtype)


def applied(matrix, source, green):
    carried = rounded(product(matrix, green))
    grown = product_adjoint(carried, matrix)
    return (source[0] + grown[0], source[1] + grown[1])


def call(body, outs, *operands, flops=0):
    outs = [jax.ShapeDtypeStruct(shape, dtype) for shape, dtype in outs]
    size = sum(math.prod(a.shape) * a.dtype.itemsize for a in [*operands, *outs])
    return pl.pallas_call(
        body,
        out_shape=outs if len(outs) > 1 else outs[0],
        compiler_params=pltpu.CompilerParams(vmem_limit_bytes=24 * 2**20),
        cost_estimate=pl.CostEstimate(flops=flops, bytes_accessed=size, transcendentals=0),
    )(*operands)


def prelude_body(lesser_ref, retarded_ref, coupling_ref, matrix_ref, source_ref, sent_ref):
    resolvent = parts(retarded_ref)
    half = rounded(product(resolvent, parts(lesser_ref)))
    source = product_adjoint(half, resolvent)
    put(source_ref, source)
    put(sent_ref, source)
    put(matrix_ref, product(resolvent, parts(coupling_ref)))


def pair_source_body(matrix_ref, source_ref, first_ref, out_ref, green_ref):
    @pl.when(lax.axis_index("core") == 1)
    def _():
        total = applied(parts(matrix_ref), parts(source_ref), parts(first_ref.at[0]))
        put(out_ref, total)
        put(green_ref, total)

    @pl.when(lax.axis_index("core") == 0)
    def _():
        put(out_ref, parts(source_ref))
        put(green_ref, parts(source_ref))


def pair_matrix_body(matrix_ref, first_ref, out_ref):
    @pl.when(lax.axis_index("core") == 1)
    def _():
        put(out_ref, product(parts(matrix_ref), parts(first_ref.at[0])))

    @pl.when(lax.axis_index("core") == 0)
    def _():
        put(out_ref, parts(matrix_ref))


def hop_body(matrix_ref, source_ref, incoming_ref, green_ref):
    put(green_ref, applied(parts(matrix_ref), parts(source_ref), parts(incoming_ref)))


def lower(shape):
    return lax.broadcasted_iota(jnp.int32, shape, 1) < ROWS // 2


def chunked(part):
    left = part[:, :LANES].reshape(-1, ROWS, LANES)
    right = part[:, LANES:].reshape(-1, ROWS, LANES)
    first = lower(left.shape)
    even = jnp.where(first, left, pltpu.roll(right, ROWS // 2, 1))
    odd = jnp.where(first, pltpu.roll(left, ROWS // 2, 1), right)
    return even, odd


def unchunked(even, odd):
    first = lower(even.shape)
    left = jnp.where(first, even, pltpu.roll(odd, ROWS // 2, 1))
    right = jnp.where(first, pltpu.roll(even, ROWS // 2, 1), odd)
    return left.reshape(-1, LANES), right.reshape(-1, LANES)


def last_body(matrix_ref, source_ref, incoming_ref, out_ref):
    green = applied(parts(matrix_ref), parts(source_ref), parts(incoming_ref.at[1]))
    even_real, odd_real = chunked(green[0])
    even_imag, odd_imag = chunked(green[1])
    out_ref[:, 0] = jnp.concatenate([even_real, even_imag], axis=1).astype(BF16)
    out_ref[:, 1] = jnp.concatenate([odd_real, odd_imag], axis=1).astype(BF16)


def spectra_body(chunks_ref, forward_ref, inverse_ref, weights_ref, out_ref, rows_ref):
    count = chunks_ref.shape[0]
    length = weights_ref.shape[0]
    stride = 2 * ROWS
    rows_ref[...] = chunks_ref[...].astype(F32).reshape(rows_ref.shape)
    taken = [rows_ref[pl.ds(i, count, stride=stride), :].astype(BF16) for i in range(stride)]
    values = jnp.concatenate(
        [jnp.concatenate(taken[:ROWS], axis=1), jnp.concatenate(taken[ROWS:], axis=1)], axis=0
    )
    spectrum = dot(forward_ref[...], values) * (count**-0.5)
    order = [2 * (i % 4) + i // 4 for i in range(ROWS)]
    weights = jnp.concatenate(
        [weights_ref[:, LANES * i : LANES * (i + 1)] for i in order], axis=1
    ).astype(F32)
    real, imag = spectrum[:length], spectrum[length:]
    squared_real = ((real * real - imag * imag) * weights).astype(BF16)
    squared_imag = (2.0 * real * imag * weights).astype(BF16)
    result = dot(inverse_ref[...], jnp.concatenate([squared_real, squared_imag], axis=0))
    result = result * (length**-0.5)
    for i in range(ROWS):
        columns = slice(LANES * i, LANES * (i + 1))
        rows_ref[pl.ds(i, count, stride=stride), :] = result[:count, columns]
        rows_ref[pl.ds(i + ROWS, count, stride=stride), :] = result[count:, columns]
    out_ref[...] = rows_ref[...].reshape(out_ref.shape).astype(BF16)


def output_body(chunks_ref, out_ref):
    even = chunks_ref[:, 0].astype(F32)
    odd = chunks_ref[:, 1].astype(F32)
    for part in range(2):
        rows = slice(ROWS * part, ROWS * (part + 1))
        left, right = unchunked(even[:, rows], odd[:, rows])
        out_ref[part] = jnp.concatenate([left, right], axis=1).astype(BF16)


def phase_table(row_count, column_count, length):
    row_index = jnp.arange(row_count, dtype=jnp.int32)[:, None]
    column_index = jnp.arange(column_count, dtype=jnp.int32)[None, :]
    residue = row_index * column_index % length
    return residue.astype(F32) * (2.0 * math.pi / length)


def complex_table(real, imag):
    return jnp.block([[real, -imag], [imag, real]]).astype(BF16)


def spectra(chunks, weights):
    count = chunks.shape[0]
    length = weights.shape[0]
    phase = phase_table(length, count, length)
    forward = complex_table(jnp.cos(phase), -jnp.sin(phase))
    phase = phase_table(count, length, length)
    inverse = complex_table(jnp.cos(phase), jnp.sin(phase))
    return pl.pallas_call(
        spectra_body,
        out_shape=jax.ShapeDtypeStruct(chunks.shape, BF16),
        scratch_shapes=[pltpu.VMEM((count * 2 * ROWS, LANES), F32)],
        compiler_params=pltpu.CompilerParams(vmem_limit_bytes=24 * 2**20),
        cost_estimate=pl.CostEstimate(
            flops=16 * length * count * LANES * ROWS, bytes_accessed=3 * 2**18, transcendentals=0
        ),
    )(chunks, forward, inverse, weights)


def local(lesser_in, retarded, coupling, interaction):
    order = coupling.shape[-1]
    chips = lax.axis_size("chip")
    energies = lax.axis_size("energy")
    shape = (2, order, order)
    chunk = (energies, 2 * ROWS, LANES)
    one = 8 * order**3

    matrix, source, sent = call(
        prelude_body,
        [(shape, BF16), (shape, F32), (shape, BF16)],
        lesser_in[0, 0],
        retarded[0, 0],
        coupling[0],
        flops=3 * one,
    )
    first_source = lax.all_gather(sent, "core")
    source, green = call(
        pair_source_body,
        [(shape, F32), (shape, BF16)],
        matrix,
        source,
        first_source,
        flops=2 * one,
    )
    first_matrix = lax.all_gather(matrix, "core")
    matrix = call(pair_matrix_body, [(shape, BF16)], matrix, first_matrix, flops=one)
    incoming = None
    for hop in range(chips - 1):
        arrived = lax.ppermute(green, SPACE, [(2 * hop + 1, 2 * hop + 3)])
        incoming = arrived if incoming is None else incoming + arrived
        if hop < chips - 2:
            green = call(hop_body, [(shape, BF16)], matrix, source, incoming, flops=2 * one)
    incoming = lax.all_gather(incoming, "core")
    chunks = call(
        last_body,
        [((energies // 2, 2, 2 * ROWS, LANES), BF16)],
        matrix,
        source,
        incoming,
        flops=2 * one,
    )
    chunks = lax.all_to_all(
        chunks.reshape(chunk), "energy", split_axis=0, concat_axis=0, tiled=True
    )
    result = spectra(chunks, interaction[0])
    returned = lax.all_to_all(result, "energy", split_axis=0, concat_axis=0, tiled=True)
    out = call(
        output_body,
        [(shape, BF16)],
        returned.reshape(energies // 2, 2, 2 * ROWS, LANES),
    )
    return out.reshape(1, 1, *shape)


def solution(mesh):
    split = Mesh(
        mesh.devices.reshape(mesh.shape["space"] // 2, 2, mesh.shape["energy"]),
        ("chip", "core", "energy"),
    )
    in_specs = (
        P("energy", SPACE, None, None, None),
        P("energy", SPACE, None, None, None),
        P(SPACE, None, None, None),
        P(SPACE, None, "energy"),
    )
    out_specs = P("energy", SPACE, None, None, None)
    return jax.shard_map(local, mesh=split, in_specs=in_specs, out_specs=out_specs, check_vma=False)
```

time: 108 us -> 99.4 us (0.920)
  blocking collectives: 87.5 us -> 50.9 us
  waiting for transfers between devices: 0.01 us -> 22.1 us
  starting transfers between devices: 2.03 us -> 17.2 us
  matrix products: 13.7 us -> 0 us
  Pallas kernels: 0 us -> 4.86 us
    all_to_all x1 -> x0, blocking collectives: 38.1 us -> none  [local(): lax.all_to_all(entries, 'energy', split_axis=0, concat_axis=0, tiled=True)]
    all_to_all x0 -> x1, waiting for transfers between devices: none -> 22.1 us  [local(): lax.all_to_all(chunks.reshape(chunk), 'energy', split_axis=0, concat_axis...]
    all_to_all x0 -> x1, starting transfers between devices: none -> 15.2 us  [local(): lax.all_to_all(chunks.reshape(chunk), 'energy', split_axis=0, concat_axis...]
    dot_general x56 -> x0, matrix products: 13.7 us -> none  [the longest x20 4.37 us: contract(): lax.dot_general(former, latter, (((1,), (1,)), ((), ())), preferred_eleme...]
    pallas_call x0 -> x8, Pallas kernels: none -> 4.86 us  [the longest x7 4.14 us: call(): pl.pallas_call(body, out_shape=outs if len(outs) > 1 else outs[0], compil...]
    unnamed x8, local copies, waits for them, and re-layouts: 1.25 us -> 2.85 us
    all_gather x3, blocking collectives: 22.8 us -> 24.2 us  [the longest x1 19.4 us: local(): incoming = lax.all_gather(incoming, 'core')]
  transfers between devices with their start and end apart: 3 -> 4, of which waited for: 0 -> 1; matrix products, arithmetic and copies ran while one was open for 1% -> 1% of each run, Pallas kernels for 0% -> 0%
where the time goes in v2:
time: 99.4 us; the launch traced here: 99.1 us
  blocking collectives  50.9 us (51%)
  waiting for transfers between devices  22.1 us (22%)
  starting transfers between devices  17.2 us (17%)
  Pallas kernels  4.86 us (5%)
  local copies, waits for them, and re-layouts  2.85 us (3%)
  other arithmetic  1.08 us (1%)
    all_to_all x1, blocking collectives, local(): lax.all_to_all(result, 'energy', split_axis=0, concat_axis=0, tiled=True)  26.7 us
    all_to_all x1, waiting for transfers between devices, local(): lax.all_to_all(chunks.reshape(chunk), 'energy', split_axis=0, concat_axis...  22.1 us
    all_gather x1, blocking collectives, local(): incoming = lax.all_gather(incoming, 'core')  19.4 us
    all_to_all x1, starting transfers between devices, local(): lax.all_to_all(chunks.reshape(chunk), 'energy', split_axis=0, concat_axis...  15.2 us
    pallas_call x7, Pallas kernels, call(): pl.pallas_call(body, out_shape=outs if len(outs) > 1 else outs[0], compil...  4.14 us
    unnamed x8, local copies, waits for them, and re-layouts  2.85 us
    all_gather x1, blocking collectives, local(): first_matrix = lax.all_gather(matrix, 'core')  2.55 us
    all_gather x1, blocking collectives, local(): first_source = lax.all_gather(sent, 'core')  2.18 us
  transfers between devices with their start and end apart: 4, of which 1 were waited for; matrix products, arithmetic and copies ran while one was open for 1% of the time, Pallas kernels for 0%

profile of v2, /device:TPU:6, one launch (start us, length us, event | category | flops | bytes accessed | tf_op | source)
XLA Modules:
  0.0 99.1 jit_solution(5061207746082501574)
XLA Ops:
  0.0 0.0 copy-start.1
  0.0 0.9 copy-done.1
  1.0 0.0 copy-start.2
  1.0 0.9 copy-done.2
  1.9 0.0 copy-start.3
  1.9 0.9 copy-done.3
  2.9 0.7 shard_map.46
  3.5 2.2 %all-gather.1 = bf16[4,256,256]{2,1,0:T(8,128)(2,1)S(1)} all-gather(bf16[2,256,256]{2,1,0:T(8,128)(2,1)S(1)} %get-tuple-element.12), channel_id=3, replica_groups=mesh['chip'=4,'core'=2,'energy'=64] {'core'}, dimensions={0}, use_global_device_ids=true | all-gather | bytes 786432 | tf_op jit(solution)/shard_map/all_gather | solution.py:213
  5.7 0.1 shard_map.48
  5.7 0.7 collective-permute-start
  6.4 2.5 %all-gather = bf16[4,256,256]{2,1,0:T(8,128)(2,1)S(1)} all-gather(bf16[2,256,256]{2,1,0:T(8,128)(2,1)S(1)} %get-tuple-element.10.matrix_ref), channel_id=2, replica_groups=mesh['chip'=4,'core'=2,'energy'=64] {'core'}, dimensions={0}, use_global_device_ids=true | all-gather | bytes 786432 | tf_op jit(solution)/shard_map/all_gather | solution.py:222
  9.0 0.0 collective-permute-done.incoming_ref
  9.0 0.7 shard_map.49
  9.7 0.7 collective-permute-start.1
  10.4 0.0 collective-permute-done.1
  10.4 0.1 add.30.incoming_ref
  10.4 0.7 shard_map.50
  11.1 0.7 collective-permute-start.2
  11.8 0.0 collective-permute-done.2
  11.8 0.1 add.31
  11.9 19.4 %all-gather.2 = bf16[4,256,256]{2,1,0:T(8,128)(2,1)S(1)} all-gather(bf16[2,256,256]{2,1,0:T(8,128)(2,1)S(1)} %add.31), channel_id=4, replica_groups=mesh['chip'=4,'core'=2,'energy'=64] {'core'}, dimensions={0}, use_global_device_ids=true | all-gather | bytes 786432 | tf_op jit(solution)/shard_map/all_gather | solution.py:230
  31.3 1.4 %shard_map.51 = bf16[32,2,16,128]{3,2,1,0:T(8,128)(2,1)} custom-call(bf16[2,256,256]{2,1,0:T(8,128)(2,1)S(1)} %shard_map.47.matrix_ref, f32[2,256,256]{2,1,0:T(8,128)S(1)} %get-tuple-element.13.source_ref, bf16[2,2,256,256]{3,2,1,0:T(8,128)(2,1)S(1)} %bitcast.10), custom_call_target="tpu_custom_call" | custom-call | flops 268435456 | bytes 1572864 | tf_op jit(solution)/shard_map/pallas_call | solution.py:61
  32.6 15.2 %all-to-all-start = ((bf16[64,16,128]{2,1,0:T(8,128)(2,1)}), bf16[64,16,128]{2,1,0:T(8,128)(2,1)S(1)}, u32[]{:S(2)}, u32[]{:S(2)}) async-start(bf16[64,16,128]{2,1,0:T(8,128)(2,1)} %bitcast.6), calls=%async_computation | async-start | bytes 524288 | tf_op jit(solution)/shard_map/all_to_all | solution.py:239
  47.9 0.0 copy-start
  47.9 0.1 fusion.15
  48.0 0.3 fusion.12
  48.3 0.2 negate_convert_fusion.1
  48.4 0.3 negate_convert_fusion
  48.7 0.1 maximum_maximum_fusion.forward_ref
  48.8 22.1 %all-to-all-done.chunks_ref = bf16[64,16,128]{2,1,0:T(8,128)(2,1)S(1)} async-done(((bf16[64,16,128]{2,1,0:T(8,128)(2,1)}), bf16[64,16,128]{2,1,0:T(8,128)(2,1)S(1)}, u32[]{:S(2)}, u32[]{:S(2)}) %all-to-all-start) | async-done | bytes 262176 | tf_op jit(solution)/shard_map/all_to_all | solution.py:239
  70.9 0.0 copy-done
  70.9 0.7 shard_map.52
  71.6 26.7 %all_to_all.10 = bf16[64,16,128]{2,1,0:T(8,128)(2,1)S(1)} all-to-all(bf16[64,16,128]{2,1,0:T(8,128)(2,1)S(1)} %shard_map.52), channel_id=1, replica_groups=mesh['chip'=4,'core'=2,'energy'=64] {'energy'}, dimensions={0} | all-to-all | bytes 524288 | tf_op jit(solution)/shard_map/all_to_all | solution.py:243
  98.3 0.8 shard_map.53
  (2 shorter events, 0.0 us)
Async XLA Ops:
  0.0 0.9 copy-start.1
  1.0 0.9 copy-start.2
  1.9 0.9 copy-start.3
  5.7 3.3 %collective-permute-start = (bf16[2,256,256]{2,1,0:T(8,128)(2,1)S(1)}, bf16[2,256,256]{2,1,0:T(8,128)(2,1)S(1)}, u32[]{:S(2)}, u32[]{:S(2)}) collective-permute-start(bf16[2,256,256]{2,1,0:T(8,128)(2,1)S(1)} %get-tuple-element.14), channel_id=1, source_target_pairs={{64,192},{65,193},{66,194},{67,195},{68,196},{69,197},{70,198},{71... | collective-permute-start | bytes 786440 | tf_op jit(solution)/shard_map/ppermute | solution.py:226
  9.7 0.7 collective-permute-start.1
  11.1 0.7 collective-permute-start.2
  32.6 38.3 %all-to-all-start = ((bf16[64,16,128]{2,1,0:T(8,128)(2,1)}), bf16[64,16,128]{2,1,0:T(8,128)(2,1)S(1)}, u32[]{:S(2)}, u32[]{:S(2)}) async-start(bf16[64,16,128]{2,1,0:T(8,128)(2,1)} %bitcast.6), calls=%async_computation | async-start | bytes 524288 | tf_op jit(solution)/shard_map/all_to_all | solution.py:239
  47.9 23.1 %copy-start = (bf16[1,128,1024]{2,1,0:T(8,128)(2,1)S(1)}, bf16[1,128,1024]{2,1,0:T(8,128)(2,1)}, u32[]{:S(2)}) copy-start(bf16[1,128,1024]{2,1,0:T(8,128)(2,1)} %param.7) | copy-start | bytes 786436

commit v3 on v2

--- a/solution.py
+++ b/solution.py
@@ -14,6 +14,8 @@
 F32 = jnp.float32
 LANES = 128
 ROWS = 8
+FIRST_OUT = 42
+FIRST_BACK = 42
 
 
 def dot(left, right):
@@ -66,13 +68,39 @@
     )(*operands)
 
 
-def prelude_body(lesser_ref, retarded_ref, coupling_ref, matrix_ref, source_ref, sent_ref):
-    resolvent = parts(retarded_ref)
-    half = rounded(product(resolvent, parts(lesser_ref)))
+def prelude_body(
+    lesser_hbm, retarded_hbm, coupling_hbm, matrix_ref, source_ref, sent_ref, loaded, semaphores
+):
+    copies = [
+        pltpu.make_async_copy(ref, loaded.at[i], semaphores.at[i])
+        for i, ref in enumerate((retarded_hbm, lesser_hbm, coupling_hbm))
+    ]
+    for copy in copies:
+        copy.start()
+    copies[0].wait()
+    copies[1].wait()
+    resolvent = parts(loaded.at[0])
+    half = rounded(product(resolvent, parts(loaded.at[1])))
     source = product_adjoint(half, resolvent)
     put(source_ref, source)
     put(sent_ref, source)
-    put(matrix_ref, product(resolvent, parts(coupling_ref)))
+    copies[2].wait()
+    put(matrix_ref, product(resolvent, parts(loaded.at[2])))
+
+
+def prelude(lesser_in, retarded, coupling):
+    shape = coupling.shape
+    return pl.pallas_call(
+        prelude_body,
+        out_shape=[jax.ShapeDtypeStruct(shape, dtype) for dtype in (BF16, F32, BF16)],
+        in_specs=[pl.BlockSpec(memory_space=pltpu.HBM)] * 3,
+        out_specs=[pl.BlockSpec(memory_space=pltpu.VMEM)] * 3,
+        scratch_shapes=[pltpu.VMEM((3, *shape), BF16), pltpu.SemaphoreType.DMA((3,))],
+        compiler_params=pltpu.CompilerParams(vmem_limit_bytes=24 * 2**20),
+        cost_estimate=pl.CostEstimate(
+            flops=24 * shape[-1] ** 3, bytes_accessed=2**20, transcendentals=0
+        ),
+    )(*(pltpu.with_memory_space_constraint(a, pltpu.HBM) for a in (lesser_in, retarded, coupling)))
 
 
 def pair_source_body(matrix_ref, source_ref, first_ref, out_ref, green_ref):
@@ -100,6 +128,16 @@
 
 def hop_body(matrix_ref, source_ref, incoming_ref, green_ref):
     put(green_ref, applied(parts(matrix_ref), parts(source_ref), parts(incoming_ref)))
+
+
+def joined_body(source_ref, matrix_ref, near_ref, far_ref, out_ref):
+    @pl.when(lax.axis_index("chip") == 3)
+    def _():
+        put(out_ref, applied(parts(matrix_ref), parts(source_ref), parts(far_ref)))
+
+    @pl.when(lax.axis_index("chip") != 3)
+    def _():
+        out_ref[...] = source_ref[...] + near_ref[...]
 
 
 def lower(shape):
@@ -122,12 +160,26 @@
     return left.reshape(-1, LANES), right.reshape(-1, LANES)
 
 
+def rolled(count, start):
+    if start == 0:
+        return [(slice(0, count), slice(0, count))]
+    return [
+        (slice(0, count - start), slice(start, count)),
+        (slice(count - start, count), slice(0, start)),
+    ]
+
+
 def last_body(matrix_ref, source_ref, incoming_ref, out_ref):
     green = applied(parts(matrix_ref), parts(source_ref), parts(incoming_ref.at[1]))
     even_real, odd_real = chunked(green[0])
     even_imag, odd_imag = chunked(green[1])
-    out_ref[:, 0] = jnp.concatenate([even_real, even_imag], axis=1).astype(BF16)
-    out_ref[:, 1] = jnp.concatenate([odd_real, odd_imag], axis=1).astype(BF16)
+    even = jnp.concatenate([even_real, even_imag], axis=1).astype(BF16)
+    odd = jnp.concatenate([odd_real, odd_imag], axis=1).astype(BF16)
+    pairs = out_ref.shape[0]
+    start = FIRST_OUT // 2
+    for target, taken in rolled(pairs, start):
+        out_ref[target, 0] = even[taken]
+        out_ref[target, 1] = odd[taken]
 
 
 def spectra_body(chunks_ref, forward_ref, inverse_ref, weights_ref, out_ref, rows_ref):
@@ -162,7 +214,9 @@
     for part in range(2):
         rows = slice(ROWS * part, ROWS * (part + 1))
         left, right = unchunked(even[:, rows], odd[:, rows])
-        out_ref[part] = jnp.concatenate([left, right], axis=1).astype(BF16)
+        value = jnp.concatenate([left, right], axis=1).astype(BF16)
+        for taken, target in rolled(value.shape[0], 2 * ROWS // 4 * FIRST_BACK):
+            out_ref[part, target] = value[taken]
 
 
 def phase_table(row_count, column_count, length):
@@ -180,8 +234,10 @@
     count = chunks.shape[0]
     length = weights.shape[0]
     phase = phase_table(length, count, length)
+    phase = jnp.roll(phase, -FIRST_OUT, axis=1)
     forward = complex_table(jnp.cos(phase), -jnp.sin(phase))
     phase = phase_table(count, length, length)
+    phase = jnp.roll(phase, -FIRST_BACK, axis=0)
     inverse = complex_table(jnp.cos(phase), jnp.sin(phase))
     return pl.pallas_call(
         spectra_body,
@@ -194,22 +250,22 @@
     )(chunks, forward, inverse, weights)
 
 
+def exchanged(chunks, first):
+    count = chunks.shape[0]
+    group = [(first + i) % count for i in range(count)]
+    return lax.all_to_all(
+        chunks, "energy", split_axis=0, concat_axis=0, axis_index_groups=[group], tiled=True
+    )
+
+
 def local(lesser_in, retarded, coupling, interaction):
     order = coupling.shape[-1]
-    chips = lax.axis_size("chip")
     energies = lax.axis_size("energy")
     shape = (2, order, order)
     chunk = (energies, 2 * ROWS, LANES)
     one = 8 * order**3
 
-    matrix, source, sent = call(
-        prelude_body,
-        [(shape, BF16), (shape, F32), (shape, BF16)],
-        lesser_in[0, 0],
-        retarded[0, 0],
-        coupling[0],
-        flops=3 * one,
-    )
+    matrix, source, sent = prelude(lesser_in[0, 0], retarded[0, 0], coupling[0])
     first_source = lax.all_gather(sent, "core")
     source, green = call(
         pair_source_body,
@@ -221,12 +277,14 @@
     )
     first_matrix = lax.all_gather(matrix, "core")
     matrix = call(pair_matrix_body, [(shape, BF16)], matrix, first_matrix, flops=one)
-    incoming = None
-    for hop in range(chips - 1):
-        arrived = lax.ppermute(green, SPACE, [(2 * hop + 1, 2 * hop + 3)])
-        incoming = arrived if incoming is None else incoming + arrived
-        if hop < chips - 2:
-            green = call(hop_body, [(shape, BF16)], matrix, source, incoming, flops=2 * one)
+    arrived_source = lax.ppermute(green, SPACE, [(1, 3), (5, 7)])
+    arrived_matrix = lax.ppermute(matrix, SPACE, [(5, 7)])
+    green = call(hop_body, [(shape, BF16)], matrix, source, arrived_source, flops=2 * one)
+    far = lax.ppermute(green, SPACE, [(3, 7)])
+    near = lax.ppermute(green, SPACE, [(3, 5)])
+    incoming = call(
+        joined_body, [(shape, BF16)], arrived_source, arrived_matrix, near, far, flops=2 * one
+    )
     incoming = lax.all_gather(incoming, "core")
     chunks = call(
         last_body,
@@ -236,11 +294,9 @@
         incoming,
         flops=2 * one,
     )
-    chunks = lax.all_to_all(
-        chunks.reshape(chunk), "energy", split_axis=0, concat_axis=0, tiled=True
-    )
+    chunks = exchanged(chunks.reshape(chunk), FIRST_OUT)
     result = spectra(chunks, interaction[0])
-    returned = lax.all_to_all(result, "energy", split_axis=0, concat_axis=0, tiled=True)
+    returned = exchanged(result, FIRST_BACK)
     out = call(
         output_body,
         [(shape, BF16)],

time: 99.4 us -> 89.5 us (0.900)
  waiting for transfers between devices: 22.1 us -> 11.9 us
  starting transfers between devices: 17.2 us -> 22 us
  blocking collectives: 50.9 us -> 46.8 us
  local copies, waits for them, and re-layouts: 2.85 us -> 1.34 us
  Pallas kernels: 4.86 us -> 6.23 us
    all_to_all x1, waiting for transfers between devices: 22.1 us -> 11.9 us  [exchanged(): lax.all_to_all(chunks, 'energy', split_axis=0, concat_axis=0, axis_index_...]
    all_gather x1, blocking collectives: 19.4 us -> 14.7 us  [local(): incoming = lax.all_gather(incoming, 'core')]
    all_to_all x1, starting transfers between devices: 15.2 us -> 19.3 us  [exchanged(): lax.all_to_all(chunks, 'energy', split_axis=0, concat_axis=0, axis_index_...]
    unnamed x8 -> x4, local copies, waits for them, and re-layouts: 2.85 us -> 0.6 us
    pallas_call x0 -> x1, Pallas kernels: none -> 2.01 us  [prelude(): pl.pallas_call(prelude_body, out_shape=[jax.ShapeDtypeStruct(shape, dtype...]
    ppermute x3 -> x4, starting transfers between devices: 2.03 us -> 2.71 us  [the longest x1 0.68 us: local(): arrived_source = lax.ppermute(green, SPACE, [(1, 3), (5, 7)])]
    pallas_call x7 -> x6, Pallas kernels: 4.14 us -> 3.51 us  [call(): pl.pallas_call(body, out_shape=outs if len(outs) > 1 else outs[0], compil...]
  transfers between devices with their start and end apart: 4 -> 5, of which waited for: 1 -> 1; matrix products, arithmetic and copies ran while one was open for 1% -> 1% of each run, Pallas kernels for 0% -> 1%
where the time goes in v3:
time: 89.5 us; the launch traced here: 89.1 us
  blocking collectives  46.8 us (52%)
  starting transfers between devices  22 us (25%)
  waiting for transfers between devices  11.9 us (13%)
  Pallas kernels  6.23 us (7%)
  local copies, waits for them, and re-layouts  1.34 us (1%)
    all_to_all x1, blocking collectives, exchanged(): lax.all_to_all(chunks, 'energy', split_axis=0, concat_axis=0, axis_index_...  26.8 us
    all_to_all x1, starting transfers between devices, exchanged(): lax.all_to_all(chunks, 'energy', split_axis=0, concat_axis=0, axis_index_...  19.3 us
    all_gather x1, blocking collectives, local(): incoming = lax.all_gather(incoming, 'core')  14.7 us
    all_to_all x1, waiting for transfers between devices, exchanged(): lax.all_to_all(chunks, 'energy', split_axis=0, concat_axis=0, axis_index_...  11.9 us
    pallas_call x6, Pallas kernels, call(): pl.pallas_call(body, out_shape=outs if len(outs) > 1 else outs[0], compil...  3.51 us
    all_gather x1, blocking collectives, local(): first_matrix = lax.all_gather(matrix, 'core')  3.16 us
    all_gather x1, blocking collectives, local(): first_source = lax.all_gather(sent, 'core')  2.18 us
    pallas_call x1, Pallas kernels, prelude(): pl.pallas_call(prelude_body, out_shape=[jax.ShapeDtypeStruct(shape, dtype...  2.01 us
  transfers between devices with their start and end apart: 5, of which 1 were waited for; matrix products, arithmetic and copies ran while one was open for 1% of the time, Pallas kernels for 1%

profile of v3, /device:TPU:6, one launch (start us, length us, event | category | flops | bytes accessed | tf_op | source)
XLA Modules:
  0.0 89.1 jit_solution(10108628475921504409)
XLA Ops:
  0.0 2.0 %shard_map.46 = (bf16[2,256,256]{2,1,0:T(8,128)(2,1)S(1)}, f32[2,256,256]{2,1,0:T(8,128)S(1)}, bf16[2,256,256]{2,1,0:T(8,128)(2,1)S(1)}) custom-call(bf16[2,256,256]{2,1,0:T(8,128)(2,1)} %bitcast.17, bf16[2,256,256]{2,1,0:T(8,128)(2,1)} %bitcast.18, bf16[2,256,256]{2,1,0:T(8,128)(2,1)} %bitcast.19), custom_call_target="tpu_custom_call" | custom-call | flops 402653184 | bytes 1048576 | tf_op jit(solution)/shard_map/pallas_call | solution.py:93
  2.0 2.2 %all-gather.1 = bf16[4,256,256]{2,1,0:T(8,128)(2,1)S(1)} all-gather(bf16[2,256,256]{2,1,0:T(8,128)(2,1)S(1)} %get-tuple-element.12), channel_id=3, replica_groups=mesh['chip'=4,'core'=2,'energy'=64] {'core'}, dimensions={0}, use_global_device_ids=true | all-gather | bytes 786432 | tf_op jit(solution)/shard_map/all_gather | solution.py:269
  4.2 0.1 shard_map.48
  4.3 0.7 collective-permute-start
  4.9 3.2 %all-gather = bf16[4,256,256]{2,1,0:T(8,128)(2,1)S(1)} all-gather(bf16[2,256,256]{2,1,0:T(8,128)(2,1)S(1)} %get-tuple-element.10.matrix_ref), channel_id=2, replica_groups=mesh['chip'=4,'core'=2,'energy'=64] {'core'}, dimensions={0}, use_global_device_ids=true | all-gather | bytes 786432 | tf_op jit(solution)/shard_map/all_gather | solution.py:278
  8.1 0.7 collective-permute-start.1
  8.8 0.0 collective-permute-done.incoming_ref.source_ref
  8.8 0.7 shard_map.49
  9.5 0.7 collective-permute-start.2
  10.2 0.7 collective-permute-start.3
  10.9 0.0 collective-permute-done.1.matrix_ref
  10.9 0.0 collective-permute-done.2.near_ref
  10.9 0.0 collective-permute-done.3.far_ref
  10.9 0.7 shard_map.50
  11.6 14.7 %all-gather.2 = bf16[4,256,256]{2,1,0:T(8,128)(2,1)S(1)} all-gather(bf16[2,256,256]{2,1,0:T(8,128)(2,1)S(1)} %shard_map.50), channel_id=4, replica_groups=mesh['chip'=4,'core'=2,'energy'=64] {'core'}, dimensions={0}, use_global_device_ids=true | all-gather | bytes 786432 | tf_op jit(solution)/shard_map/all_gather | solution.py:288
  26.3 1.4 %shard_map.51 = bf16[32,2,16,128]{3,2,1,0:T(8,128)(2,1)} custom-call(bf16[2,256,256]{2,1,0:T(8,128)(2,1)S(1)} %shard_map.47.matrix_ref, f32[2,256,256]{2,1,0:T(8,128)S(1)} %get-tuple-element.13.source_ref, bf16[2,2,256,256]{3,2,1,0:T(8,128)(2,1)S(1)} %bitcast.11), custom_call_target="tpu_custom_call" | custom-call | flops 268435456 | bytes 1572864 | tf_op jit(solution)/shard_map/pallas_call | solution.py:63
  27.6 19.3 %all-to-all-start = ((bf16[64,16,128]{2,1,0:T(8,128)(2,1)}), bf16[64,16,128]{2,1,0:T(8,128)(2,1)S(1)}, u32[]{:S(2)}, u32[]{:S(2)}) async-start(bf16[64,16,128]{2,1,0:T(8,128)(2,1)} %bitcast.6), calls=%async_computation | async-start | bytes 524288 | tf_op jit(solution)/shard_map/all_to_all | solution.py:256
  46.9 0.0 copy-start.1
  46.9 0.6 copy-done.1
  47.6 0.0 slice-start
  47.6 0.1 slice.20
  47.7 0.7 slice-done
  48.3 0.1 negate_convert_fusion.1
  48.5 0.0 copy-start
  48.5 0.3 fusion.15
  48.8 0.1 maximum_maximum_fusion.forward_ref
  48.9 11.9 %all-to-all-done.chunks_ref = bf16[64,16,128]{2,1,0:T(8,128)(2,1)S(1)} async-done(((bf16[64,16,128]{2,1,0:T(8,128)(2,1)}), bf16[64,16,128]{2,1,0:T(8,128)(2,1)S(1)}, u32[]{:S(2)}, u32[]{:S(2)}) %all-to-all-start) | async-done | bytes 262176 | tf_op jit(solution)/shard_map/all_to_all | solution.py:256
  60.8 0.0 copy-done
  60.8 0.7 shard_map.52
  61.5 26.8 %all_to_all.10 = bf16[64,16,128]{2,1,0:T(8,128)(2,1)S(1)} all-to-all(bf16[64,16,128]{2,1,0:T(8,128)(2,1)S(1)} %shard_map.52), channel_id=1, replica_groups={{42,43,44,45,46,47,48,49,50,51,52,53,54,55,56,57,58,59,60,61,62,63,0,1,..., dimensions={0} | all-to-all | bytes 524288 | tf_op jit(solution)/shard_map/all_to_all | solution.py:256
  88.3 0.8 shard_map.53
  (5 shorter events, 0.1 us)
Async XLA Ops:
  4.3 4.6 %collective-permute-start = (bf16[2,256,256]{2,1,0:T(8,128)(2,1)S(1)}, bf16[2,256,256]{2,1,0:T(8,128)(2,1)S(1)}, u32[]{:S(2)}, u32[]{:S(2)}) collective-permute-start(bf16[2,256,256]{2,1,0:T(8,128)(2,1)S(1)} %get-tuple-element.14), channel_id=1, source_target_pairs={{64,192},{320,448},{65,193},{321,449},{66,194},{322,450},{67,195},... | collective-permute-start | bytes 786440 | tf_op jit(solution)/shard_map/ppermute | solution.py:280
  8.1 2.7 %collective-permute-start.1 = (bf16[2,256,256]{2,1,0:T(8,128)(2,1)S(1)}, bf16[2,256,256]{2,1,0:T(8,128)(2,1)S(1)}, u32[]{:S(2)}, u32[]{:S(2)}) collective-permute-start(bf16[2,256,256]{2,1,0:T(8,128)(2,1)S(1)} %shard_map.47.matrix_ref), channel_id=1, source_target_pairs={{320,448},{321,449},{322,450},{323,451},{324,452},{325,453},{326,4... | collective-permute-start | bytes 786440 | tf_op jit(solution)/shard_map/ppermute | solution.py:281
  9.5 1.4 %collective-permute-start.2 = (bf16[2,256,256]{2,1,0:T(8,128)(2,1)S(1)}, bf16[2,256,256]{2,1,0:T(8,128)(2,1)S(1)}, u32[]{:S(2)}, u32[]{:S(2)}) collective-permute-start(bf16[2,256,256]{2,1,0:T(8,128)(2,1)S(1)} %shard_map.49), channel_id=1, source_target_pairs={{192,320},{193,321},{194,322},{195,323},{196,324},{197,325},{198,3... | collective-permute-start | bytes 786440 | tf_op jit(solution)/shard_map/ppermute | solution.py:284
  10.2 0.7 collective-permute-start.3
  27.6 33.2 %all-to-all-start = ((bf16[64,16,128]{2,1,0:T(8,128)(2,1)}), bf16[64,16,128]{2,1,0:T(8,128)(2,1)S(1)}, u32[]{:S(2)}, u32[]{:S(2)}) async-start(bf16[64,16,128]{2,1,0:T(8,128)(2,1)} %bitcast.6), calls=%async_computation | async-start | bytes 524288 | tf_op jit(solution)/shard_map/all_to_all | solution.py:256
  46.9 0.6 copy-start.1
  47.6 0.7 slice-start
  48.5 12.4 %copy-start = (bf16[1,128,1024]{2,1,0:T(8,128)(2,1)S(1)}, bf16[1,128,1024]{2,1,0:T(8,128)(2,1)}, u32[]{:S(2)}) copy-start(bf16[1,128,1024]{2,1,0:T(8,128)(2,1)} %param.7) | copy-start | bytes 786436

commit v4 on v3

--- a/solution.py
+++ b/solution.py
@@ -103,41 +103,50 @@
     )(*(pltpu.with_memory_space_constraint(a, pltpu.HBM) for a in (lesser_in, retarded, coupling)))
 
 
-def pair_source_body(matrix_ref, source_ref, first_ref, out_ref, green_ref):
-    @pl.when(lax.axis_index("core") == 1)
-    def _():
-        total = applied(parts(matrix_ref), parts(source_ref), parts(first_ref.at[0]))
-        put(out_ref, total)
-        put(green_ref, total)
-
-    @pl.when(lax.axis_index("core") == 0)
-    def _():
-        put(out_ref, parts(source_ref))
-        put(green_ref, parts(source_ref))
-
-
-def pair_matrix_body(matrix_ref, first_ref, out_ref):
-    @pl.when(lax.axis_index("core") == 1)
-    def _():
-        put(out_ref, product(parts(matrix_ref), parts(first_ref.at[0])))
-
-    @pl.when(lax.axis_index("core") == 0)
+def is_at(**place):
+    tests = [lax.axis_index(axis) == index for axis, index in place.items()]
+    return functools.reduce(jnp.logical_and, tests)
+
+
+def leading_body(matrix_ref, source_ref, first_ref, green_ref):
+    @pl.when(is_at(chip=0, core=1))
+    def _():
+        put(green_ref, applied(parts(matrix_ref), parts(source_ref), parts(first_ref.at[0])))
+
+
+def pair_body(
+    matrix_ref, source_ref, first_source_ref, first_matrix_ref, out_ref, total_ref, sent_ref
+):
+    @pl.when(is_at(core=1))
+    def _():
+        matrix = parts(matrix_ref)
+        total = applied(matrix, parts(source_ref), parts(first_source_ref.at[0]))
+        put(total_ref, total)
+        put(sent_ref.at[0], total)
+        both = product(matrix, parts(first_matrix_ref.at[0]))
+        put(out_ref, both)
+        put(sent_ref.at[1], both)
+
+    @pl.when(is_at(core=0))
     def _():
         put(out_ref, parts(matrix_ref))
+        put(total_ref, parts(source_ref))
 
 
 def hop_body(matrix_ref, source_ref, incoming_ref, green_ref):
-    put(green_ref, applied(parts(matrix_ref), parts(source_ref), parts(incoming_ref)))
-
-
-def joined_body(source_ref, matrix_ref, near_ref, far_ref, out_ref):
-    @pl.when(lax.axis_index("chip") == 3)
-    def _():
-        put(out_ref, applied(parts(matrix_ref), parts(source_ref), parts(far_ref)))
-
-    @pl.when(lax.axis_index("chip") != 3)
-    def _():
-        out_ref[...] = source_ref[...] + near_ref[...]
+    @pl.when(is_at(chip=1, core=1))
+    def _():
+        put(green_ref, applied(parts(matrix_ref), parts(source_ref), parts(incoming_ref)))
+
+
+def joined_body(arrived_ref, map_ref, far_ref, near_ref, out_ref):
+    @pl.when(is_at(chip=3, core=1))
+    def _():
+        put(out_ref, applied(parts(map_ref.at[1]), parts(map_ref.at[0]), parts(far_ref)))
+
+    @pl.when(jnp.logical_not(is_at(chip=3, core=1)))
+    def _():
+        out_ref[...] = arrived_ref[...] + near_ref[...]
 
 
 def lower(shape):
@@ -267,24 +276,23 @@
 
     matrix, source, sent = prelude(lesser_in[0, 0], retarded[0, 0], coupling[0])
     first_source = lax.all_gather(sent, "core")
-    source, green = call(
-        pair_source_body,
-        [(shape, F32), (shape, BF16)],
+    green = call(leading_body, [(shape, BF16)], matrix, source, first_source, flops=2 * one)
+    arrived = lax.ppermute(green, SPACE, [(1, 3)])
+    first_matrix = lax.all_gather(matrix, "core")
+    matrix, source, sent = call(
+        pair_body,
+        [(shape, BF16), (shape, F32), ((2, *shape), BF16)],
         matrix,
         source,
         first_source,
-        flops=2 * one,
-    )
-    first_matrix = lax.all_gather(matrix, "core")
-    matrix = call(pair_matrix_body, [(shape, BF16)], matrix, first_matrix, flops=one)
-    arrived_source = lax.ppermute(green, SPACE, [(1, 3), (5, 7)])
-    arrived_matrix = lax.ppermute(matrix, SPACE, [(5, 7)])
-    green = call(hop_body, [(shape, BF16)], matrix, source, arrived_source, flops=2 * one)
+        first_matrix,
+        flops=3 * one,
+    )
+    chip_map = lax.ppermute(sent, SPACE, [(5, 7)])
+    green = call(hop_body, [(shape, BF16)], matrix, source, arrived, flops=2 * one)
+    near = lax.ppermute(green, SPACE, [(3, 5)])
     far = lax.ppermute(green, SPACE, [(3, 7)])
-    near = lax.ppermute(green, SPACE, [(3, 5)])
-    incoming = call(
-        joined_body, [(shape, BF16)], arrived_source, arrived_matrix, near, far, flops=2 * one
-    )
+    incoming = call(joined_body, [(shape, BF16)], arrived, chip_map, far, near, flops=2 * one)
     incoming = lax.all_gather(incoming, "core")
     chunks = call(
         last_body,

time: 89.5 us -> 85.7 us (0.958)
  starting transfers between devices: 22 us -> 19.5 us
  Pallas kernels: 6.23 us -> 4.96 us
    all_to_all x1, starting transfers between devices: 19.3 us -> 16.8 us  [exchanged(): lax.all_to_all(chunks, 'energy', split_axis=0, concat_axis=0, axis_index_...]
    pallas_call x6, Pallas kernels: 3.51 us -> 2.24 us  [call(): pl.pallas_call(body, out_shape=outs if len(outs) > 1 else outs[0], compil...]
    all_gather x1, blocking collectives: 3.16 us -> 2.18 us  [local(): first_matrix = lax.all_gather(matrix, 'core')]
    all_gather x1, blocking collectives: 14.7 us -> 15.6 us  [local(): incoming = lax.all_gather(incoming, 'core')]
  transfers between devices with their start and end apart: 5 -> 5, of which waited for: 1 -> 1; matrix products, arithmetic and copies ran while one was open for 1% -> 1% of each run, Pallas kernels for 1% -> 0%
where the time goes in v4:
time: 85.7 us; the launch traced here: 85.3 us
  blocking collectives  46.8 us (55%)
  starting transfers between devices  19.5 us (23%)
  waiting for transfers between devices  11.9 us (14%)
  Pallas kernels  4.96 us (6%)
  local copies, waits for them, and re-layouts  1.34 us (2%)
    all_to_all x1, blocking collectives, exchanged(): lax.all_to_all(chunks, 'energy', split_axis=0, concat_axis=0, axis_index_...  26.8 us
    all_to_all x1, starting transfers between devices, exchanged(): lax.all_to_all(chunks, 'energy', split_axis=0, concat_axis=0, axis_index_...  16.8 us
    all_gather x1, blocking collectives, local(): incoming = lax.all_gather(incoming, 'core')  15.6 us
    all_to_all x1, waiting for transfers between devices, exchanged(): lax.all_to_all(chunks, 'energy', split_axis=0, concat_axis=0, axis_index_...  11.9 us
    pallas_call x6, Pallas kernels, call(): pl.pallas_call(body, out_shape=outs if len(outs) > 1 else outs[0], compil...  2.24 us
    all_gather x1, blocking collectives, local(): first_source = lax.all_gather(sent, 'core')  2.18 us
    all_gather x1, blocking collectives, local(): first_matrix = lax.all_gather(matrix, 'core')  2.18 us
    pallas_call x1, Pallas kernels, prelude(): pl.pallas_call(prelude_body, out_shape=[jax.ShapeDtypeStruct(shape, dtype...  2.01 us
  transfers between devices with their start and end apart: 5, of which 1 were waited for; matrix products, arithmetic and copies ran while one was open for 1% of the time, Pallas kernels for 0%

profile of v4, /device:TPU:6, one launch (start us, length us, event | category | flops | bytes accessed | tf_op | source)
XLA Modules:
  0.0 85.3 jit_solution(8500475291316589185)
XLA Ops:
  0.0 2.0 %shard_map.46 = (bf16[2,256,256]{2,1,0:T(8,128)(2,1)S(1)}, f32[2,256,256]{2,1,0:T(8,128)S(1)}, bf16[2,256,256]{2,1,0:T(8,128)(2,1)S(1)}) custom-call(bf16[2,256,256]{2,1,0:T(8,128)(2,1)} %bitcast.18, bf16[2,256,256]{2,1,0:T(8,128)(2,1)} %bitcast.19, bf16[2,256,256]{2,1,0:T(8,128)(2,1)} %bitcast.20), custom_call_target="tpu_custom_call" | custom-call | flops 402653184 | bytes 1048576 | tf_op jit(solution)/shard_map/pallas_call | solution.py:93
  2.0 2.2 %all-gather = bf16[4,256,256]{2,1,0:T(8,128)(2,1)S(1)} all-gather(bf16[2,256,256]{2,1,0:T(8,128)(2,1)S(1)} %get-tuple-element.13), channel_id=2, replica_groups=mesh['chip'=4,'core'=2,'energy'=64] {'core'}, dimensions={0}, use_global_device_ids=true | all-gather | bytes 786432 | tf_op jit(solution)/shard_map/all_gather | solution.py:278
  4.2 0.7 collective-permute-start
  4.9 2.2 %all-gather.1 = bf16[4,256,256]{2,1,0:T(8,128)(2,1)S(1)} all-gather(bf16[2,256,256]{2,1,0:T(8,128)(2,1)S(1)} %get-tuple-element.11.matrix_ref), channel_id=3, replica_groups=mesh['chip'=4,'core'=2,'energy'=64] {'core'}, dimensions={0}, use_global_device_ids=true | all-gather | bytes 786432 | tf_op jit(solution)/shard_map/all_gather | solution.py:281
  7.1 0.1 shard_map.47
  7.1 0.7 collective-permute-start.1
  7.8 0.0 collective-permute-done.incoming_ref.arrived_ref
  7.9 0.7 collective-permute-start.2
  8.5 0.7 collective-permute-start.3
  9.2 0.0 collective-permute-done.2.far_ref
  9.2 0.0 collective-permute-done.3.near_ref
  9.2 0.0 collective-permute-done.1.map_ref
  9.3 15.6 %all-gather.2 = bf16[4,256,256]{2,1,0:T(8,128)(2,1)S(1)} all-gather(bf16[2,256,256]{2,1,0:T(8,128)(2,1)S(1)} %shard_map.50), channel_id=4, replica_groups=mesh['chip'=4,'core'=2,'energy'=64] {'core'}, dimensions={0}, use_global_device_ids=true | all-gather | bytes 786432 | tf_op jit(solution)/shard_map/all_gather | solution.py:296
  25.0 1.4 %shard_map.51 = bf16[32,2,16,128]{3,2,1,0:T(8,128)(2,1)} custom-call(bf16[2,256,256]{2,1,0:T(8,128)(2,1)S(1)} %get-tuple-element.14.matrix_ref, f32[2,256,256]{2,1,0:T(8,128)S(1)} %get-tuple-element.15.source_ref, bf16[2,2,256,256]{3,2,1,0:T(8,128)(2,1)S(1)} %bitcast.14), custom_call_target="tpu_custom_call" | custom-call | flops 268435456 | bytes 1572864 | tf_op jit(solution)/shard_map/pallas_call | solution.py:63
  26.3 16.8 %all-to-all-start = ((bf16[64,16,128]{2,1,0:T(8,128)(2,1)}), bf16[64,16,128]{2,1,0:T(8,128)(2,1)S(1)}, u32[]{:S(2)}, u32[]{:S(2)}) async-start(bf16[64,16,128]{2,1,0:T(8,128)(2,1)} %bitcast.6), calls=%async_computation | async-start | bytes 524288 | tf_op jit(solution)/shard_map/all_to_all | solution.py:265
  43.1 0.0 copy-start.1
  43.1 0.6 copy-done.1
  43.8 0.0 slice-start
  43.8 0.1 slice.20
  43.9 0.7 slice-done
  44.5 0.1 negate_convert_fusion.1
  44.6 0.0 copy-start
  44.7 0.3 fusion.15
  45.0 0.1 maximum_maximum_fusion.forward_ref
  45.1 11.9 %all-to-all-done.chunks_ref = bf16[64,16,128]{2,1,0:T(8,128)(2,1)S(1)} async-done(((bf16[64,16,128]{2,1,0:T(8,128)(2,1)}), bf16[64,16,128]{2,1,0:T(8,128)(2,1)S(1)}, u32[]{:S(2)}, u32[]{:S(2)}) %all-to-all-start) | async-done | bytes 262176 | tf_op jit(solution)/shard_map/all_to_all | solution.py:265
  57.0 0.0 copy-done
  57.0 0.7 shard_map.52
  57.7 26.8 %all_to_all.10 = bf16[64,16,128]{2,1,0:T(8,128)(2,1)S(1)} all-to-all(bf16[64,16,128]{2,1,0:T(8,128)(2,1)S(1)} %shard_map.52), channel_id=1, replica_groups={{42,43,44,45,46,47,48,49,50,51,52,53,54,55,56,57,58,59,60,61,62,63,0,1,..., dimensions={0} | all-to-all | bytes 524288 | tf_op jit(solution)/shard_map/all_to_all | solution.py:265
  84.5 0.8 shard_map.53
  (7 shorter events, 0.1 us)
Async XLA Ops:
  4.2 3.6 %collective-permute-start = (bf16[2,256,256]{2,1,0:T(8,128)(2,1)S(1)}, bf16[2,256,256]{2,1,0:T(8,128)(2,1)S(1)}, u32[]{:S(2)}, u32[]{:S(2)}) collective-permute-start(bf16[2,256,256]{2,1,0:T(8,128)(2,1)S(1)} %shard_map.48), channel_id=1, source_target_pairs={{64,192},{65,193},{66,194},{67,195},{68,196},{69,197},{70,198},{71... | collective-permute-start | bytes 786440 | tf_op jit(solution)/shard_map/ppermute | solution.py:280
  7.1 2.1 %collective-permute-start.1 = (bf16[2,2,256,256]{3,2,1,0:T(8,128)(2,1)S(1)}, bf16[2,2,256,256]{3,2,1,0:T(8,128)(2,1)S(1)}, u32[]{:S(2)}, u32[]{:S(2)}) collective-permute-start(bf16[2,2,256,256]{3,2,1,0:T(8,128)(2,1)S(1)} %get-tuple-element.16), channel_id=1, source_target_pairs={{320,448},{321,449},{322,450},{323,451},{324,452},{325,453},{326,4... | collective-permute-start | bytes 1572872 | tf_op jit(solution)/shard_map/ppermute | solution.py:291
  7.9 1.4 %collective-permute-start.2 = (bf16[2,256,256]{2,1,0:T(8,128)(2,1)S(1)}, bf16[2,256,256]{2,1,0:T(8,128)(2,1)S(1)}, u32[]{:S(2)}, u32[]{:S(2)}) collective-permute-start(bf16[2,256,256]{2,1,0:T(8,128)(2,1)S(1)} %shard_map.49), channel_id=1, source_target_pairs={{192,448},{193,449},{194,450},{195,451},{196,452},{197,453},{198,4... | collective-permute-start | bytes 786440 | tf_op jit(solution)/shard_map/ppermute | solution.py:294
  8.5 0.7 collective-permute-start.3
  26.3 30.7 %all-to-all-start = ((bf16[64,16,128]{2,1,0:T(8,128)(2,1)}), bf16[64,16,128]{2,1,0:T(8,128)(2,1)S(1)}, u32[]{:S(2)}, u32[]{:S(2)}) async-start(bf16[64,16,128]{2,1,0:T(8,128)(2,1)} %bitcast.6), calls=%async_computation | async-start | bytes 524288 | tf_op jit(solution)/shard_map/all_to_all | solution.py:265
  43.1 0.6 copy-start.1
  43.8 0.7 slice-start
  44.6 12.4 %copy-start = (bf16[1,128,1024]{2,1,0:T(8,128)(2,1)S(1)}, bf16[1,128,1024]{2,1,0:T(8,128)(2,1)}, u32[]{:S(2)}) copy-start(bf16[1,128,1024]{2,1,0:T(8,128)(2,1)} %param.7) | copy-start | bytes 786436

commit v5 on v4

--- a/solution.py
+++ b/solution.py
@@ -3,6 +3,8 @@
 
 import jax
 import jax.numpy as jnp
+import ml_dtypes
+import numpy as np
 from jax import lax
 from jax.experimental import pallas as pl
 from jax.experimental.pallas import tpu as pltpu
@@ -115,8 +117,26 @@
 
 
 def pair_body(
-    matrix_ref, source_ref, first_source_ref, first_matrix_ref, out_ref, total_ref, sent_ref
+    matrix_ref,
+    source_ref,
+    first_source_ref,
+    first_matrix_ref,
+    weights_hbm,
+    forward_hbm,
+    inverse_hbm,
+    out_ref,
+    total_ref,
+    sent_ref,
+    weights_ref,
+    forward_ref,
+    inverse_ref,
+    semaphores,
 ):
+    pairs = ((weights_hbm, weights_ref), (forward_hbm, forward_ref), (inverse_hbm, inverse_ref))
+    copies = [pltpu.make_async_copy(*pair, semaphores.at[i]) for i, pair in enumerate(pairs)]
+    for copy in copies:
+        copy.start()
+
     @pl.when(is_at(core=1))
     def _():
         matrix = parts(matrix_ref)
@@ -132,6 +152,37 @@
         put(out_ref, parts(matrix_ref))
         put(total_ref, parts(source_ref))
 
+    for copy in copies:
+        copy.wait()
+
+
+def pair_map(matrix, source, first_source, first_matrix, *loads):
+    shape = matrix.shape
+    vmem = pl.BlockSpec(memory_space=pltpu.VMEM)
+    hbm = pl.BlockSpec(memory_space=pltpu.HBM)
+    return pl.pallas_call(
+        pair_body,
+        out_shape=[
+            jax.ShapeDtypeStruct(shape, BF16),
+            jax.ShapeDtypeStruct(shape, F32),
+            jax.ShapeDtypeStruct((2, *shape), BF16),
+            *(jax.ShapeDtypeStruct(a.shape, BF16) for a in loads),
+        ],
+        in_specs=[vmem] * 4 + [hbm] * 3,
+        out_specs=[vmem] * 6,
+        scratch_shapes=[pltpu.SemaphoreType.DMA((3,))],
+        compiler_params=pltpu.CompilerParams(vmem_limit_bytes=24 * 2**20),
+        cost_estimate=pl.CostEstimate(
+            flops=24 * shape[-1] ** 3, bytes_accessed=2**20, transcendentals=0
+        ),
+    )(
+        matrix,
+        source,
+        first_source,
+        first_matrix,
+        *(pltpu.with_memory_space_constraint(a, pltpu.HBM) for a in loads),
+    )
+
 
 def hop_body(matrix_ref, source_ref, incoming_ref, green_ref):
     @pl.when(is_at(chip=1, core=1))
@@ -139,14 +190,14 @@
         put(green_ref, applied(parts(matrix_ref), parts(source_ref), parts(incoming_ref)))
 
 
-def joined_body(arrived_ref, map_ref, far_ref, near_ref, out_ref):
+def joined_body(arrived_ref, map_ref, far_ref, out_ref):
     @pl.when(is_at(chip=3, core=1))
     def _():
         put(out_ref, applied(parts(map_ref.at[1]), parts(map_ref.at[0]), parts(far_ref)))
 
     @pl.when(jnp.logical_not(is_at(chip=3, core=1)))
     def _():
-        out_ref[...] = arrived_ref[...] + near_ref[...]
+        out_ref[...] = arrived_ref[...]
 
 
 def lower(shape):
@@ -229,25 +280,25 @@
 
 
 def phase_table(row_count, column_count, length):
-    row_index = jnp.arange(row_count, dtype=jnp.int32)[:, None]
-    column_index = jnp.arange(column_count, dtype=jnp.int32)[None, :]
-    residue = row_index * column_index % length
-    return residue.astype(F32) * (2.0 * math.pi / length)
+    residue = np.arange(row_count)[:, None] * np.arange(column_count)[None, :] % length
+    return residue.astype(np.float32) * np.float32(2.0 * math.pi / length)
 
 
 def complex_table(real, imag):
-    return jnp.block([[real, -imag], [imag, real]]).astype(BF16)
-
-
-def spectra(chunks, weights):
+    return jnp.asarray(np.block([[real, -imag], [imag, real]]).astype(ml_dtypes.bfloat16))
+
+
+def tables(count, length):
+    phase = np.roll(phase_table(length, count, length), -FIRST_OUT, axis=1)
+    forward = complex_table(np.cos(phase), -np.sin(phase))
+    phase = np.roll(phase_table(count, length, length), -FIRST_BACK, axis=0)
+    inverse = complex_table(np.cos(phase), np.sin(phase))
+    return forward, inverse
+
+
+def spectra(chunks, forward, inverse, weights):
     count = chunks.shape[0]
     length = weights.shape[0]
-    phase = phase_table(length, count, length)
-    phase = jnp.roll(phase, -FIRST_OUT, axis=1)
-    forward = complex_table(jnp.cos(phase), -jnp.sin(phase))
-    phase = phase_table(count, length, length)
-    phase = jnp.roll(phase, -FIRST_BACK, axis=0)
-    inverse = complex_table(jnp.cos(phase), jnp.sin(phase))
     return pl.pallas_call(
         spectra_body,
         out_shape=jax.ShapeDtypeStruct(chunks.shape, BF16),
@@ -279,20 +330,19 @@
     green = call(leading_body, [(shape, BF16)], matrix, source, first_source, flops=2 * one)
     arrived = lax.ppermute(green, SPACE, [(1, 3)])
     first_matrix = lax.all_gather(matrix, "core")
-    matrix, source, sent = call(
-        pair_body,
-        [(shape, BF16), (shape, F32), ((2, *shape), BF16)],
+    matrix, source, sent, weights, forward, inverse = pair_map(
         matrix,
         source,
         first_source,
         first_matrix,
-        flops=3 * one,
+        interaction[0],
+        *tables(energies, interaction.shape[1]),
     )
     chip_map = lax.ppermute(sent, SPACE, [(5, 7)])
     green = call(hop_body, [(shape, BF16)], matrix, source, arrived, flops=2 * one)
     near = lax.ppermute(green, SPACE, [(3, 5)])
     far = lax.ppermute(green, SPACE, [(3, 7)])
-    incoming = call(joined_body, [(shape, BF16)], arrived, chip_map, far, near, flops=2 * one)
+    incoming = call(joined_body, [(shape, BF16)], arrived, chip_map, far, flops=2 * one) + near
     incoming = lax.all_gather(incoming, "core")
     chunks = call(
         last_body,
@@ -303,7 +353,7 @@
         flops=2 * one,
     )
     chunks = exchanged(chunks.reshape(chunk), FIRST_OUT)
-    result = spectra(chunks, interaction[0])
+    result = spectra(chunks, forward, inverse, weights)
     returned = exchanged(result, FIRST_BACK)
     out = call(
         output_body,

time: 85.7 us -> 84.8 us (0.989)
  blocking collectives: 46.8 us -> 76.4 us
  starting transfers between devices: 19.5 us -> 2.71 us
  waiting for transfers between devices: 11.9 us -> 0.01 us
  local copies, waits for them, and re-layouts: 1.34 us -> 0 us
    all_to_all x1 -> x2, blocking collectives: 26.8 us -> 57.3 us  [exchanged(): lax.all_to_all(chunks, 'energy', split_axis=0, concat_axis=0, axis_index_...]
    all_to_all x1 -> x0, starting transfers between devices: 16.8 us -> none  [exchanged(): lax.all_to_all(chunks, 'energy', split_axis=0, concat_axis=0, axis_index_...]
    all_to_all x1 -> x0, waiting for transfers between devices: 11.9 us -> none  [exchanged(): lax.all_to_all(chunks, 'energy', split_axis=0, concat_axis=0, axis_index_...]
    pallas_call x0 -> x1, Pallas kernels: none -> 0.98 us  [pair_map(): pl.pallas_call(pair_body, out_shape=[jax.ShapeDtypeStruct(shape, BF16), j...]
    all_gather x1, blocking collectives: 15.6 us -> 14.7 us  [local(): incoming = lax.all_gather(incoming, 'core')]
    pallas_call x6 -> x5, Pallas kernels: 2.24 us -> 1.47 us  [call(): pl.pallas_call(body, out_shape=outs if len(outs) > 1 else outs[0], compil...]
  transfers between devices with their start and end apart: 5 -> 4, of which waited for: 1 -> 0; matrix products, arithmetic and copies ran while one was open for 1% -> 0% of each run, Pallas kernels for 0% -> 1%
where the time goes in v5:
time: 84.8 us; the launch traced here: 84.4 us
  blocking collectives  76.4 us (90%)
  Pallas kernels  5.17 us (6%)
  starting transfers between devices  2.71 us (3%)
    all_to_all x2, blocking collectives, exchanged(): lax.all_to_all(chunks, 'energy', split_axis=0, concat_axis=0, axis_index_...  57.3 us
    all_gather x1, blocking collectives, local(): incoming = lax.all_gather(incoming, 'core')  14.7 us
    all_gather x1, blocking collectives, local(): first_source = lax.all_gather(sent, 'core')  2.18 us
    all_gather x1, blocking collectives, local(): first_matrix = lax.all_gather(matrix, 'core')  2.18 us
    pallas_call x1, Pallas kernels, prelude(): pl.pallas_call(prelude_body, out_shape=[jax.ShapeDtypeStruct(shape, dtype...  2.01 us
  transfers between devices with their start and end apart: 4, of which 0 were waited for; matrix products, arithmetic and copies ran while one was open for 0% of the time, Pallas kernels for 1%

profile of v5, /device:TPU:6, one launch (start us, length us, event | category | flops | bytes accessed | tf_op | source)
XLA Modules:
  0.0 84.4 jit_solution(1078434121335001233)
XLA Ops:
  0.0 2.0 %shard_map.64 = (bf16[2,256,256]{2,1,0:T(8,128)(2,1)S(1)}, f32[2,256,256]{2,1,0:T(8,128)S(1)}, bf16[2,256,256]{2,1,0:T(8,128)(2,1)S(1)}) custom-call(bf16[2,256,256]{2,1,0:T(8,128)(2,1)} %bitcast.17, bf16[2,256,256]{2,1,0:T(8,128)(2,1)} %bitcast.18, bf16[2,256,256]{2,1,0:T(8,128)(2,1)} %bitcast.19), custom_call_target="tpu_custom_call" | custom-call | flops 402653184 | bytes 1048576 | tf_op jit(solution)/shard_map/pallas_call | solution.py:95
  2.0 2.2 %all-gather = bf16[4,256,256]{2,1,0:T(8,128)(2,1)S(1)} all-gather(bf16[2,256,256]{2,1,0:T(8,128)(2,1)S(1)} %get-tuple-element.16), channel_id=2, replica_groups=mesh['chip'=4,'core'=2,'energy'=64] {'core'}, dimensions={0}, use_global_device_ids=true | all-gather | bytes 786432 | tf_op jit(solution)/shard_map/all_gather | solution.py:329
  4.2 0.7 collective-permute-start
  4.9 2.2 %all-gather.1 = bf16[4,256,256]{2,1,0:T(8,128)(2,1)S(1)} all-gather(bf16[2,256,256]{2,1,0:T(8,128)(2,1)S(1)} %get-tuple-element.14.matrix_ref), channel_id=3, replica_groups=mesh['chip'=4,'core'=2,'energy'=64] {'core'}, dimensions={0}, use_global_device_ids=true | all-gather | bytes 786432 | tf_op jit(solution)/shard_map/all_gather | solution.py:332
  7.1 1.0 %shard_map.65 = (bf16[2,256,256]{2,1,0:T(8,128)(2,1)S(1)}, f32[2,256,256]{2,1,0:T(8,128)S(1)}, bf16[2,2,256,256]{3,2,1,0:T(8,128)(2,1)S(1)}, bf16[128,1024]{1,0:...) custom-call(bf16[2,256,256]{2,1,0:T(8,128)(2,1)S(1)} %get-tuple-element.14.matrix_ref, ...), custom_call_target="tpu_custom_call" | custom-call | flops 402653184 | bytes 1048576 | tf_op jit(solution)/shard_map/pallas_call | solution.py:163
  8.0 0.7 collective-permute-start.1
  8.7 0.0 collective-permute-done.incoming_ref.arrived_ref
  8.8 0.7 collective-permute-start.2
  9.5 0.7 collective-permute-start.3
  10.2 0.0 collective-permute-done.2.far_ref
  10.2 0.0 collective-permute-done.1.map_ref
  10.2 0.0 collective-permute-done.3
  10.2 0.1 add.3
  10.3 14.7 %all-gather.2 = bf16[4,256,256]{2,1,0:T(8,128)(2,1)S(1)} all-gather(bf16[2,256,256]{2,1,0:T(8,128)(2,1)S(1)} %add.3), channel_id=4, replica_groups=mesh['chip'=4,'core'=2,'energy'=64] {'core'}, dimensions={0}, use_global_device_ids=true | all-gather | bytes 786432 | tf_op jit(solution)/shard_map/all_gather | solution.py:346
  25.0 0.6 shard_map.69
  25.7 30.5 %all_to_all.10.chunks_ref = bf16[64,16,128]{2,1,0:T(8,128)(2,1)S(1)} all-to-all(bf16[64,16,128]{2,1,0:T(8,128)(2,1)S(1)} %bitcast.15), channel_id=1, replica_groups={{42,43,44,45,46,47,48,49,50,51,52,53,54,55,56,57,58,59,60,61,62,63,0,1,..., dimensions={0} | all-to-all | bytes 524288 | tf_op jit(solution)/shard_map/all_to_all | solution.py:316
  56.2 0.7 shard_map.70
  56.9 26.8 %all_to_all.11 = bf16[64,16,128]{2,1,0:T(8,128)(2,1)S(1)} all-to-all(bf16[64,16,128]{2,1,0:T(8,128)(2,1)S(1)} %shard_map.70), channel_id=1, replica_groups={{42,43,44,45,46,47,48,49,50,51,52,53,54,55,56,57,58,59,60,61,62,63,0,1,..., dimensions={0} | all-to-all | bytes 524288 | tf_op jit(solution)/shard_map/all_to_all | solution.py:316
  83.7 0.8 shard_map.71
  (3 shorter events, 0.1 us)
Async XLA Ops:
  4.2 4.5 %collective-permute-start = (bf16[2,256,256]{2,1,0:T(8,128)(2,1)S(1)}, bf16[2,256,256]{2,1,0:T(8,128)(2,1)S(1)}, u32[]{:S(2)}, u32[]{:S(2)}) collective-permute-start(bf16[2,256,256]{2,1,0:T(8,128)(2,1)S(1)} %shard_map.66), channel_id=1, source_target_pairs={{64,192},{65,193},{66,194},{67,195},{68,196},{69,197},{70,198},{71... | collective-permute-start | bytes 786440 | tf_op jit(solution)/shard_map/ppermute | solution.py:331
  8.0 2.1 %collective-permute-start.1 = (bf16[2,2,256,256]{3,2,1,0:T(8,128)(2,1)S(1)}, bf16[2,2,256,256]{3,2,1,0:T(8,128)(2,1)S(1)}, u32[]{:S(2)}, u32[]{:S(2)}) collective-permute-start(bf16[2,2,256,256]{3,2,1,0:T(8,128)(2,1)S(1)} %get-tuple-element.19), channel_id=1, source_target_pairs={{320,448},{321,449},{322,450},{323,451},{324,452},{325,453},{326,4... | collective-permute-start | bytes 1572872 | tf_op jit(solution)/shard_map/ppermute | solution.py:341
  8.8 1.4 %collective-permute-start.2 = (bf16[2,256,256]{2,1,0:T(8,128)(2,1)S(1)}, bf16[2,256,256]{2,1,0:T(8,128)(2,1)S(1)}, u32[]{:S(2)}, u32[]{:S(2)}) collective-permute-start(bf16[2,256,256]{2,1,0:T(8,128)(2,1)S(1)} %shard_map.67), channel_id=1, source_target_pairs={{192,448},{193,449},{194,450},{195,451},{196,452},{197,453},{198,4... | collective-permute-start | bytes 786440 | tf_op jit(solution)/shard_map/ppermute | solution.py:344
  9.5 0.8 collective-permute-start.3

commit v6 on v5

--- a/solution.py
+++ b/solution.py
@@ -29,14 +29,19 @@
 
 
 def product(left, right):
-    real_part = dot(left[0], right[0]) - dot(left[1], right[1])
-    imag_part = dot(left[0], right[1]) + dot(left[1], right[0])
+    real_part = dot(
+        jnp.concatenate([left[0], -left[1]], axis=1), jnp.concatenate([right[0], right[1]], axis=0)
+    )
+    imag_part = dot(
+        jnp.concatenate([left[0], left[1]], axis=1), jnp.concatenate([right[1], right[0]], axis=0)
+    )
     return (real_part, imag_part)
 
 
 def product_adjoint(left, right):
-    real_part = dot_adjoint(left[0], right[0]) + dot_adjoint(left[1], right[1])
-    imag_part = dot_adjoint(left[1], right[0]) - dot_adjoint(left[0], right[1])
+    right = jnp.concatenate(right, axis=1)
+    real_part = dot_adjoint(jnp.concatenate([left[0], left[1]], axis=1), right)
+    imag_part = dot_adjoint(jnp.concatenate([left[1], -left[0]], axis=1), right)
     return (real_part, imag_part)
 
 
@@ -59,12 +64,13 @@
     return (source[0] + grown[0], source[1] + grown[1])
 
 
-def call(body, outs, *operands, flops=0):
+def call(body, outs, *operands, flops=0, in_place=False):
     outs = [jax.ShapeDtypeStruct(shape, dtype) for shape, dtype in outs]
     size = sum(math.prod(a.shape) * a.dtype.itemsize for a in [*operands, *outs])
     return pl.pallas_call(
         body,
         out_shape=outs if len(outs) > 1 else outs[0],
+        input_output_aliases={len(operands) - 1: 0} if in_place else {},
         compiler_params=pltpu.CompilerParams(vmem_limit_bytes=24 * 2**20),
         cost_estimate=pl.CostEstimate(flops=flops, bytes_accessed=size, transcendentals=0),
     )(*operands)
@@ -117,16 +123,15 @@
 
 
 def pair_body(
-    matrix_ref,
     source_ref,
-    first_source_ref,
-    first_matrix_ref,
+    sources_ref,
+    matrices_ref,
     weights_hbm,
     forward_hbm,
     inverse_hbm,
-    out_ref,
     total_ref,
-    sent_ref,
+    green_ref,
+    map_ref,
     weights_ref,
     forward_ref,
     inverse_ref,
@@ -137,67 +142,64 @@
     for copy in copies:
         copy.start()
 
+    def composed(second_source):
+        second_matrix = parts(matrices_ref.at[1])
+        total = applied(second_matrix, second_source, parts(sources_ref.at[0]))
+        put(total_ref, total)
+        put(green_ref, total)
+        put(map_ref.at[0], total)
+        put(map_ref.at[1], product(second_matrix, parts(matrices_ref.at[0])))
+
     @pl.when(is_at(core=1))
     def _():
-        matrix = parts(matrix_ref)
-        total = applied(matrix, parts(source_ref), parts(first_source_ref.at[0]))
-        put(total_ref, total)
-        put(sent_ref.at[0], total)
-        both = product(matrix, parts(first_matrix_ref.at[0]))
-        put(out_ref, both)
-        put(sent_ref.at[1], both)
+        composed(parts(source_ref))
 
     @pl.when(is_at(core=0))
     def _():
-        put(out_ref, parts(matrix_ref))
-        put(total_ref, parts(source_ref))
+        composed(parts(sources_ref.at[1]))
 
     for copy in copies:
         copy.wait()
 
 
-def pair_map(matrix, source, first_source, first_matrix, *loads):
-    shape = matrix.shape
+def pair_map(source, sources, matrices, *loads):
+    shape = source.shape
     vmem = pl.BlockSpec(memory_space=pltpu.VMEM)
     hbm = pl.BlockSpec(memory_space=pltpu.HBM)
     return pl.pallas_call(
         pair_body,
         out_shape=[
+            jax.ShapeDtypeStruct(shape, F32),
             jax.ShapeDtypeStruct(shape, BF16),
-            jax.ShapeDtypeStruct(shape, F32),
             jax.ShapeDtypeStruct((2, *shape), BF16),
             *(jax.ShapeDtypeStruct(a.shape, BF16) for a in loads),
         ],
-        in_specs=[vmem] * 4 + [hbm] * 3,
+        in_specs=[vmem] * 3 + [hbm] * 3,
         out_specs=[vmem] * 6,
         scratch_shapes=[pltpu.SemaphoreType.DMA((3,))],
         compiler_params=pltpu.CompilerParams(vmem_limit_bytes=24 * 2**20),
         cost_estimate=pl.CostEstimate(
             flops=24 * shape[-1] ** 3, bytes_accessed=2**20, transcendentals=0
         ),
-    )(
-        matrix,
-        source,
-        first_source,
-        first_matrix,
-        *(pltpu.with_memory_space_constraint(a, pltpu.HBM) for a in loads),
-    )
-
-
-def hop_body(matrix_ref, source_ref, incoming_ref, green_ref):
-    @pl.when(is_at(chip=1, core=1))
-    def _():
-        put(green_ref, applied(parts(matrix_ref), parts(source_ref), parts(incoming_ref)))
-
-
-def joined_body(arrived_ref, map_ref, far_ref, out_ref):
+    )(source, sources, matrices, *(pltpu.with_memory_space_constraint(a, pltpu.HBM) for a in loads))
+
+
+def hop_body(map_ref, total_ref, arrived_later_ref, arrived_ref, green_ref):
+    for core, ref in ((1, arrived_ref), (0, arrived_later_ref)):
+
+        @pl.when(is_at(chip=1, core=core))
+        def _():
+            put(green_ref, applied(parts(map_ref.at[1]), parts(total_ref), parts(ref)))
+
+
+def joined_body(arrived_later_ref, arrived_ref, map_ref, far_ref, out_ref):
     @pl.when(is_at(chip=3, core=1))
     def _():
         put(out_ref, applied(parts(map_ref.at[1]), parts(map_ref.at[0]), parts(far_ref)))
 
-    @pl.when(jnp.logical_not(is_at(chip=3, core=1)))
-    def _():
-        out_ref[...] = arrived_ref[...]
+    @pl.when(lax.axis_index("chip") != 3)
+    def _():
+        out_ref[...] = arrived_ref[...] + arrived_later_ref[...]
 
 
 def lower(shape):
@@ -229,17 +231,45 @@
     ]
 
 
-def last_body(matrix_ref, source_ref, incoming_ref, out_ref):
-    green = applied(parts(matrix_ref), parts(source_ref), parts(incoming_ref.at[1]))
+def cut(matrix, source, incoming, out_ref):
+    green = applied(matrix, source, incoming)
     even_real, odd_real = chunked(green[0])
     even_imag, odd_imag = chunked(green[1])
     even = jnp.concatenate([even_real, even_imag], axis=1).astype(BF16)
     odd = jnp.concatenate([odd_real, odd_imag], axis=1).astype(BF16)
-    pairs = out_ref.shape[0]
-    start = FIRST_OUT // 2
-    for target, taken in rolled(pairs, start):
+    for target, taken in rolled(out_ref.shape[0], FIRST_OUT // 2):
         out_ref[target, 0] = even[taken]
         out_ref[target, 1] = odd[taken]
+
+
+def entered(incoming_ref, near_ref):
+    total = incoming_ref[...] + near_ref[...]
+    return (total[0], total[1])
+
+
+def last_body(map_ref, total_ref, incoming_ref, near_ref, out_ref):
+    @pl.when(is_at(core=1))
+    def _():
+        incoming = entered(incoming_ref, near_ref)
+        cut(parts(map_ref.at[1]), parts(total_ref), incoming, out_ref)
+
+
+def last_later_body(
+    matrix_ref, source_ref, map_ref, far_ref, incoming_ref, near_ref, before_ref, out_ref
+):
+    in_last_chip = lax.axis_index("chip") == 3
+    on_first_core = lax.axis_index("core") == 0
+
+    @pl.when(on_first_core & jnp.logical_not(in_last_chip))
+    def _():
+        incoming = entered(incoming_ref, near_ref)
+        cut(parts(matrix_ref), parts(source_ref), incoming, out_ref)
+
+    @pl.when(on_first_core & in_last_chip)
+    def _():
+        map_source, map_matrix = parts(map_ref.at[0]), parts(map_ref.at[1])
+        incoming = rounded(applied(map_matrix, map_source, parts(far_ref)))
+        cut(parts(matrix_ref), parts(source_ref), incoming, out_ref)
 
 
 def spectra_body(chunks_ref, forward_ref, inverse_ref, weights_ref, out_ref, rows_ref):
@@ -268,15 +298,32 @@
     out_ref[...] = rows_ref[...].reshape(out_ref.shape).astype(BF16)
 
 
-def output_body(chunks_ref, out_ref):
+def output_body(chunks_ref, out_hbm, out_ref, semaphores):
     even = chunks_ref[:, 0].astype(F32)
     odd = chunks_ref[:, 1].astype(F32)
+    copies = []
     for part in range(2):
         rows = slice(ROWS * part, ROWS * (part + 1))
         left, right = unchunked(even[:, rows], odd[:, rows])
         value = jnp.concatenate([left, right], axis=1).astype(BF16)
         for taken, target in rolled(value.shape[0], 2 * ROWS // 4 * FIRST_BACK):
             out_ref[part, target] = value[taken]
+        copy = pltpu.make_async_copy(out_ref.at[part], out_hbm.at[part], semaphores.at[part])
+        copy.start()
+        copies.append(copy)
+    for copy in copies:
+        copy.wait()
+
+
+def output(chunks, shape):
+    return pl.pallas_call(
+        output_body,
+        out_shape=jax.ShapeDtypeStruct(shape, BF16),
+        out_specs=pl.BlockSpec(memory_space=pltpu.HBM),
+        scratch_shapes=[pltpu.VMEM(shape, BF16), pltpu.SemaphoreType.DMA((2,))],
+        compiler_params=pltpu.CompilerParams(vmem_limit_bytes=24 * 2**20),
+        cost_estimate=pl.CostEstimate(flops=0, bytes_accessed=2**19, transcendentals=0),
+    )(chunks)
 
 
 def phase_table(row_count, column_count, length):
@@ -310,6 +357,10 @@
     )(chunks, forward, inverse, weights)
 
 
+def after(array, other):
+    return lax.optimization_barrier((array, other))[0]
+
+
 def exchanged(chunks, first):
     count = chunks.shape[0]
     group = [(first + i) % count for i in range(count)]
@@ -326,40 +377,55 @@
     one = 8 * order**3
 
     matrix, source, sent = prelude(lesser_in[0, 0], retarded[0, 0], coupling[0])
-    first_source = lax.all_gather(sent, "core")
-    green = call(leading_body, [(shape, BF16)], matrix, source, first_source, flops=2 * one)
+    sources = lax.all_gather(sent, "core")
+    green = call(leading_body, [(shape, BF16)], matrix, source, sources, flops=60 * one)
     arrived = lax.ppermute(green, SPACE, [(1, 3)])
-    first_matrix = lax.all_gather(matrix, "core")
-    matrix, source, sent, weights, forward, inverse = pair_map(
+    matrices = lax.all_gather(matrix, "core")
+    total, green, chip_map, weights, forward, inverse = pair_map(
+        source,
+        sources,
+        matrices,
+        interaction[0],
+        *tables(energies, interaction.shape[1]),
+    )
+    map_arrived = lax.ppermute(chip_map, SPACE, [(5, 7)])
+    arrived_later = lax.ppermute(after(green, arrived), SPACE, [(0, 2)])
+    green = call(
+        hop_body, [(shape, BF16)], chip_map, total, arrived_later, arrived, flops=60 * one
+    )
+    near = lax.ppermute(green, SPACE, [(3, 5), (2, 4)])
+    far = lax.ppermute(green, SPACE, [(3, 7), (2, 6)])
+    map_later = lax.ppermute(after(map_arrived, green), SPACE, [(7, 6)])
+    incoming = call(
+        joined_body,
+        [(shape, BF16)],
+        arrived_later,
+        arrived,
+        map_arrived,
+        far,
+        flops=60 * one,
+    )
+    cut_shape = (energies // 2, 2, 2 * ROWS, LANES)
+    chunks = call(
+        last_body, [(cut_shape, BF16)], chip_map, total, incoming, near, flops=2 * one
+    )
+    chunks = call(
+        last_later_body,
+        [(cut_shape, BF16)],
         matrix,
         source,
-        first_source,
-        first_matrix,
-        interaction[0],
-        *tables(energies, interaction.shape[1]),
-    )
-    chip_map = lax.ppermute(sent, SPACE, [(5, 7)])
-    green = call(hop_body, [(shape, BF16)], matrix, source, arrived, flops=2 * one)
-    near = lax.ppermute(green, SPACE, [(3, 5)])
-    far = lax.ppermute(green, SPACE, [(3, 7)])
-    incoming = call(joined_body, [(shape, BF16)], arrived, chip_map, far, flops=2 * one) + near
-    incoming = lax.all_gather(incoming, "core")
-    chunks = call(
-        last_body,
-        [((energies // 2, 2, 2 * ROWS, LANES), BF16)],
-        matrix,
-        source,
+        map_later,
+        far,
         incoming,
+        near,
+        chunks,
         flops=2 * one,
+        in_place=True,
     )
     chunks = exchanged(chunks.reshape(chunk), FIRST_OUT)
     result = spectra(chunks, forward, inverse, weights)
     returned = exchanged(result, FIRST_BACK)
-    out = call(
-        output_body,
-        [(shape, BF16)],
-        returned.reshape(energies // 2, 2, 2 * ROWS, LANES),
-    )
+    out = output(returned.reshape(energies // 2, 2, 2 * ROWS, LANES), shape)
     return out.reshape(1, 1, *shape)
 
 

time: 84.8 us -> 80.9 us (0.954)
  blocking collectives: 76.4 us -> 54.6 us
  waiting for transfers between devices: 0.01 us -> 15.3 us
  starting transfers between devices: 2.71 us -> 5.3 us
    ppermute x3 -> x5, waiting for transfers between devices: 0.01 us -> 15.3 us  [the longest x1 15.3 us: local(): far = lax.ppermute(green, SPACE, [(3, 7), (2, 6)])]
    all_gather x3 -> x2, blocking collectives: 19.1 us -> 4.36 us  [the longest x1 2.18 us: local(): sources = lax.all_gather(sent, 'core')]
    all_to_all x2, blocking collectives: 57.3 us -> 50.2 us  [exchanged(): lax.all_to_all(chunks, 'energy', split_axis=0, concat_axis=0, axis_index_...]
    ppermute x3 -> x5, starting transfers between devices: 2.05 us -> 4.63 us  [the longest x1 1.29 us: local(): map_later = lax.ppermute(after(map_arrived, green), SPACE, [(7, 6)])]
    pallas_call x6 -> x7, Pallas kernels: 2.45 us -> 2.78 us  [the longest x5 1.05 us: call(): pl.pallas_call(body, out_shape=outs if len(outs) > 1 else outs[0], input_...]
  transfers between devices with their start and end apart: 4 -> 6, of which waited for: 0 -> 1; matrix products, arithmetic and copies ran while one was open for 0% -> 0% of each run, Pallas kernels for 1% -> 1%
where the time goes in v6:
time: 80.9 us; the launch traced here: 80.7 us
  blocking collectives  54.6 us (67%)
  waiting for transfers between devices  15.3 us (19%)
  Pallas kernels  5.36 us (7%)
  starting transfers between devices  5.3 us (7%)
    all_to_all x2, blocking collectives, exchanged(): lax.all_to_all(chunks, 'energy', split_axis=0, concat_axis=0, axis_index_...  50.2 us
    ppermute x1, waiting for transfers between devices, local(): far = lax.ppermute(green, SPACE, [(3, 7), (2, 6)])  15.3 us
    all_gather x1, blocking collectives, local(): sources = lax.all_gather(sent, 'core')  2.18 us
    all_gather x1, blocking collectives, local(): matrices = lax.all_gather(matrix, 'core')  2.18 us
    pallas_call x1, Pallas kernels, prelude(): pl.pallas_call(prelude_body, out_shape=[jax.ShapeDtypeStruct(shape, dtype...  1.87 us
  transfers between devices with their start and end apart: 6, of which 1 were waited for; matrix products, arithmetic and copies ran while one was open for 0% of the time, Pallas kernels for 1%

profile of v6, /device:TPU:6, one launch (start us, length us, event | category | flops | bytes accessed | tf_op | source)
XLA Modules:
  0.0 80.7 jit_solution(13874435757303172418)
XLA Ops:
  0.0 1.9 %shard_map.64 = (bf16[2,256,256]{2,1,0:T(8,128)(2,1)S(1)}, f32[2,256,256]{2,1,0:T(8,128)S(1)}, bf16[2,256,256]{2,1,0:T(8,128)(2,1)S(1)}) custom-call(bf16[2,256,256]{2,1,0:T(8,128)(2,1)} %bitcast.15, bf16[2,256,256]{2,1,0:T(8,128)(2,1)} %bitcast.16, bf16[2,256,256]{2,1,0:T(8,128)(2,1)} %bitcast.17), custom_call_target="tpu_custom_call" | custom-call | flops 402653184 | bytes 1048576 | tf_op jit(solution)/shard_map/pallas_call | solution.py:101
  1.9 2.2 %all-gather = bf16[4,256,256]{2,1,0:T(8,128)(2,1)S(1)} all-gather(bf16[2,256,256]{2,1,0:T(8,128)(2,1)S(1)} %get-tuple-element.18), channel_id=2, replica_groups=mesh['chip'=4,'core'=2,'energy'=64] {'core'}, dimensions={0}, use_global_device_ids=true | all-gather | bytes 786432 | tf_op jit(solution)/shard_map/all_gather | solution.py:380
  4.1 0.7 collective-permute-start.1
  4.7 2.2 %all-gather.1 = bf16[4,256,256]{2,1,0:T(8,128)(2,1)S(1)} all-gather(bf16[2,256,256]{2,1,0:T(8,128)(2,1)S(1)} %get-tuple-element.16.matrix_ref), channel_id=3, replica_groups=mesh['chip'=4,'core'=2,'energy'=64] {'core'}, dimensions={0}, use_global_device_ids=true | all-gather | bytes 786432 | tf_op jit(solution)/shard_map/all_gather | solution.py:383
  6.9 1.0 %shard_map.65 = (f32[2,256,256]{2,1,0:T(8,128)S(1)}, bf16[2,256,256]{2,1,0:T(8,128)(2,1)S(1)}, bf16[2,2,256,256]{3,2,1,0:T(8,128)(2,1)S(1)}, bf16[128,1024]{1,0:...) custom-call(f32[2,256,256]{2,1,0:T(8,128)S(1)} %get-tuple-element.17.source_ref, ...), custom_call_target="tpu_custom_call" | custom-call | flops 402653184 | bytes 1048576 | tf_op jit(solution)/shard_map/pallas_call | solution.py:169
  7.9 0.0 collective-permute-done.1.arrived_ref
  7.9 0.7 collective-permute-start.2
  8.6 0.7 collective-permute-start
  9.3 0.0 collective-permute-done.2.arrived_later_ref
  9.3 1.3 %collective-permute-start.4 = (bf16[2,256,256]{2,1,0:T(8,128)(2,1)S(1)}, bf16[2,256,256]{2,1,0:T(8,128)(2,1)S(1)}, u32[]{:S(2)}, u32[]{:S(2)}) collective-permute-start(bf16[2,256,256]{2,1,0:T(8,128)(2,1)S(1)} %shard_map.67), channel_id=1, source_target_pairs={{192,448},{128,384},{193,449},{129,385},{194,450},{130,386},{195,4... | collective-permute-start | bytes 786440 | tf_op jit(solution)/shard_map/ppermute | solution.py:397
  10.6 0.7 collective-permute-start.5
  11.3 0.0 collective-permute-done.map_ref
  11.3 1.3 %collective-permute-start.3 = (bf16[2,2,256,256]{3,2,1,0:T(8,128)(2,1)S(1)}, bf16[2,2,256,256]{3,2,1,0:T(8,128)(2,1)S(1)}, u32[]{:S(2)}, u32[]{:S(2)}) collective-permute-start(bf16[2,2,256,256]{3,2,1,0:T(8,128)(2,1)S(1)} %collective-permute-done.map_ref), channel_id=1, source_target_pairs={{448,384},{449,385},{450,386},{451,387},{452,388},{453,389},{454,3... | collective-permute-start | bytes 1572872 | tf_op jit(solution)/shard_map/ppermute | solution.py:398
  12.6 15.3 %collective-permute-done.4.far_ref = bf16[2,256,256]{2,1,0:T(8,128)(2,1)S(1)} collective-permute-done((bf16[2,256,256]{2,1,0:T(8,128)(2,1)S(1)}, bf16[2,256,256]{2,1,0:T(8,128)(2,1)S(1)}, u32[]{:S(2)}, u32[]{:S(2)}) %collective-permute-start.4) | collective-permute-done | bytes 262176 | tf_op jit(solution)/shard_map/ppermute | solution.py:397
  27.9 0.0 collective-permute-done.5.near_ref
  27.9 0.0 collective-permute-done.3.map_ref
  27.9 1.0 %shard_map.70 = bf16[32,2,16,128]{3,2,1,0:T(8,128)(2,1)S(1)} custom-call(bf16[2,256,256]{2,1,0:T(8,128)(2,1)S(1)} %get-tuple-element.16.matrix_ref, f32[2,256,256]{2,1,0:T(8,128)S(1)} %get-tuple-element.17.source_ref, bf16[2,2,256,256]{3,2,1,0:T(8,128)(2,1)S(1)} %collective-permute-done.3.map_ref, ...), custom_call_target="tpu_custom_call", output_to_operand_aliasing={{}: (6, {})} | custom-call | flops 268435456 | bytes 2621440 | tf_op jit(solution)/shard_map/pallas_call | solution.py:70
  29.0 26.9 %all_to_all.10.chunks_ref = bf16[64,16,128]{2,1,0:T(8,128)(2,1)S(1)} all-to-all(bf16[64,16,128]{2,1,0:T(8,128)(2,1)S(1)} %bitcast.9), channel_id=1, replica_groups={{42,43,44,45,46,47,48,49,50,51,52,53,54,55,56,57,58,59,60,61,62,63,0,1,..., dimensions={0} | all-to-all | bytes 524288 | tf_op jit(solution)/shard_map/all_to_all | solution.py:367
  55.9 0.7 shard_map.71
  56.6 23.3 %all_to_all.11 = bf16[64,16,128]{2,1,0:T(8,128)(2,1)S(1)} all-to-all(bf16[64,16,128]{2,1,0:T(8,128)(2,1)S(1)} %shard_map.71), channel_id=1, replica_groups={{42,43,44,45,46,47,48,49,50,51,52,53,54,55,56,57,58,59,60,61,62,63,0,1,..., dimensions={0} | all-to-all | bytes 524288 | tf_op jit(solution)/shard_map/all_to_all | solution.py:367
  79.9 0.7 shard_map.72
  (4 shorter events, 0.0 us)
Async XLA Ops:
  4.1 3.8 %collective-permute-start.1 = (bf16[2,256,256]{2,1,0:T(8,128)(2,1)S(1)}, bf16[2,256,256]{2,1,0:T(8,128)(2,1)S(1)}, u32[]{:S(2)}, u32[]{:S(2)}) collective-permute-start(bf16[2,256,256]{2,1,0:T(8,128)(2,1)S(1)} %shard_map.66), channel_id=1, source_target_pairs={{64,192},{65,193},{66,194},{67,195},{68,196},{69,197},{70,198},{71... | collective-permute-start | bytes 786440 | tf_op jit(solution)/shard_map/ppermute | solution.py:382
  7.9 1.4 %collective-permute-start.2 = (bf16[2,256,256]{2,1,0:T(8,128)(2,1)S(1)}, bf16[2,256,256]{2,1,0:T(8,128)(2,1)S(1)}, u32[]{:S(2)}, u32[]{:S(2)}) collective-permute-start(bf16[2,256,256]{2,1,0:T(8,128)(2,1)S(1)} %get-tuple-element.22), channel_id=1, source_target_pairs={{0,128},{1,129},{2,130},{3,131},{4,132},{5,133},{6,134},{7,135},{8... | collective-permute-start | bytes 786440 | tf_op jit(solution)/shard_map/ppermute | solution.py:392
  8.6 2.7 %collective-permute-start = (bf16[2,2,256,256]{3,2,1,0:T(8,128)(2,1)S(1)}, bf16[2,2,256,256]{3,2,1,0:T(8,128)(2,1)S(1)}, u32[]{:S(2)}, u32[]{:S(2)}) collective-permute-start(bf16[2,2,256,256]{3,2,1,0:T(8,128)(2,1)S(1)} %get-tuple-element.19.map_ref), channel_id=1, source_target_pairs={{320,448},{321,449},{322,450},{323,451},{324,452},{325,453},{326,4... | collective-permute-start | bytes 1572872 | tf_op jit(solution)/shard_map/ppermute | solution.py:391
  9.3 18.6 %collective-permute-start.4 = (bf16[2,256,256]{2,1,0:T(8,128)(2,1)S(1)}, bf16[2,256,256]{2,1,0:T(8,128)(2,1)S(1)}, u32[]{:S(2)}, u32[]{:S(2)}) collective-permute-start(bf16[2,256,256]{2,1,0:T(8,128)(2,1)S(1)} %shard_map.67), channel_id=1, source_target_pairs={{192,448},{128,384},{193,449},{129,385},{194,450},{130,386},{195,4... | collective-permute-start | bytes 786440 | tf_op jit(solution)/shard_map/ppermute | solution.py:397
  10.6 17.3 %collective-permute-start.5 = (bf16[2,256,256]{2,1,0:T(8,128)(2,1)S(1)}, bf16[2,256,256]{2,1,0:T(8,128)(2,1)S(1)}, u32[]{:S(2)}, u32[]{:S(2)}) collective-permute-start(bf16[2,256,256]{2,1,0:T(8,128)(2,1)S(1)} %shard_map.67), channel_id=1, source_target_pairs={{192,320},{128,256},{193,321},{129,257},{194,322},{130,258},{195,3... | collective-permute-start | bytes 786440 | tf_op jit(solution)/shard_map/ppermute | solution.py:396
  11.3 16.6 %collective-permute-start.3 = (bf16[2,2,256,256]{3,2,1,0:T(8,128)(2,1)S(1)}, bf16[2,2,256,256]{3,2,1,0:T(8,128)(2,1)S(1)}, u32[]{:S(2)}, u32[]{:S(2)}) collective-permute-start(bf16[2,2,256,256]{3,2,1,0:T(8,128)(2,1)S(1)} %collective-permute-done.map_ref), channel_id=1, source_target_pairs={{448,384},{449,385},{450,386},{451,387},{452,388},{453,389},{454,3... | collective-permute-start | bytes 1572872 | tf_op jit(solution)/shard_map/ppermute | solution.py:398

commit v7 on v6

--- a/solution.py
+++ b/solution.py
@@ -130,7 +130,6 @@
     forward_hbm,
     inverse_hbm,
     total_ref,
-    green_ref,
     map_ref,
     weights_ref,
     forward_ref,
@@ -146,7 +145,6 @@
         second_matrix = parts(matrices_ref.at[1])
         total = applied(second_matrix, second_source, parts(sources_ref.at[0]))
         put(total_ref, total)
-        put(green_ref, total)
         put(map_ref.at[0], total)
         put(map_ref.at[1], product(second_matrix, parts(matrices_ref.at[0])))
 
@@ -170,12 +168,11 @@
         pair_body,
         out_shape=[
             jax.ShapeDtypeStruct(shape, F32),
-            jax.ShapeDtypeStruct(shape, BF16),
             jax.ShapeDtypeStruct((2, *shape), BF16),
             *(jax.ShapeDtypeStruct(a.shape, BF16) for a in loads),
         ],
         in_specs=[vmem] * 3 + [hbm] * 3,
-        out_specs=[vmem] * 6,
+        out_specs=[vmem] * 5,
         scratch_shapes=[pltpu.SemaphoreType.DMA((3,))],
         compiler_params=pltpu.CompilerParams(vmem_limit_bytes=24 * 2**20),
         cost_estimate=pl.CostEstimate(
@@ -184,22 +181,26 @@
     )(source, sources, matrices, *(pltpu.with_memory_space_constraint(a, pltpu.HBM) for a in loads))
 
 
-def hop_body(map_ref, total_ref, arrived_later_ref, arrived_ref, green_ref):
-    for core, ref in ((1, arrived_ref), (0, arrived_later_ref)):
-
-        @pl.when(is_at(chip=1, core=core))
-        def _():
-            put(green_ref, applied(parts(map_ref.at[1]), parts(total_ref), parts(ref)))
-
-
-def joined_body(arrived_later_ref, arrived_ref, map_ref, far_ref, out_ref):
+def hop_body(map_ref, total_ref, arrived_ref, green_ref):
+    @pl.when(is_at(chip=1, core=1))
+    def _():
+        put(green_ref, applied(parts(map_ref.at[1]), parts(total_ref), parts(arrived_ref)))
+
+
+def hop_later_body(map_ref, total_ref, arrived_ref, green_ref):
+    @pl.when(is_at(chip=1, core=0))
+    def _():
+        put(green_ref, applied(parts(map_ref.at[1]), parts(total_ref), parts(arrived_ref.at[1])))
+
+
+def joined_body(arrived_ref, map_ref, far_ref, out_ref):
     @pl.when(is_at(chip=3, core=1))
     def _():
         put(out_ref, applied(parts(map_ref.at[1]), parts(map_ref.at[0]), parts(far_ref)))
 
     @pl.when(lax.axis_index("chip") != 3)
     def _():
-        out_ref[...] = arrived_ref[...] + arrived_later_ref[...]
+        out_ref[...] = arrived_ref[...]
 
 
 def lower(shape):
@@ -243,8 +244,7 @@
 
 
 def entered(incoming_ref, near_ref):
-    total = incoming_ref[...] + near_ref[...]
-    return (total[0], total[1])
+    return (incoming_ref[0] + near_ref[0], incoming_ref[1] + near_ref[1])
 
 
 def last_body(map_ref, total_ref, incoming_ref, near_ref, out_ref):
@@ -262,7 +262,7 @@
 
     @pl.when(on_first_core & jnp.logical_not(in_last_chip))
     def _():
-        incoming = entered(incoming_ref, near_ref)
+        incoming = entered(incoming_ref.at[1], near_ref)
         cut(parts(matrix_ref), parts(source_ref), incoming, out_ref)
 
     @pl.when(on_first_core & in_last_chip)
@@ -305,9 +305,9 @@
     for part in range(2):
         rows = slice(ROWS * part, ROWS * (part + 1))
         left, right = unchunked(even[:, rows], odd[:, rows])
-        value = jnp.concatenate([left, right], axis=1).astype(BF16)
-        for taken, target in rolled(value.shape[0], 2 * ROWS // 4 * FIRST_BACK):
-            out_ref[part, target] = value[taken]
+        value = jnp.concatenate([left, right], axis=1)
+        rest = value.shape[0] - ROWS // 2 * FIRST_BACK
+        out_ref[part] = jnp.concatenate([value[rest:], value[:rest]], axis=0).astype(BF16)
         copy = pltpu.make_async_copy(out_ref.at[part], out_hbm.at[part], semaphores.at[part])
         copy.start()
         copies.append(copy)
@@ -378,10 +378,10 @@
 
     matrix, source, sent = prelude(lesser_in[0, 0], retarded[0, 0], coupling[0])
     sources = lax.all_gather(sent, "core")
-    green = call(leading_body, [(shape, BF16)], matrix, source, sources, flops=60 * one)
+    green = call(leading_body, [(shape, BF16)], matrix, source, sources, flops=2 * one)
     arrived = lax.ppermute(green, SPACE, [(1, 3)])
     matrices = lax.all_gather(matrix, "core")
-    total, green, chip_map, weights, forward, inverse = pair_map(
+    total, chip_map, weights, forward, inverse = pair_map(
         source,
         sources,
         matrices,
@@ -389,21 +389,25 @@
         *tables(energies, interaction.shape[1]),
     )
     map_arrived = lax.ppermute(chip_map, SPACE, [(5, 7)])
-    arrived_later = lax.ppermute(after(green, arrived), SPACE, [(0, 2)])
     green = call(
-        hop_body, [(shape, BF16)], chip_map, total, arrived_later, arrived, flops=60 * one
-    )
-    near = lax.ppermute(green, SPACE, [(3, 5), (2, 4)])
-    far = lax.ppermute(green, SPACE, [(3, 7), (2, 6)])
-    map_later = lax.ppermute(after(map_arrived, green), SPACE, [(7, 6)])
+        hop_body, [(shape, BF16)], chip_map, total, arrived, flops=2 * one
+    )
+    near = lax.ppermute(green, SPACE, [(3, 5)])
+    far = lax.ppermute(green, SPACE, [(3, 7)])
+    arrived_later = lax.all_gather(after(arrived, green), "core")
+    green = call(
+        hop_later_body,
+        [(shape, BF16)],
+        chip_map,
+        total,
+        arrived_later,
+        flops=2 * one,
+    )
+    near_later = lax.ppermute(green, SPACE, [(2, 4)])
+    far_later = lax.ppermute(green, SPACE, [(2, 6)])
+    map_later = lax.ppermute(map_arrived, SPACE, [(7, 6)])
     incoming = call(
-        joined_body,
-        [(shape, BF16)],
-        arrived_later,
-        arrived,
-        map_arrived,
-        far,
-        flops=60 * one,
+        joined_body, [(shape, BF16)], arrived, map_arrived, far, flops=60 * one
     )
     cut_shape = (energies // 2, 2, 2 * ROWS, LANES)
     chunks = call(
@@ -415,9 +419,9 @@
         matrix,
         source,
         map_later,
-        far,
-        incoming,
-        near,
+        far_later,
+        arrived_later,
+        near_later,
         chunks,
         flops=2 * one,
         in_place=True,

time: 80.9 us -> 80.5 us (level)
  waiting for transfers between devices: 15.3 us -> 11.4 us
  blocking collectives: 54.6 us -> 56.6 us
    ppermute x4 -> x5, waiting for transfers between devices: 15.3 us -> 11.4 us  [the longest x1 11.4 us: local(): far_later = lax.ppermute(green, SPACE, [(2, 6)])]
    all_gather x0 -> x1, blocking collectives: none -> 3.16 us  [local(): arrived_later = lax.all_gather(after(arrived, green), 'core')]
    all_to_all x2, blocking collectives: 50.2 us -> 49.1 us  [exchanged(): lax.all_to_all(chunks, 'energy', split_axis=0, concat_axis=0, axis_index_...]
    ppermute x4 -> x5, starting transfers between devices: 3.94 us -> 4.6 us  [the longest x1 1.29 us: local(): map_later = lax.ppermute(map_arrived, SPACE, [(7, 6)])]
  transfers between devices with their start and end apart: 6 -> 7, of which waited for: 1 -> 1; matrix products, arithmetic and copies ran while one was open for 0% -> 0% of each run, Pallas kernels for 1% -> 1%
where the time goes in v7:
time: 80.5 us; the launch traced here: 79.5 us
  blocking collectives  56.6 us (70%)
  waiting for transfers between devices  11.4 us (14%)
  starting transfers between devices  5.96 us (7%)
  Pallas kernels  5.38 us (7%)
    all_to_all x2, blocking collectives, exchanged(): lax.all_to_all(chunks, 'energy', split_axis=0, concat_axis=0, axis_index_...  49.1 us
    ppermute x1, waiting for transfers between devices, local(): far_later = lax.ppermute(green, SPACE, [(2, 6)])  11.4 us
    all_gather x1, blocking collectives, local(): arrived_later = lax.all_gather(after(arrived, green), 'core')  3.16 us
    all_gather x1, blocking collectives, local(): sources = lax.all_gather(sent, 'core')  2.18 us
    all_gather x1, blocking collectives, local(): matrices = lax.all_gather(matrix, 'core')  2.18 us
    pallas_call x1, Pallas kernels, prelude(): pl.pallas_call(prelude_body, out_shape=[jax.ShapeDtypeStruct(shape, dtype...  1.87 us
  transfers between devices with their start and end apart: 7, of which 1 were waited for; matrix products, arithmetic and copies ran while one was open for 0% of the time, Pallas kernels for 1%

profile of v7, /device:TPU:6, one launch (start us, length us, event | category | flops | bytes accessed | tf_op | source)
XLA Modules:
  0.0 79.5 jit_solution(5197236186029661228)
XLA Ops:
  0.0 1.9 %shard_map.64 = (bf16[2,256,256]{2,1,0:T(8,128)(2,1)S(1)}, f32[2,256,256]{2,1,0:T(8,128)S(1)}, bf16[2,256,256]{2,1,0:T(8,128)(2,1)S(1)}) custom-call(bf16[2,256,256]{2,1,0:T(8,128)(2,1)} %bitcast.18, bf16[2,256,256]{2,1,0:T(8,128)(2,1)} %bitcast.19, bf16[2,256,256]{2,1,0:T(8,128)(2,1)} %bitcast.20), custom_call_target="tpu_custom_call" | custom-call | flops 402653184 | bytes 1048576 | tf_op jit(solution)/shard_map/pallas_call | solution.py:101
  1.9 2.2 %all-gather = bf16[4,256,256]{2,1,0:T(8,128)(2,1)S(1)} all-gather(bf16[2,256,256]{2,1,0:T(8,128)(2,1)S(1)} %get-tuple-element.16), channel_id=2, replica_groups=mesh['chip'=4,'core'=2,'energy'=64] {'core'}, dimensions={0}, use_global_device_ids=true | all-gather | bytes 786432 | tf_op jit(solution)/shard_map/all_gather | solution.py:380
  4.1 0.7 collective-permute-start.2
  4.7 2.2 %all-gather.1 = bf16[4,256,256]{2,1,0:T(8,128)(2,1)S(1)} all-gather(bf16[2,256,256]{2,1,0:T(8,128)(2,1)S(1)} %get-tuple-element.14.matrix_ref), channel_id=3, replica_groups=mesh['chip'=4,'core'=2,'energy'=64] {'core'}, dimensions={0}, use_global_device_ids=true | all-gather | bytes 786432 | tf_op jit(solution)/shard_map/all_gather | solution.py:383
  6.9 1.0 %shard_map.65 = (f32[2,256,256]{2,1,0:T(8,128)S(1)}, bf16[2,2,256,256]{3,2,1,0:T(8,128)(2,1)S(1)}, bf16[128,1024]{1,0:T(8,128)(2,1)S(1)}, bf16[256,128]{1,0:T(8,128)(2,1)S(1)}, bf16[128,256]{1,0:T(8,128)(2,1)S(1)}) custom-call(f32[2,256,256]{2,1,0:T(8,128)S(1)} %get-tuple-element.15.source_ref, bf16[2,2,256,256]{3,2,1,0:T(8,128)(2,1)S(1)} %bitcast.13, ...), custom_call_target="tpu_custom_call" | custom-call | flops 402653184 | bytes 1048576 | tf_op jit(solution)/shard_map/pallas_call | solution.py:167
  7.9 0.7 collective-permute-start
  8.6 0.0 collective-permute-done.2.arrived_ref
  8.6 0.7 collective-permute-start.5
  9.3 0.7 collective-permute-start.6
  10.0 3.2 %all-gather.2 = bf16[4,256,256]{2,1,0:T(8,128)(2,1)S(1)} all-gather(bf16[2,256,256]{2,1,0:T(8,128)(2,1)S(1)} %collective-permute-done.2.arrived_ref), channel_id=4, replica_groups=mesh['chip'=4,'core'=2,'energy'=64] {'core'}, dimensions={0}, use_global_device_ids=true | all-gather | bytes 786432 | tf_op jit(solution)/shard_map/all_gather | solution.py:397
  13.2 1.3 %collective-permute-start.3 = (bf16[2,256,256]{2,1,0:T(8,128)(2,1)S(1)}, bf16[2,256,256]{2,1,0:T(8,128)(2,1)S(1)}, u32[]{:S(2)}, u32[]{:S(2)}) collective-permute-start(bf16[2,256,256]{2,1,0:T(8,128)(2,1)S(1)} %shard_map.68), channel_id=1, source_target_pairs={{128,384},{129,385},{130,386},{131,387},{132,388},{133,389},{134,3... | collective-permute-start | bytes 786440 | tf_op jit(solution)/shard_map/ppermute | solution.py:407
  14.5 0.7 collective-permute-start.4
  15.1 0.0 collective-permute-done.map_ref
  15.2 1.3 %collective-permute-start.1 = (bf16[2,2,256,256]{3,2,1,0:T(8,128)(2,1)S(1)}, bf16[2,2,256,256]{3,2,1,0:T(8,128)(2,1)S(1)}, u32[]{:S(2)}, u32[]{:S(2)}) collective-permute-start(bf16[2,2,256,256]{3,2,1,0:T(8,128)(2,1)S(1)} %collective-permute-done.map_ref), channel_id=1, source_target_pairs={{448,384},{449,385},{450,386},{451,387},{452,388},{453,389},{454,3... | collective-permute-start | bytes 1572872 | tf_op jit(solution)/shard_map/ppermute | solution.py:408
  16.5 0.0 collective-permute-done.5.far_ref
  16.5 0.0 collective-permute-done.6.near_ref
  16.5 11.4 %collective-permute-done.3.far_ref = bf16[2,256,256]{2,1,0:T(8,128)(2,1)S(1)} collective-permute-done((bf16[2,256,256]{2,1,0:T(8,128)(2,1)S(1)}, bf16[2,256,256]{2,1,0:T(8,128)(2,1)S(1)}, u32[]{:S(2)}, u32[]{:S(2)}) %collective-permute-start.3) | collective-permute-done | bytes 262176 | tf_op jit(solution)/shard_map/ppermute | solution.py:407
  27.9 0.0 collective-permute-done.4.near_ref
  27.9 0.0 collective-permute-done.1.map_ref
  27.9 1.0 %shard_map.71 = bf16[32,2,16,128]{3,2,1,0:T(8,128)(2,1)S(1)} custom-call(bf16[2,256,256]{2,1,0:T(8,128)(2,1)S(1)} %get-tuple-element.14.matrix_ref, f32[2,256,256]{2,1,0:T(8,128)S(1)} %get-tuple-element.15.source_ref, bf16[2,2,256,256]{3,2,1,0:T(8,128)(2,1)S(1)} %collective-permute-done.1.map_ref, ...), custom_call_target="tpu_custom_call", output_to_operand_aliasing={{}: (6, {})} | custom-call | flops 268435456 | bytes 2883584 | tf_op jit(solution)/shard_map/pallas_call | solution.py:70
  28.9 26.1 %all_to_all.10.chunks_ref = bf16[64,16,128]{2,1,0:T(8,128)(2,1)S(1)} all-to-all(bf16[64,16,128]{2,1,0:T(8,128)(2,1)S(1)} %bitcast.14), channel_id=1, replica_groups={{42,43,44,45,46,47,48,49,50,51,52,53,54,55,56,57,58,59,60,61,62,63,0,1,..., dimensions={0} | all-to-all | bytes 524288 | tf_op jit(solution)/shard_map/all_to_all | solution.py:367
  55.0 0.7 shard_map.72
  55.7 23.0 %all_to_all.11 = bf16[64,16,128]{2,1,0:T(8,128)(2,1)S(1)} all-to-all(bf16[64,16,128]{2,1,0:T(8,128)(2,1)S(1)} %shard_map.72), channel_id=1, replica_groups={{42,43,44,45,46,47,48,49,50,51,52,53,54,55,56,57,58,59,60,61,62,63,0,1,..., dimensions={0} | all-to-all | bytes 524288 | tf_op jit(solution)/shard_map/all_to_all | solution.py:367
  78.7 0.7 shard_map.73
  (5 shorter events, 0.1 us)
Async XLA Ops:
  4.1 4.5 %collective-permute-start.2 = (bf16[2,256,256]{2,1,0:T(8,128)(2,1)S(1)}, bf16[2,256,256]{2,1,0:T(8,128)(2,1)S(1)}, u32[]{:S(2)}, u32[]{:S(2)}) collective-permute-start(bf16[2,256,256]{2,1,0:T(8,128)(2,1)S(1)} %shard_map.66), channel_id=1, source_target_pairs={{64,192},{65,193},{66,194},{67,195},{68,196},{69,197},{70,198},{71... | collective-permute-start | bytes 786440 | tf_op jit(solution)/shard_map/ppermute | solution.py:382
  7.9 7.2 %collective-permute-start = (bf16[2,2,256,256]{3,2,1,0:T(8,128)(2,1)S(1)}, bf16[2,2,256,256]{3,2,1,0:T(8,128)(2,1)S(1)}, u32[]{:S(2)}, u32[]{:S(2)}) collective-permute-start(bf16[2,2,256,256]{3,2,1,0:T(8,128)(2,1)S(1)} %get-tuple-element.17.map_ref), channel_id=1, source_target_pairs={{320,448},{321,449},{322,450},{323,451},{324,452},{325,453},{326,4... | collective-permute-start | bytes 1572872 | tf_op jit(solution)/shard_map/ppermute | solution.py:391
  8.6 7.8 %collective-permute-start.5 = (bf16[2,256,256]{2,1,0:T(8,128)(2,1)S(1)}, bf16[2,256,256]{2,1,0:T(8,128)(2,1)S(1)}, u32[]{:S(2)}, u32[]{:S(2)}) collective-permute-start(bf16[2,256,256]{2,1,0:T(8,128)(2,1)S(1)} %shard_map.67), channel_id=1, source_target_pairs={{192,448},{193,449},{194,450},{195,451},{196,452},{197,453},{198,4... | collective-permute-start | bytes 786440 | tf_op jit(solution)/shard_map/ppermute | solution.py:396
  9.3 7.2 %collective-permute-start.6 = (bf16[2,256,256]{2,1,0:T(8,128)(2,1)S(1)}, bf16[2,256,256]{2,1,0:T(8,128)(2,1)S(1)}, u32[]{:S(2)}, u32[]{:S(2)}) collective-permute-start(bf16[2,256,256]{2,1,0:T(8,128)(2,1)S(1)} %shard_map.67), channel_id=1, source_target_pairs={{192,320},{193,321},{194,322},{195,323},{196,324},{197,325},{198,3... | collective-permute-start | bytes 786440 | tf_op jit(solution)/shard_map/ppermute | solution.py:395
  13.2 14.7 %collective-permute-start.3 = (bf16[2,256,256]{2,1,0:T(8,128)(2,1)S(1)}, bf16[2,256,256]{2,1,0:T(8,128)(2,1)S(1)}, u32[]{:S(2)}, u32[]{:S(2)}) collective-permute-start(bf16[2,256,256]{2,1,0:T(8,128)(2,1)S(1)} %shard_map.68), channel_id=1, source_target_pairs={{128,384},{129,385},{130,386},{131,387},{132,388},{133,389},{134,3... | collective-permute-start | bytes 786440 | tf_op jit(solution)/shard_map/ppermute | solution.py:407
  14.5 13.4 %collective-permute-start.4 = (bf16[2,256,256]{2,1,0:T(8,128)(2,1)S(1)}, bf16[2,256,256]{2,1,0:T(8,128)(2,1)S(1)}, u32[]{:S(2)}, u32[]{:S(2)}) collective-permute-start(bf16[2,256,256]{2,1,0:T(8,128)(2,1)S(1)} %shard_map.68), channel_id=1, source_target_pairs={{128,256},{129,257},{130,258},{131,259},{132,260},{133,261},{134,2... | collective-permute-start | bytes 786440 | tf_op jit(solution)/shard_map/ppermute | solution.py:406
  15.2 12.8 %collective-permute-start.1 = (bf16[2,2,256,256]{3,2,1,0:T(8,128)(2,1)S(1)}, bf16[2,2,256,256]{3,2,1,0:T(8,128)(2,1)S(1)}, u32[]{:S(2)}, u32[]{:S(2)}) collective-permute-start(bf16[2,2,256,256]{3,2,1,0:T(8,128)(2,1)S(1)} %collective-permute-done.map_ref), channel_id=1, source_target_pairs={{448,384},{449,385},{450,386},{451,387},{452,388},{453,389},{454,3... | collective-permute-start | bytes 1572872 | tf_op jit(solution)/shard_map/ppermute | solution.py:408

commit v8 on v7

--- a/solution.py
+++ b/solution.py
@@ -16,8 +16,8 @@
 F32 = jnp.float32
 LANES = 128
 ROWS = 8
-FIRST_OUT = 42
-FIRST_BACK = 42
+FIRST_OUT = 46
+FIRST_BACK = 34
 
 
 def dot(left, right):

time: 80.5 us -> 79.8 us (level)
  no operation moved by 1% of the time
where the time goes in v8:
time: 79.8 us; the launch traced here: 79.5 us
  blocking collectives  56.6 us (71%)
  waiting for transfers between devices  11.4 us (14%)
  starting transfers between devices  5.96 us (7%)
  Pallas kernels  5.38 us (7%)
    all_to_all x2, blocking collectives, exchanged(): lax.all_to_all(chunks, 'energy', split_axis=0, concat_axis=0, axis_index_...  49.1 us
    ppermute x1, waiting for transfers between devices, local(): far_later = lax.ppermute(green, SPACE, [(2, 6)])  11.4 us
    all_gather x1, blocking collectives, local(): arrived_later = lax.all_gather(after(arrived, green), 'core')  3.16 us
    all_gather x1, blocking collectives, local(): sources = lax.all_gather(sent, 'core')  2.18 us
    all_gather x1, blocking collectives, local(): matrices = lax.all_gather(matrix, 'core')  2.18 us
    pallas_call x1, Pallas kernels, prelude(): pl.pallas_call(prelude_body, out_shape=[jax.ShapeDtypeStruct(shape, dtype...  1.87 us
  transfers between devices with their start and end apart: 7, of which 1 were waited for; matrix products, arithmetic and copies ran while one was open for 0% of the time, Pallas kernels for 1%

profile of v8, /device:TPU:6, one launch (start us, length us, event | category | flops | bytes accessed | tf_op | source)
XLA Modules:
  0.0 79.5 jit_solution(4184360630212223754)
XLA Ops:
  0.0 1.9 %shard_map.64 = (bf16[2,256,256]{2,1,0:T(8,128)(2,1)S(1)}, f32[2,256,256]{2,1,0:T(8,128)S(1)}, bf16[2,256,256]{2,1,0:T(8,128)(2,1)S(1)}) custom-call(bf16[2,256,256]{2,1,0:T(8,128)(2,1)} %bitcast.18, bf16[2,256,256]{2,1,0:T(8,128)(2,1)} %bitcast.19, bf16[2,256,256]{2,1,0:T(8,128)(2,1)} %bitcast.20), custom_call_target="tpu_custom_call" | custom-call | flops 402653184 | bytes 1048576 | tf_op jit(solution)/shard_map/pallas_call | solution.py:101
  1.9 2.2 %all-gather = bf16[4,256,256]{2,1,0:T(8,128)(2,1)S(1)} all-gather(bf16[2,256,256]{2,1,0:T(8,128)(2,1)S(1)} %get-tuple-element.16), channel_id=2, replica_groups=mesh['chip'=4,'core'=2,'energy'=64] {'core'}, dimensions={0}, use_global_device_ids=true | all-gather | bytes 786432 | tf_op jit(solution)/shard_map/all_gather | solution.py:380
  4.1 0.7 collective-permute-start.2
  4.7 2.2 %all-gather.1 = bf16[4,256,256]{2,1,0:T(8,128)(2,1)S(1)} all-gather(bf16[2,256,256]{2,1,0:T(8,128)(2,1)S(1)} %get-tuple-element.14.matrix_ref), channel_id=3, replica_groups=mesh['chip'=4,'core'=2,'energy'=64] {'core'}, dimensions={0}, use_global_device_ids=true | all-gather | bytes 786432 | tf_op jit(solution)/shard_map/all_gather | solution.py:383
  6.9 1.0 %shard_map.65 = (f32[2,256,256]{2,1,0:T(8,128)S(1)}, bf16[2,2,256,256]{3,2,1,0:T(8,128)(2,1)S(1)}, bf16[128,1024]{1,0:T(8,128)(2,1)S(1)}, bf16[256,128]{1,0:T(8,128)(2,1)S(1)}, bf16[128,256]{1,0:T(8,128)(2,1)S(1)}) custom-call(f32[2,256,256]{2,1,0:T(8,128)S(1)} %get-tuple-element.15.source_ref, bf16[2,2,256,256]{3,2,1,0:T(8,128)(2,1)S(1)} %bitcast.13, ...), custom_call_target="tpu_custom_call" | custom-call | flops 402653184 | bytes 1048576 | tf_op jit(solution)/shard_map/pallas_call | solution.py:167
  7.9 0.7 collective-permute-start
  8.6 0.0 collective-permute-done.2.arrived_ref
  8.6 0.7 collective-permute-start.5
  9.3 0.7 collective-permute-start.6
  10.0 3.2 %all-gather.2 = bf16[4,256,256]{2,1,0:T(8,128)(2,1)S(1)} all-gather(bf16[2,256,256]{2,1,0:T(8,128)(2,1)S(1)} %collective-permute-done.2.arrived_ref), channel_id=4, replica_groups=mesh['chip'=4,'core'=2,'energy'=64] {'core'}, dimensions={0}, use_global_device_ids=true | all-gather | bytes 786432 | tf_op jit(solution)/shard_map/all_gather | solution.py:397
  13.2 1.3 %collective-permute-start.3 = (bf16[2,256,256]{2,1,0:T(8,128)(2,1)S(1)}, bf16[2,256,256]{2,1,0:T(8,128)(2,1)S(1)}, u32[]{:S(2)}, u32[]{:S(2)}) collective-permute-start(bf16[2,256,256]{2,1,0:T(8,128)(2,1)S(1)} %shard_map.68), channel_id=1, source_target_pairs={{128,384},{129,385},{130,386},{131,387},{132,388},{133,389},{134,3... | collective-permute-start | bytes 786440 | tf_op jit(solution)/shard_map/ppermute | solution.py:407
  14.5 0.7 collective-permute-start.4
  15.1 0.0 collective-permute-done.map_ref
  15.2 1.3 %collective-permute-start.1 = (bf16[2,2,256,256]{3,2,1,0:T(8,128)(2,1)S(1)}, bf16[2,2,256,256]{3,2,1,0:T(8,128)(2,1)S(1)}, u32[]{:S(2)}, u32[]{:S(2)}) collective-permute-start(bf16[2,2,256,256]{3,2,1,0:T(8,128)(2,1)S(1)} %collective-permute-done.map_ref), channel_id=1, source_target_pairs={{448,384},{449,385},{450,386},{451,387},{452,388},{453,389},{454,3... | collective-permute-start | bytes 1572872 | tf_op jit(solution)/shard_map/ppermute | solution.py:408
  16.5 0.0 collective-permute-done.5.far_ref
  16.5 0.0 collective-permute-done.6.near_ref
  16.5 11.4 %collective-permute-done.3.far_ref = bf16[2,256,256]{2,1,0:T(8,128)(2,1)S(1)} collective-permute-done((bf16[2,256,256]{2,1,0:T(8,128)(2,1)S(1)}, bf16[2,256,256]{2,1,0:T(8,128)(2,1)S(1)}, u32[]{:S(2)}, u32[]{:S(2)}) %collective-permute-start.3) | collective-permute-done | bytes 262176 | tf_op jit(solution)/shard_map/ppermute | solution.py:407
  27.9 0.0 collective-permute-done.4.near_ref
  27.9 0.0 collective-permute-done.1.map_ref
  27.9 1.0 %shard_map.71 = bf16[32,2,16,128]{3,2,1,0:T(8,128)(2,1)S(1)} custom-call(bf16[2,256,256]{2,1,0:T(8,128)(2,1)S(1)} %get-tuple-element.14.matrix_ref, f32[2,256,256]{2,1,0:T(8,128)S(1)} %get-tuple-element.15.source_ref, bf16[2,2,256,256]{3,2,1,0:T(8,128)(2,1)S(1)} %collective-permute-done.1.map_ref, ...), custom_call_target="tpu_custom_call", output_to_operand_aliasing={{}: (6, {})} | custom-call | flops 268435456 | bytes 2883584 | tf_op jit(solution)/shard_map/pallas_call | solution.py:70
  28.9 25.9 %all_to_all.10.chunks_ref = bf16[64,16,128]{2,1,0:T(8,128)(2,1)S(1)} all-to-all(bf16[64,16,128]{2,1,0:T(8,128)(2,1)S(1)} %bitcast.14), channel_id=1, replica_groups={{46,47,48,49,50,51,52,53,54,55,56,57,58,59,60,61,62,63,0,1,2,3,4,5,6,7,..., dimensions={0} | all-to-all | bytes 524288 | tf_op jit(solution)/shard_map/all_to_all | solution.py:367
  54.8 0.7 shard_map.72
  55.5 23.2 %all_to_all.11 = bf16[64,16,128]{2,1,0:T(8,128)(2,1)S(1)} all-to-all(bf16[64,16,128]{2,1,0:T(8,128)(2,1)S(1)} %shard_map.72), channel_id=1, replica_groups={{34,35,36,37,38,39,40,41,42,43,44,45,46,47,48,49,50,51,52,53,54,55,56,5..., dimensions={0} | all-to-all | bytes 524288 | tf_op jit(solution)/shard_map/all_to_all | solution.py:367
  78.8 0.7 shard_map.73
  (5 shorter events, 0.1 us)
Async XLA Ops:
  4.1 4.5 %collective-permute-start.2 = (bf16[2,256,256]{2,1,0:T(8,128)(2,1)S(1)}, bf16[2,256,256]{2,1,0:T(8,128)(2,1)S(1)}, u32[]{:S(2)}, u32[]{:S(2)}) collective-permute-start(bf16[2,256,256]{2,1,0:T(8,128)(2,1)S(1)} %shard_map.66), channel_id=1, source_target_pairs={{64,192},{65,193},{66,194},{67,195},{68,196},{69,197},{70,198},{71... | collective-permute-start | bytes 786440 | tf_op jit(solution)/shard_map/ppermute | solution.py:382
  7.9 7.2 %collective-permute-start = (bf16[2,2,256,256]{3,2,1,0:T(8,128)(2,1)S(1)}, bf16[2,2,256,256]{3,2,1,0:T(8,128)(2,1)S(1)}, u32[]{:S(2)}, u32[]{:S(2)}) collective-permute-start(bf16[2,2,256,256]{3,2,1,0:T(8,128)(2,1)S(1)} %get-tuple-element.17.map_ref), channel_id=1, source_target_pairs={{320,448},{321,449},{322,450},{323,451},{324,452},{325,453},{326,4... | collective-permute-start | bytes 1572872 | tf_op jit(solution)/shard_map/ppermute | solution.py:391
  8.6 7.8 %collective-permute-start.5 = (bf16[2,256,256]{2,1,0:T(8,128)(2,1)S(1)}, bf16[2,256,256]{2,1,0:T(8,128)(2,1)S(1)}, u32[]{:S(2)}, u32[]{:S(2)}) collective-permute-start(bf16[2,256,256]{2,1,0:T(8,128)(2,1)S(1)} %shard_map.67), channel_id=1, source_target_pairs={{192,448},{193,449},{194,450},{195,451},{196,452},{197,453},{198,4... | collective-permute-start | bytes 786440 | tf_op jit(solution)/shard_map/ppermute | solution.py:396
  9.3 7.2 %collective-permute-start.6 = (bf16[2,256,256]{2,1,0:T(8,128)(2,1)S(1)}, bf16[2,256,256]{2,1,0:T(8,128)(2,1)S(1)}, u32[]{:S(2)}, u32[]{:S(2)}) collective-permute-start(bf16[2,256,256]{2,1,0:T(8,128)(2,1)S(1)} %shard_map.67), channel_id=1, source_target_pairs={{192,320},{193,321},{194,322},{195,323},{196,324},{197,325},{198,3... | collective-permute-start | bytes 786440 | tf_op jit(solution)/shard_map/ppermute | solution.py:395
  13.2 14.7 %collective-permute-start.3 = (bf16[2,256,256]{2,1,0:T(8,128)(2,1)S(1)}, bf16[2,256,256]{2,1,0:T(8,128)(2,1)S(1)}, u32[]{:S(2)}, u32[]{:S(2)}) collective-permute-start(bf16[2,256,256]{2,1,0:T(8,128)(2,1)S(1)} %shard_map.68), channel_id=1, source_target_pairs={{128,384},{129,385},{130,386},{131,387},{132,388},{133,389},{134,3... | collective-permute-start | bytes 786440 | tf_op jit(solution)/shard_map/ppermute | solution.py:407
  14.5 13.4 %collective-permute-start.4 = (bf16[2,256,256]{2,1,0:T(8,128)(2,1)S(1)}, bf16[2,256,256]{2,1,0:T(8,128)(2,1)S(1)}, u32[]{:S(2)}, u32[]{:S(2)}) collective-permute-start(bf16[2,256,256]{2,1,0:T(8,128)(2,1)S(1)} %shard_map.68), channel_id=1, source_target_pairs={{128,256},{129,257},{130,258},{131,259},{132,260},{133,261},{134,2... | collective-permute-start | bytes 786440 | tf_op jit(solution)/shard_map/ppermute | solution.py:406
  15.2 12.8 %collective-permute-start.1 = (bf16[2,2,256,256]{3,2,1,0:T(8,128)(2,1)S(1)}, bf16[2,2,256,256]{3,2,1,0:T(8,128)(2,1)S(1)}, u32[]{:S(2)}, u32[]{:S(2)}) collective-permute-start(bf16[2,2,256,256]{3,2,1,0:T(8,128)(2,1)S(1)} %collective-permute-done.map_ref), channel_id=1, source_target_pairs={{448,384},{449,385},{450,386},{451,387},{452,388},{453,389},{454,3... | collective-permute-start | bytes 1572872 | tf_op jit(solution)/shard_map/ppermute | solution.py:408

commit v9 on v8

--- a/solution.py
+++ b/solution.py
@@ -277,24 +277,26 @@
     length = weights_ref.shape[0]
     stride = 2 * ROWS
     rows_ref[...] = chunks_ref[...].astype(F32).reshape(rows_ref.shape)
-    taken = [rows_ref[pl.ds(i, count, stride=stride), :].astype(BF16) for i in range(stride)]
-    values = jnp.concatenate(
-        [jnp.concatenate(taken[:ROWS], axis=1), jnp.concatenate(taken[ROWS:], axis=1)], axis=0
-    )
-    spectrum = dot(forward_ref[...], values) * (count**-0.5)
-    order = [2 * (i % 4) + i // 4 for i in range(ROWS)]
-    weights = jnp.concatenate(
-        [weights_ref[:, LANES * i : LANES * (i + 1)] for i in order], axis=1
-    ).astype(F32)
-    real, imag = spectrum[:length], spectrum[length:]
-    squared_real = ((real * real - imag * imag) * weights).astype(BF16)
-    squared_imag = (2.0 * real * imag * weights).astype(BF16)
-    result = dot(inverse_ref[...], jnp.concatenate([squared_real, squared_imag], axis=0))
-    result = result * (length**-0.5)
-    for i in range(ROWS):
-        columns = slice(LANES * i, LANES * (i + 1))
-        rows_ref[pl.ds(i, count, stride=stride), :] = result[:count, columns]
-        rows_ref[pl.ds(i + ROWS, count, stride=stride), :] = result[count:, columns]
+    for blocks in ((i, i + 1) for i in range(0, ROWS, 2)):
+
+        def taken(offset):
+            rows = [rows_ref[pl.ds(i + offset, count, stride=stride), :] for i in blocks]
+            return jnp.concatenate([row.astype(BF16) for row in rows], axis=1)
+
+        values = jnp.concatenate([taken(0), taken(ROWS)], axis=0)
+        spectrum = dot(forward_ref[...], values) * (count**-0.5)
+        places = [LANES * (2 * (i % 4) + i // 4) for i in blocks]
+        weights = [weights_ref[:, at : at + LANES] for at in places]
+        weights = jnp.concatenate(weights, axis=1).astype(F32)
+        real, imag = spectrum[:length], spectrum[length:]
+        squared_real = ((real * real - imag * imag) * weights).astype(BF16)
+        squared_imag = (2.0 * real * imag * weights).astype(BF16)
+        result = dot(inverse_ref[...], jnp.concatenate([squared_real, squared_imag], axis=0))
+        result = result * (length**-0.5)
+        for at, i in enumerate(blocks):
+            columns = slice(LANES * at, LANES * (at + 1))
+            rows_ref[pl.ds(i, count, stride=stride), :] = result[:count, columns]
+            rows_ref[pl.ds(i + ROWS, count, stride=stride), :] = result[count:, columns]
     out_ref[...] = rows_ref[...].reshape(out_ref.shape).astype(BF16)
 
 

time: 79.8 us -> 80.3 us (level)
  no operation moved by 1% of the time
where the time goes in v9:
time: 80.3 us; the launch traced here: 80 us
  blocking collectives  56.6 us (70%)
  waiting for transfers between devices  11.4 us (14%)
  starting transfers between devices  5.96 us (7%)
  Pallas kernels  5.86 us (7%)
    all_to_all x2, blocking collectives, exchanged(): lax.all_to_all(chunks, 'energy', split_axis=0, concat_axis=0, axis_index_...  49.1 us
    ppermute x1, waiting for transfers between devices, local(): far_later = lax.ppermute(green, SPACE, [(2, 6)])  11.4 us
    all_gather x1, blocking collectives, local(): arrived_later = lax.all_gather(after(arrived, green), 'core')  3.16 us
    all_gather x1, blocking collectives, local(): sources = lax.all_gather(sent, 'core')  2.18 us
    all_gather x1, blocking collectives, local(): matrices = lax.all_gather(matrix, 'core')  2.18 us
    pallas_call x1, Pallas kernels, prelude(): pl.pallas_call(prelude_body, out_shape=[jax.ShapeDtypeStruct(shape, dtype...  1.87 us
  transfers between devices with their start and end apart: 7, of which 1 were waited for; matrix products, arithmetic and copies ran while one was open for 0% of the time, Pallas kernels for 1%

profile of v9, /device:TPU:6, one launch (start us, length us, event | category | flops | bytes accessed | tf_op | source)
XLA Modules:
  0.0 80.0 jit_solution(7736260377678166638)
XLA Ops:
  0.0 1.9 %shard_map.64 = (bf16[2,256,256]{2,1,0:T(8,128)(2,1)S(1)}, f32[2,256,256]{2,1,0:T(8,128)S(1)}, bf16[2,256,256]{2,1,0:T(8,128)(2,1)S(1)}) custom-call(bf16[2,256,256]{2,1,0:T(8,128)(2,1)} %bitcast.18, bf16[2,256,256]{2,1,0:T(8,128)(2,1)} %bitcast.19, bf16[2,256,256]{2,1,0:T(8,128)(2,1)} %bitcast.20), custom_call_target="tpu_custom_call" | custom-call | flops 402653184 | bytes 1048576 | tf_op jit(solution)/shard_map/pallas_call | solution.py:101
  1.9 2.2 %all-gather = bf16[4,256,256]{2,1,0:T(8,128)(2,1)S(1)} all-gather(bf16[2,256,256]{2,1,0:T(8,128)(2,1)S(1)} %get-tuple-element.16), channel_id=2, replica_groups=mesh['chip'=4,'core'=2,'energy'=64] {'core'}, dimensions={0}, use_global_device_ids=true | all-gather | bytes 786432 | tf_op jit(solution)/shard_map/all_gather | solution.py:382
  4.1 0.7 collective-permute-start.2
  4.7 2.2 %all-gather.1 = bf16[4,256,256]{2,1,0:T(8,128)(2,1)S(1)} all-gather(bf16[2,256,256]{2,1,0:T(8,128)(2,1)S(1)} %get-tuple-element.14.matrix_ref), channel_id=3, replica_groups=mesh['chip'=4,'core'=2,'energy'=64] {'core'}, dimensions={0}, use_global_device_ids=true | all-gather | bytes 786432 | tf_op jit(solution)/shard_map/all_gather | solution.py:385
  6.9 1.0 %shard_map.65 = (f32[2,256,256]{2,1,0:T(8,128)S(1)}, bf16[2,2,256,256]{3,2,1,0:T(8,128)(2,1)S(1)}, bf16[128,1024]{1,0:T(8,128)(2,1)S(1)}, bf16[256,128]{1,0:T(8,128)(2,1)S(1)}, bf16[128,256]{1,0:T(8,128)(2,1)S(1)}) custom-call(f32[2,256,256]{2,1,0:T(8,128)S(1)} %get-tuple-element.15.source_ref, bf16[2,2,256,256]{3,2,1,0:T(8,128)(2,1)S(1)} %bitcast.13, ...), custom_call_target="tpu_custom_call" | custom-call | flops 402653184 | bytes 1048576 | tf_op jit(solution)/shard_map/pallas_call | solution.py:167
  7.9 0.7 collective-permute-start
  8.6 0.0 collective-permute-done.2.arrived_ref
  8.6 0.7 collective-permute-start.5
  9.3 0.7 collective-permute-start.6
  10.0 3.2 %all-gather.2 = bf16[4,256,256]{2,1,0:T(8,128)(2,1)S(1)} all-gather(bf16[2,256,256]{2,1,0:T(8,128)(2,1)S(1)} %collective-permute-done.2.arrived_ref), channel_id=4, replica_groups=mesh['chip'=4,'core'=2,'energy'=64] {'core'}, dimensions={0}, use_global_device_ids=true | all-gather | bytes 786432 | tf_op jit(solution)/shard_map/all_gather | solution.py:399
  13.2 1.3 %collective-permute-start.3 = (bf16[2,256,256]{2,1,0:T(8,128)(2,1)S(1)}, bf16[2,256,256]{2,1,0:T(8,128)(2,1)S(1)}, u32[]{:S(2)}, u32[]{:S(2)}) collective-permute-start(bf16[2,256,256]{2,1,0:T(8,128)(2,1)S(1)} %shard_map.68), channel_id=1, source_target_pairs={{128,384},{129,385},{130,386},{131,387},{132,388},{133,389},{134,3... | collective-permute-start | bytes 786440 | tf_op jit(solution)/shard_map/ppermute | solution.py:409
  14.5 0.7 collective-permute-start.4
  15.1 0.0 collective-permute-done.map_ref
  15.2 1.3 %collective-permute-start.1 = (bf16[2,2,256,256]{3,2,1,0:T(8,128)(2,1)S(1)}, bf16[2,2,256,256]{3,2,1,0:T(8,128)(2,1)S(1)}, u32[]{:S(2)}, u32[]{:S(2)}) collective-permute-start(bf16[2,2,256,256]{3,2,1,0:T(8,128)(2,1)S(1)} %collective-permute-done.map_ref), channel_id=1, source_target_pairs={{448,384},{449,385},{450,386},{451,387},{452,388},{453,389},{454,3... | collective-permute-start | bytes 1572872 | tf_op jit(solution)/shard_map/ppermute | solution.py:410
  16.5 0.0 collective-permute-done.5.far_ref
  16.5 0.0 collective-permute-done.6.near_ref
  16.5 11.4 %collective-permute-done.3.far_ref = bf16[2,256,256]{2,1,0:T(8,128)(2,1)S(1)} collective-permute-done((bf16[2,256,256]{2,1,0:T(8,128)(2,1)S(1)}, bf16[2,256,256]{2,1,0:T(8,128)(2,1)S(1)}, u32[]{:S(2)}, u32[]{:S(2)}) %collective-permute-start.3) | collective-permute-done | bytes 262176 | tf_op jit(solution)/shard_map/ppermute | solution.py:409
  27.9 0.0 collective-permute-done.4.near_ref
  27.9 0.0 collective-permute-done.1.map_ref
  27.9 1.0 %shard_map.71 = bf16[32,2,16,128]{3,2,1,0:T(8,128)(2,1)S(1)} custom-call(bf16[2,256,256]{2,1,0:T(8,128)(2,1)S(1)} %get-tuple-element.14.matrix_ref, f32[2,256,256]{2,1,0:T(8,128)S(1)} %get-tuple-element.15.source_ref, bf16[2,2,256,256]{3,2,1,0:T(8,128)(2,1)S(1)} %collective-permute-done.1.map_ref, ...), custom_call_target="tpu_custom_call", output_to_operand_aliasing={{}: (6, {})} | custom-call | flops 268435456 | bytes 2883584 | tf_op jit(solution)/shard_map/pallas_call | solution.py:70
  28.9 25.9 %all_to_all.10.chunks_ref = bf16[64,16,128]{2,1,0:T(8,128)(2,1)S(1)} all-to-all(bf16[64,16,128]{2,1,0:T(8,128)(2,1)S(1)} %bitcast.14), channel_id=1, replica_groups={{46,47,48,49,50,51,52,53,54,55,56,57,58,59,60,61,62,63,0,1,2,3,4,5,6,7,..., dimensions={0} | all-to-all | bytes 524288 | tf_op jit(solution)/shard_map/all_to_all | solution.py:369
  54.8 1.2 %shard_map.72 = bf16[64,16,128]{2,1,0:T(8,128)(2,1)S(1)} custom-call(bf16[64,16,128]{2,1,0:T(8,128)(2,1)S(1)} %all_to_all.10.chunks_ref, bf16[256,128]{1,0:T(8,128)(2,1)S(1)} %get-tuple-element.20.forward_ref, bf16[128,256]{1,0:T(8,128)(2,1)S(1)} %get-tuple-element.21.inverse_ref, bf16[128,1024]{1,0:T(8,128)(2,1)S(1)} %get-tuple-element.22.weights_ref), custom_call_target="tpu_custom_call" | custom-call | flops 134217728 | bytes 786432 | tf_op jit(solution)/shard_map/pallas_call | solution.py:351
  56.0 23.2 %all_to_all.11 = bf16[64,16,128]{2,1,0:T(8,128)(2,1)S(1)} all-to-all(bf16[64,16,128]{2,1,0:T(8,128)(2,1)S(1)} %shard_map.72), channel_id=1, replica_groups={{34,35,36,37,38,39,40,41,42,43,44,45,46,47,48,49,50,51,52,53,54,55,56,5..., dimensions={0} | all-to-all | bytes 524288 | tf_op jit(solution)/shard_map/all_to_all | solution.py:369
  79.3 0.7 shard_map.73
  (5 shorter events, 0.1 us)
Async XLA Ops:
  4.1 4.5 %collective-permute-start.2 = (bf16[2,256,256]{2,1,0:T(8,128)(2,1)S(1)}, bf16[2,256,256]{2,1,0:T(8,128)(2,1)S(1)}, u32[]{:S(2)}, u32[]{:S(2)}) collective-permute-start(bf16[2,256,256]{2,1,0:T(8,128)(2,1)S(1)} %shard_map.66), channel_id=1, source_target_pairs={{64,192},{65,193},{66,194},{67,195},{68,196},{69,197},{70,198},{71... | collective-permute-start | bytes 786440 | tf_op jit(solution)/shard_map/ppermute | solution.py:384
  7.9 7.2 %collective-permute-start = (bf16[2,2,256,256]{3,2,1,0:T(8,128)(2,1)S(1)}, bf16[2,2,256,256]{3,2,1,0:T(8,128)(2,1)S(1)}, u32[]{:S(2)}, u32[]{:S(2)}) collective-permute-start(bf16[2,2,256,256]{3,2,1,0:T(8,128)(2,1)S(1)} %get-tuple-element.17.map_ref), channel_id=1, source_target_pairs={{320,448},{321,449},{322,450},{323,451},{324,452},{325,453},{326,4... | collective-permute-start | bytes 1572872 | tf_op jit(solution)/shard_map/ppermute | solution.py:393
  8.6 7.8 %collective-permute-start.5 = (bf16[2,256,256]{2,1,0:T(8,128)(2,1)S(1)}, bf16[2,256,256]{2,1,0:T(8,128)(2,1)S(1)}, u32[]{:S(2)}, u32[]{:S(2)}) collective-permute-start(bf16[2,256,256]{2,1,0:T(8,128)(2,1)S(1)} %shard_map.67), channel_id=1, source_target_pairs={{192,448},{193,449},{194,450},{195,451},{196,452},{197,453},{198,4... | collective-permute-start | bytes 786440 | tf_op jit(solution)/shard_map/ppermute | solution.py:398
  9.3 7.2 %collective-permute-start.6 = (bf16[2,256,256]{2,1,0:T(8,128)(2,1)S(1)}, bf16[2,256,256]{2,1,0:T(8,128)(2,1)S(1)}, u32[]{:S(2)}, u32[]{:S(2)}) collective-permute-start(bf16[2,256,256]{2,1,0:T(8,128)(2,1)S(1)} %shard_map.67), channel_id=1, source_target_pairs={{192,320},{193,321},{194,322},{195,323},{196,324},{197,325},{198,3... | collective-permute-start | bytes 786440 | tf_op jit(solution)/shard_map/ppermute | solution.py:397
  13.2 14.7 %collective-permute-start.3 = (bf16[2,256,256]{2,1,0:T(8,128)(2,1)S(1)}, bf16[2,256,256]{2,1,0:T(8,128)(2,1)S(1)}, u32[]{:S(2)}, u32[]{:S(2)}) collective-permute-start(bf16[2,256,256]{2,1,0:T(8,128)(2,1)S(1)} %shard_map.68), channel_id=1, source_target_pairs={{128,384},{129,385},{130,386},{131,387},{132,388},{133,389},{134,3... | collective-permute-start | bytes 786440 | tf_op jit(solution)/shard_map/ppermute | solution.py:409
  14.5 13.4 %collective-permute-start.4 = (bf16[2,256,256]{2,1,0:T(8,128)(2,1)S(1)}, bf16[2,256,256]{2,1,0:T(8,128)(2,1)S(1)}, u32[]{:S(2)}, u32[]{:S(2)}) collective-permute-start(bf16[2,256,256]{2,1,0:T(8,128)(2,1)S(1)} %shard_map.68), channel_id=1, source_target_pairs={{128,256},{129,257},{130,258},{131,259},{132,260},{133,261},{134,2... | collective-permute-start | bytes 786440 | tf_op jit(solution)/shard_map/ppermute | solution.py:408
  15.2 12.8 %collective-permute-start.1 = (bf16[2,2,256,256]{3,2,1,0:T(8,128)(2,1)S(1)}, bf16[2,2,256,256]{3,2,1,0:T(8,128)(2,1)S(1)}, u32[]{:S(2)}, u32[]{:S(2)}) collective-permute-start(bf16[2,2,256,256]{3,2,1,0:T(8,128)(2,1)S(1)} %collective-permute-done.map_ref), channel_id=1, source_target_pairs={{448,384},{449,385},{450,386},{451,387},{452,388},{453,389},{454,3... | collective-permute-start | bytes 1572872 | tf_op jit(solution)/shard_map/ppermute | solution.py:410

commit v10 on v8

--- a/solution.py
+++ b/solution.py
@@ -281,7 +281,7 @@
     values = jnp.concatenate(
         [jnp.concatenate(taken[:ROWS], axis=1), jnp.concatenate(taken[ROWS:], axis=1)], axis=0
     )
-    spectrum = dot(forward_ref[...], values) * (count**-0.5)
+    spectrum = dot(forward_ref[...], values)
     order = [2 * (i % 4) + i // 4 for i in range(ROWS)]
     weights = jnp.concatenate(
         [weights_ref[:, LANES * i : LANES * (i + 1)] for i in order], axis=1
@@ -337,7 +337,8 @@
 
 def tables(count, length):
     phase = np.roll(phase_table(length, count, length), -FIRST_OUT, axis=1)
-    forward = complex_table(np.cos(phase), -np.sin(phase))
+    scale = count**-0.5
+    forward = complex_table(scale * np.cos(phase), -scale * np.sin(phase))
     phase = np.roll(phase_table(count, length, length), -FIRST_BACK, axis=0)
     inverse = complex_table(np.cos(phase), np.sin(phase))
     return forward, inverse

time: 79.8 us -> 79.8 us (level)
  no operation moved by 1% of the time
where the time goes in v10:
time: 79.8 us; the launch traced here: 79.5 us
  blocking collectives  56.6 us (71%)
  waiting for transfers between devices  11.4 us (14%)
  starting transfers between devices  5.96 us (7%)
  Pallas kernels  5.37 us (7%)
    all_to_all x2, blocking collectives, exchanged(): lax.all_to_all(chunks, 'energy', split_axis=0, concat_axis=0, axis_index_...  49.1 us
    ppermute x1, waiting for transfers between devices, local(): far_later = lax.ppermute(green, SPACE, [(2, 6)])  11.4 us
    all_gather x1, blocking collectives, local(): arrived_later = lax.all_gather(after(arrived, green), 'core')  3.16 us
    all_gather x1, blocking collectives, local(): sources = lax.all_gather(sent, 'core')  2.18 us
    all_gather x1, blocking collectives, local(): matrices = lax.all_gather(matrix, 'core')  2.18 us
    pallas_call x1, Pallas kernels, prelude(): pl.pallas_call(prelude_body, out_shape=[jax.ShapeDtypeStruct(shape, dtype...  1.87 us
  transfers between devices with their start and end apart: 7, of which 1 were waited for; matrix products, arithmetic and copies ran while one was open for 0% of the time, Pallas kernels for 1%

profile of v10, /device:TPU:6, one launch (start us, length us, event | category | flops | bytes accessed | tf_op | source)
XLA Modules:
  0.0 79.5 jit_solution(2185920395674120025)
XLA Ops:
  0.0 1.9 %shard_map.64 = (bf16[2,256,256]{2,1,0:T(8,128)(2,1)S(1)}, f32[2,256,256]{2,1,0:T(8,128)S(1)}, bf16[2,256,256]{2,1,0:T(8,128)(2,1)S(1)}) custom-call(bf16[2,256,256]{2,1,0:T(8,128)(2,1)} %bitcast.18, bf16[2,256,256]{2,1,0:T(8,128)(2,1)} %bitcast.19, bf16[2,256,256]{2,1,0:T(8,128)(2,1)} %bitcast.20), custom_call_target="tpu_custom_call" | custom-call | flops 402653184 | bytes 1048576 | tf_op jit(solution)/shard_map/pallas_call | solution.py:101
  1.9 2.2 %all-gather = bf16[4,256,256]{2,1,0:T(8,128)(2,1)S(1)} all-gather(bf16[2,256,256]{2,1,0:T(8,128)(2,1)S(1)} %get-tuple-element.16), channel_id=2, replica_groups=mesh['chip'=4,'core'=2,'energy'=64] {'core'}, dimensions={0}, use_global_device_ids=true | all-gather | bytes 786432 | tf_op jit(solution)/shard_map/all_gather | solution.py:381
  4.1 0.7 collective-permute-start.2
  4.7 2.2 %all-gather.1 = bf16[4,256,256]{2,1,0:T(8,128)(2,1)S(1)} all-gather(bf16[2,256,256]{2,1,0:T(8,128)(2,1)S(1)} %get-tuple-element.14.matrix_ref), channel_id=3, replica_groups=mesh['chip'=4,'core'=2,'energy'=64] {'core'}, dimensions={0}, use_global_device_ids=true | all-gather | bytes 786432 | tf_op jit(solution)/shard_map/all_gather | solution.py:384
  6.9 1.0 %shard_map.65 = (f32[2,256,256]{2,1,0:T(8,128)S(1)}, bf16[2,2,256,256]{3,2,1,0:T(8,128)(2,1)S(1)}, bf16[128,1024]{1,0:T(8,128)(2,1)S(1)}, bf16[256,128]{1,0:T(8,128)(2,1)S(1)}, bf16[128,256]{1,0:T(8,128)(2,1)S(1)}) custom-call(f32[2,256,256]{2,1,0:T(8,128)S(1)} %get-tuple-element.15.source_ref, bf16[2,2,256,256]{3,2,1,0:T(8,128)(2,1)S(1)} %bitcast.13, ...), custom_call_target="tpu_custom_call" | custom-call | flops 402653184 | bytes 1048576 | tf_op jit(solution)/shard_map/pallas_call | solution.py:167
  7.9 0.7 collective-permute-start
  8.6 0.0 collective-permute-done.2.arrived_ref
  8.6 0.7 collective-permute-start.5
  9.3 0.7 collective-permute-start.6
  10.0 3.2 %all-gather.2 = bf16[4,256,256]{2,1,0:T(8,128)(2,1)S(1)} all-gather(bf16[2,256,256]{2,1,0:T(8,128)(2,1)S(1)} %collective-permute-done.2.arrived_ref), channel_id=4, replica_groups=mesh['chip'=4,'core'=2,'energy'=64] {'core'}, dimensions={0}, use_global_device_ids=true | all-gather | bytes 786432 | tf_op jit(solution)/shard_map/all_gather | solution.py:398
  13.2 1.3 %collective-permute-start.3 = (bf16[2,256,256]{2,1,0:T(8,128)(2,1)S(1)}, bf16[2,256,256]{2,1,0:T(8,128)(2,1)S(1)}, u32[]{:S(2)}, u32[]{:S(2)}) collective-permute-start(bf16[2,256,256]{2,1,0:T(8,128)(2,1)S(1)} %shard_map.68), channel_id=1, source_target_pairs={{128,384},{129,385},{130,386},{131,387},{132,388},{133,389},{134,3... | collective-permute-start | bytes 786440 | tf_op jit(solution)/shard_map/ppermute | solution.py:408
  14.5 0.7 collective-permute-start.4
  15.1 0.0 collective-permute-done.map_ref
  15.2 1.3 %collective-permute-start.1 = (bf16[2,2,256,256]{3,2,1,0:T(8,128)(2,1)S(1)}, bf16[2,2,256,256]{3,2,1,0:T(8,128)(2,1)S(1)}, u32[]{:S(2)}, u32[]{:S(2)}) collective-permute-start(bf16[2,2,256,256]{3,2,1,0:T(8,128)(2,1)S(1)} %collective-permute-done.map_ref), channel_id=1, source_target_pairs={{448,384},{449,385},{450,386},{451,387},{452,388},{453,389},{454,3... | collective-permute-start | bytes 1572872 | tf_op jit(solution)/shard_map/ppermute | solution.py:409
  16.5 0.0 collective-permute-done.5.far_ref
  16.5 0.0 collective-permute-done.6.near_ref
  16.5 11.4 %collective-permute-done.3.far_ref = bf16[2,256,256]{2,1,0:T(8,128)(2,1)S(1)} collective-permute-done((bf16[2,256,256]{2,1,0:T(8,128)(2,1)S(1)}, bf16[2,256,256]{2,1,0:T(8,128)(2,1)S(1)}, u32[]{:S(2)}, u32[]{:S(2)}) %collective-permute-start.3) | collective-permute-done | bytes 262176 | tf_op jit(solution)/shard_map/ppermute | solution.py:408
  27.9 0.0 collective-permute-done.4.near_ref
  27.9 0.0 collective-permute-done.1.map_ref
  27.9 1.0 %shard_map.71 = bf16[32,2,16,128]{3,2,1,0:T(8,128)(2,1)S(1)} custom-call(bf16[2,256,256]{2,1,0:T(8,128)(2,1)S(1)} %get-tuple-element.14.matrix_ref, f32[2,256,256]{2,1,0:T(8,128)S(1)} %get-tuple-element.15.source_ref, bf16[2,2,256,256]{3,2,1,0:T(8,128)(2,1)S(1)} %collective-permute-done.1.map_ref, ...), custom_call_target="tpu_custom_call", output_to_operand_aliasing={{}: (6, {})} | custom-call | flops 268435456 | bytes 2883584 | tf_op jit(solution)/shard_map/pallas_call | solution.py:70
  28.9 25.9 %all_to_all.10.chunks_ref = bf16[64,16,128]{2,1,0:T(8,128)(2,1)S(1)} all-to-all(bf16[64,16,128]{2,1,0:T(8,128)(2,1)S(1)} %bitcast.14), channel_id=1, replica_groups={{46,47,48,49,50,51,52,53,54,55,56,57,58,59,60,61,62,63,0,1,2,3,4,5,6,7,..., dimensions={0} | all-to-all | bytes 524288 | tf_op jit(solution)/shard_map/all_to_all | solution.py:368
  54.8 0.7 shard_map.72
  55.5 23.2 %all_to_all.11 = bf16[64,16,128]{2,1,0:T(8,128)(2,1)S(1)} all-to-all(bf16[64,16,128]{2,1,0:T(8,128)(2,1)S(1)} %shard_map.72), channel_id=1, replica_groups={{34,35,36,37,38,39,40,41,42,43,44,45,46,47,48,49,50,51,52,53,54,55,56,5..., dimensions={0} | all-to-all | bytes 524288 | tf_op jit(solution)/shard_map/all_to_all | solution.py:368
  78.8 0.7 shard_map.73
  (5 shorter events, 0.1 us)
Async XLA Ops:
  4.1 4.5 %collective-permute-start.2 = (bf16[2,256,256]{2,1,0:T(8,128)(2,1)S(1)}, bf16[2,256,256]{2,1,0:T(8,128)(2,1)S(1)}, u32[]{:S(2)}, u32[]{:S(2)}) collective-permute-start(bf16[2,256,256]{2,1,0:T(8,128)(2,1)S(1)} %shard_map.66), channel_id=1, source_target_pairs={{64,192},{65,193},{66,194},{67,195},{68,196},{69,197},{70,198},{71... | collective-permute-start | bytes 786440 | tf_op jit(solution)/shard_map/ppermute | solution.py:383
  7.9 7.2 %collective-permute-start = (bf16[2,2,256,256]{3,2,1,0:T(8,128)(2,1)S(1)}, bf16[2,2,256,256]{3,2,1,0:T(8,128)(2,1)S(1)}, u32[]{:S(2)}, u32[]{:S(2)}) collective-permute-start(bf16[2,2,256,256]{3,2,1,0:T(8,128)(2,1)S(1)} %get-tuple-element.17.map_ref), channel_id=1, source_target_pairs={{320,448},{321,449},{322,450},{323,451},{324,452},{325,453},{326,4... | collective-permute-start | bytes 1572872 | tf_op jit(solution)/shard_map/ppermute | solution.py:392
  8.6 7.8 %collective-permute-start.5 = (bf16[2,256,256]{2,1,0:T(8,128)(2,1)S(1)}, bf16[2,256,256]{2,1,0:T(8,128)(2,1)S(1)}, u32[]{:S(2)}, u32[]{:S(2)}) collective-permute-start(bf16[2,256,256]{2,1,0:T(8,128)(2,1)S(1)} %shard_map.67), channel_id=1, source_target_pairs={{192,448},{193,449},{194,450},{195,451},{196,452},{197,453},{198,4... | collective-permute-start | bytes 786440 | tf_op jit(solution)/shard_map/ppermute | solution.py:397
  9.3 7.2 %collective-permute-start.6 = (bf16[2,256,256]{2,1,0:T(8,128)(2,1)S(1)}, bf16[2,256,256]{2,1,0:T(8,128)(2,1)S(1)}, u32[]{:S(2)}, u32[]{:S(2)}) collective-permute-start(bf16[2,256,256]{2,1,0:T(8,128)(2,1)S(1)} %shard_map.67), channel_id=1, source_target_pairs={{192,320},{193,321},{194,322},{195,323},{196,324},{197,325},{198,3... | collective-permute-start | bytes 786440 | tf_op jit(solution)/shard_map/ppermute | solution.py:396
  13.2 14.7 %collective-permute-start.3 = (bf16[2,256,256]{2,1,0:T(8,128)(2,1)S(1)}, bf16[2,256,256]{2,1,0:T(8,128)(2,1)S(1)}, u32[]{:S(2)}, u32[]{:S(2)}) collective-permute-start(bf16[2,256,256]{2,1,0:T(8,128)(2,1)S(1)} %shard_map.68), channel_id=1, source_target_pairs={{128,384},{129,385},{130,386},{131,387},{132,388},{133,389},{134,3... | collective-permute-start | bytes 786440 | tf_op jit(solution)/shard_map/ppermute | solution.py:408
  14.5 13.4 %collective-permute-start.4 = (bf16[2,256,256]{2,1,0:T(8,128)(2,1)S(1)}, bf16[2,256,256]{2,1,0:T(8,128)(2,1)S(1)}, u32[]{:S(2)}, u32[]{:S(2)}) collective-permute-start(bf16[2,256,256]{2,1,0:T(8,128)(2,1)S(1)} %shard_map.68), channel_id=1, source_target_pairs={{128,256},{129,257},{130,258},{131,259},{132,260},{133,261},{134,2... | collective-permute-start | bytes 786440 | tf_op jit(solution)/shard_map/ppermute | solution.py:407
  15.2 12.8 %collective-permute-start.1 = (bf16[2,2,256,256]{3,2,1,0:T(8,128)(2,1)S(1)}, bf16[2,2,256,256]{3,2,1,0:T(8,128)(2,1)S(1)}, u32[]{:S(2)}, u32[]{:S(2)}) collective-permute-start(bf16[2,2,256,256]{3,2,1,0:T(8,128)(2,1)S(1)} %collective-permute-done.map_ref), channel_id=1, source_target_pairs={{448,384},{449,385},{450,386},{451,387},{452,388},{453,389},{454,3... | collective-permute-start | bytes 1572872 | tf_op jit(solution)/shard_map/ppermute | solution.py:409
